TPU v7x, 32 devices: a whole 2x2x4 slice. The times are simulated.
32 devices in a mesh: mp: 4 (over y, x), dp: 8 (over z, core).
Axes of the slice: x: 2, y: 2, z: 4, core: 2. Of those that a mesh axis runs over, the one named last changes fastest.
Arguments:
- tokens: bfloat16 [8192, 2048], P('dp', 'mp')
- cotangent: bfloat16 [8192, 2048], P('dp', 'mp'), may hold values from -6 to 6
- seq_lengths: int32 [8, 16], P('dp'), may hold values from 0 to 1024, as said below
- w_qkv: float32 [2048, 3, 2048], P('dp', None, 'mp'), may hold values from -0.125 to 0.125
- qkv_bias_state: float32 [2, 3, 2048], P(None, None, ('mp', 'dp')), as said below
- w_out: float32 [2048, 2048], P('mp', 'dp'), may hold values from -0.5 to 0.5
- out_bias_state: float32 [2, 2, 2048], P(None, None, ('mp', 'dp')), as said below
- w_up: float32 [2048, 8192], P('dp', 'mp'), may hold values from -0.125 to 0.125
- up_bias_state: float32 [2, 8192], P(None, ('mp', 'dp')), as said below
- w_down: float32 [8192, 2048], P('mp', 'dp'), may hold values from -0.0625 to 0.0625
- ln_state: float32 [2, 2, 2048], P(None, None, ('mp', 'dp')), as said below
- qkv_left: float32 [2, 4, 8, 256, 256], P(None, 'mp', 'dp')
- qkv_right: float32 [2, 4, 8, 1536, 1536], P(None, 'mp', 'dp')
- out_left: float32 [2, 4, 8, 512, 512], P(None, 'mp', 'dp')
- out_right: float32 [2, 4, 8, 256, 256], P(None, 'mp', 'dp')
- up_left: float32 [2, 4, 8, 256, 256], P(None, 'mp', 'dp')
- up_right: float32 [2, 4, 8, 2048, 2048], P(None, 'mp', 'dp')
- down_left: float32 [2, 4, 8, 2048, 2048], P(None, 'mp', 'dp')
- down_right: float32 [2, 4, 8, 256, 256], P(None, 'mp', 'dp')
Outputs:
- output: bfloat16 [8192, 2048], P('dp', 'mp')
- input_grad: float32 [8192, 2048], P('dp', 'mp')
- new_w_qkv: float32 [2048, 3, 2048], P('dp', None, 'mp')
- new_w_out: float32 [2048, 2048], P('mp', 'dp')
- new_w_up: float32 [2048, 8192], P('dp', 'mp')
- new_w_down: float32 [8192, 2048], P('mp', 'dp')
- new_vector_params: float32 [7, 2048], P(None, ('mp', 'dp'))
- new_vector_stats: float32 [7, 2048], P(None, ('mp', 'dp'))
- new_up_bias: float32 [8192], P(('mp', 'dp'))
- new_up_stat: float32 [8192], P(('mp', 'dp'))
- qkv_left_new: float32 [4, 8, 256, 256], P('mp', 'dp')
- qkv_right_new: float32 [4, 8, 1536, 1536], P('mp', 'dp')
- out_left_new: float32 [4, 8, 512, 512], P('mp', 'dp')
- out_right_new: float32 [4, 8, 256, 256], P('mp', 'dp')
- up_left_new: float32 [4, 8, 256, 256], P('mp', 'dp')
- up_right_new: float32 [4, 8, 2048, 2048], P('mp', 'dp')
- down_left_new: float32 [4, 8, 2048, 2048], P('mp', 'dp')
- down_right_new: float32 [4, 8, 256, 256], P('mp', 'dp')
Inputs may be any that keep to these rules, and one draw needn't show every extreme that they name: `seq_lengths`: row b lists, in order, the lengths of the sequences packed back to back from the first row of block b of 1024 rows; 0 marks an empty slot, every other length is 64 or more; a row sums to at most 1024, the rest of the block is padding; some block holds a sequence of 1024. `ln_state`: index 1 holds positive statistics. `qkv_bias_state`: index 1 holds positive statistics. `out_bias_state`: index 1 holds positive statistics. `up_bias_state`: index 1 holds positive statistics.
All inputs are finite; a program needn't handle non-finite values.
Results may differ from a plain program's by a relative error of at most 0.033.
Values may be sent and summed in bfloat16 or wider, within the bound.
A program may use at most 320 MiB of HBM per device.

v0:
```python
import math

import jax
import jax.numpy as jnp
from jax import lax
from jax.sharding import PartitionSpec as P

HEAD_DIM = 64
ROT_DIM = 32
TILE = 512


norm_eps = 1e-05
matrix_rate = 1.0
vector_rate = 0.4
masked_score = -1e30
highest = lax.Precision.HIGHEST


def segment_layout(lengths, row_count):
    positions = jnp.arange(row_count, dtype=jnp.int32)
    seq_ends = jnp.cumsum(lengths)
    finished = seq_ends[None, :] <= positions[:, None]
    segment = jnp.sum(finished.astype(jnp.int32), axis=1)
    starting = jnp.max(jnp.where(finished, seq_ends[None, :], 0), axis=1)
    is_valid = positions < seq_ends[-1]
    segment = jnp.where(is_valid, segment, lengths.shape[0] + positions)
    offsets = (positions - starting).astype(jnp.float32)
    return (segment, offsets, is_valid.astype(jnp.float32))


def rope_tables(offsets):
    half_rot = ROT_DIM // 2
    freq_index = jnp.arange(half_rot, dtype=jnp.float32)
    inverse = jnp.exp(-(2.0 * freq_index / ROT_DIM) * math.log(10000.0))
    angles = offsets[:, None] * inverse[None, :]
    return (jnp.cos(angles)[:, None, :], jnp.sin(angles)[:, None, :])


def rotate(values, cosine, sine, direction):
    half_rot = ROT_DIM // 2
    first_half = values[..., :half_rot]
    second_half = values[..., half_rot:ROT_DIM]
    untouched = values[..., ROT_DIM:]
    new_first = first_half * cosine - direction * second_half * sine
    new_second = second_half * cosine + direction * first_half * sine
    return jnp.concatenate([new_first, new_second, untouched], axis=-1)


def gelu_tanh(values):
    return jax.nn.gelu(values, approximate=True)


def tile_scores(queries, key_rows, segment, row_start, key_start, tile_rows):
    query_block = queries[row_start : row_start + tile_rows]
    key_block = key_rows[key_start : key_start + tile_rows]
    scores = jnp.einsum(
        "qhd,khd->hqk", query_block, key_block, preferred_element_type=jnp.float32
    ) * HEAD_DIM ** (-0.5)
    row_ids = row_start + jnp.arange(tile_rows)
    key_ids = key_start + jnp.arange(tile_rows)
    same_seq = (
        segment[row_start : row_start + tile_rows][:, None]
        == segment[key_start : key_start + tile_rows][None, :]
    )
    allowed = same_seq & (key_ids[None, :] <= row_ids[:, None])
    return (scores, allowed[None])


def guarded(segment, row_start, key_start, tile_rows, update, fallback):
    if key_start == row_start:
        return update()
    return lax.cond(segment[row_start] <= segment[key_start + tile_rows - 1], update, fallback)


def attention_forward(queries, key_rows, value_rows, segment, tile_rows):
    row_count, head_count, head_width = queries.shape
    tile_count = row_count // tile_rows
    outputs = []
    lse_tiles = []
    for row_tile in range(tile_count):
        row_start = row_tile * tile_rows
        running = (
            jnp.full((head_count, tile_rows), masked_score, jnp.float32),
            jnp.zeros((head_count, tile_rows), jnp.float32),
        )
        for key_tile in range(row_tile + 1):
            key_start = key_tile * tile_rows

            def advance(state=running, row_start=row_start, key_start=key_start):
                scores, allowed = tile_scores(
                    queries, key_rows, segment, row_start, key_start, tile_rows
                )
                kept_scores = jnp.where(allowed, scores, masked_score)
                peak = jnp.maximum(state[0], jnp.max(kept_scores, axis=-1))
                weights = jnp.where(allowed, jnp.exp(kept_scores - peak[..., None]), 0.0)
                return (peak, state[1] * jnp.exp(state[0] - peak) + jnp.sum(weights, axis=-1))

            def unchanged(state=running):
                return state

            running = guarded(segment, row_start, key_start, tile_rows, advance, unchanged)
        lse_tile = running[0] + jnp.log(running[1])
        lse_tiles.append(lse_tile)
        zero_block = jnp.zeros((tile_rows, head_count, head_width), jnp.float32)
        collected = zero_block
        for key_tile in range(row_tile + 1):
            key_start = key_tile * tile_rows

            def weigh_values(lse_tile=lse_tile, row_start=row_start, key_start=key_start):
                scores, allowed = tile_scores(
                    queries, key_rows, segment, row_start, key_start, tile_rows
                )
                probability = jnp.where(allowed, jnp.exp(scores - lse_tile[..., None]), 0.0).astype(
                    jnp.bfloat16
                )
                return jnp.einsum(
                    "hqk,khd->qhd",
                    probability,
                    value_rows[key_start : key_start + tile_rows],
                    preferred_element_type=jnp.float32,
                )

            def nothing(zero_block=zero_block):
                return zero_block

            collected = collected + guarded(
                segment, row_start, key_start, tile_rows, weigh_values, nothing
            )
        outputs.append(collected)
    return (jnp.concatenate(outputs, axis=0), lse_tiles)


def attention_backward(
    queries, key_rows, value_rows, segment, tile_rows, grad_attended, attended, lse_tiles
):
    row_count, head_count, head_width = queries.shape
    tile_count = row_count // tile_rows
    score_scale = HEAD_DIM ** (-0.5)
    row_delta = jnp.sum(grad_attended.astype(jnp.float32) * attended, axis=-1).T
    zero_block = jnp.zeros((tile_rows, head_count, head_width), jnp.float32)
    query_grads = []
    key_grads = [zero_block for key_tile in range(tile_count)]
    value_grads = [zero_block for key_tile in range(tile_count)]
    for row_tile in range(tile_count):
        row_start = row_tile * tile_rows
        query_acc = zero_block
        for key_tile in range(row_tile + 1):
            key_start = key_tile * tile_rows

            def contribute(lse_tile=lse_tiles[row_tile], row_start=row_start, key_start=key_start):
                scores, allowed = tile_scores(
                    queries, key_rows, segment, row_start, key_start, tile_rows
                )
                probability = jnp.where(allowed, jnp.exp(scores - lse_tile[..., None]), 0.0)
                out_block = grad_attended[row_start : row_start + tile_rows]
                value_block = value_rows[key_start : key_start + tile_rows]
                key_block = key_rows[key_start : key_start + tile_rows]
                query_block = queries[row_start : row_start + tile_rows]
                grad_probs = jnp.einsum(
                    "qhd,khd->hqk", out_block, value_block, preferred_element_type=jnp.float32
                )
                delta_tile = row_delta[:, row_start : row_start + tile_rows][..., None]
                grad_scores = (probability * (grad_probs - delta_tile)).astype(jnp.bfloat16)
                part_value = jnp.einsum(
                    "hqk,qhd->khd",
                    probability.astype(jnp.bfloat16),
                    out_block,
                    preferred_element_type=jnp.float32,
                )
                part_query = (
                    jnp.einsum(
                        "hqk,khd->qhd", grad_scores, key_block, preferred_element_type=jnp.float32
                    )
                    * score_scale
                )
                part_key = (
                    jnp.einsum(
                        "hqk,qhd->khd", grad_scores, query_block, preferred_element_type=jnp.float32
                    )
                    * score_scale
                )
                return (part_query, part_key, part_value)

            def nothing(zero_block=zero_block):
                return (zero_block, zero_block, zero_block)

            part_query, part_key, part_value = guarded(
                segment, row_start, key_start, tile_rows, contribute, nothing
            )
            query_acc = query_acc + part_query
            key_grads[key_tile] = key_grads[key_tile] + part_key
            value_grads[key_tile] = value_grads[key_tile] + part_value
        query_grads.append(query_acc)
    return (
        jnp.concatenate(query_grads, axis=0),
        jnp.concatenate(key_grads, axis=0),
        jnp.concatenate(value_grads, axis=0),
    )


def shampoo(weight_block, grad_block, left, right):
    left_new = 0.5 * left[0, 0, 0] + 0.5 * jnp.dot(grad_block, grad_block.T, precision=highest)
    right_new = 0.5 * right[0, 0, 0] + 0.5 * jnp.dot(grad_block.T, grad_block, precision=highest)
    step_block = jnp.dot(
        jnp.dot(left[1, 0, 0], grad_block, precision=highest), right[1, 0, 0], precision=highest
    )
    return (weight_block - matrix_rate * step_block, left_new[None, None], right_new[None, None])


def vector_update(state, grad):
    stat_new = 0.5 * state[1] + 0.5 * grad * grad
    param_new = state[0] - vector_rate * grad * lax.rsqrt(stat_new)
    return (param_new, stat_new)


def local(
    tokens,
    cotangent,
    seq_lengths,
    w_qkv,
    qkv_bias_state,
    w_out,
    out_bias_state,
    w_up,
    up_bias_state,
    w_down,
    ln_state,
    qkv_left,
    qkv_right,
    out_left,
    out_right,
    up_left,
    up_right,
    down_left,
    down_right,
):
    row_count = tokens.shape[0]
    model_width = tokens.shape[1] * lax.axis_size("mp")
    heads_here = w_qkv.shape[2] // HEAD_DIM
    tile_rows = min(TILE, row_count)
    sent = (
        w_qkv.astype(jnp.bfloat16),
        w_out.astype(jnp.bfloat16),
        w_up.astype(jnp.bfloat16),
        w_down.astype(jnp.bfloat16),
        qkv_bias_state[0].astype(jnp.bfloat16),
        up_bias_state[0].astype(jnp.bfloat16),
        ln_state[0].astype(jnp.bfloat16),
        out_bias_state[0].astype(jnp.bfloat16),
    )
    full_qkv, full_out, full_up, full_down, bias_qkv, bias_up, norm_params, bias_out = (
        lax.all_gather(sent[0], "dp", axis=0, tiled=True),
        lax.all_gather(sent[1], "dp", axis=1, tiled=True),
        lax.all_gather(sent[2], "dp", axis=0, tiled=True),
        lax.all_gather(sent[3], "dp", axis=1, tiled=True),
        lax.all_gather(sent[4], "dp", axis=1, tiled=True),
        lax.all_gather(sent[5], "dp", axis=0, tiled=True),
        lax.all_gather(sent[6], "dp", axis=1, tiled=True),
        lax.all_gather(sent[7], "dp", axis=1, tiled=True),
    )
    inputs = tokens.astype(jnp.float32)
    moments = lax.psum((jnp.sum(inputs, axis=1), jnp.sum(inputs * inputs, axis=1)), "mp")
    row_mean = moments[0] / model_width
    row_var = moments[1] / model_width - row_mean * row_mean
    inv_std = lax.rsqrt(row_var + norm_eps)[:, None]
    normalized = (inputs - row_mean[:, None]) * inv_std
    norm_gain = norm_params[0].astype(jnp.float32)
    norm_shift = norm_params[1].astype(jnp.float32)
    normed_share = (normalized * norm_gain + norm_shift).astype(jnp.bfloat16)
    normed, upstream = (
        lax.all_gather(normed_share, "mp", axis=1, tiled=True),
        lax.all_gather(cotangent, "mp", axis=1, tiled=True),
    )
    segment, offsets, is_valid = segment_layout(seq_lengths[0], row_count)
    cosine, sine = rope_tables(offsets)
    qkv_matrix = full_qkv.reshape(model_width, -1)
    projected = jnp.dot(normed, qkv_matrix, preferred_element_type=jnp.float32) + bias_qkv.astype(
        jnp.float32
    ).reshape(-1)
    projected = projected.reshape(row_count, 3, heads_here, HEAD_DIM)
    queries = rotate(projected[:, 0], cosine, sine, 1.0).astype(jnp.bfloat16)
    key_rows = rotate(projected[:, 1], cosine, sine, 1.0).astype(jnp.bfloat16)
    value_rows = projected[:, 2].astype(jnp.bfloat16)
    attended, lse_tiles = attention_forward(queries, key_rows, value_rows, segment, tile_rows)
    attended_low = attended.reshape(row_count, -1).astype(jnp.bfloat16)
    hidden = jnp.dot(normed, full_up, preferred_element_type=jnp.float32) + bias_up.astype(
        jnp.float32
    )
    activated, gelu_pullback = jax.vjp(gelu_tanh, hidden)
    activated_low = activated.astype(jnp.bfloat16)
    partial_sum = jnp.dot(attended_low, full_out, preferred_element_type=jnp.float32) + jnp.dot(
        activated_low, full_down, preferred_element_type=jnp.float32
    )
    branches = lax.psum_scatter(
        partial_sum.astype(jnp.bfloat16), "mp", scatter_dimension=1, tiled=True
    ).astype(jnp.float32)
    out_bias = bias_out.astype(jnp.float32)
    output = (inputs + branches + out_bias[0] + out_bias[1]).astype(jnp.bfloat16)
    back_qkv, back_out, back_up, back_down = (qkv_matrix, full_out, full_up, full_down)
    grad_rows = (upstream.astype(jnp.float32) * is_valid[:, None]).astype(jnp.bfloat16)
    grad_act = jnp.dot(grad_rows, back_down.T, preferred_element_type=jnp.float32)
    grad_hidden = gelu_pullback(grad_act)[0].astype(jnp.bfloat16)
    grad_down_w = jnp.dot(activated_low.T, grad_rows, preferred_element_type=jnp.float32)
    grad_up_w = jnp.dot(normed.T, grad_hidden, preferred_element_type=jnp.float32)
    grad_up_b = jnp.sum(grad_hidden.astype(jnp.float32), axis=0)
    grad_attended = (
        jnp.dot(grad_rows, back_out.T, preferred_element_type=jnp.float32)
        .reshape(row_count, heads_here, HEAD_DIM)
        .astype(jnp.bfloat16)
    )
    grad_out_w = jnp.dot(attended_low.T, grad_rows, preferred_element_type=jnp.float32)
    grad_query, grad_key, grad_value = attention_backward(
        queries, key_rows, value_rows, segment, tile_rows, grad_attended, attended, lse_tiles
    )
    grad_projected = jnp.stack(
        [rotate(grad_query, cosine, sine, -1.0), rotate(grad_key, cosine, sine, -1.0), grad_value],
        axis=1,
    )
    grad_projected = grad_projected.reshape(row_count, -1).astype(jnp.bfloat16)
    grad_qkv_w = jnp.dot(normed.T, grad_projected, preferred_element_type=jnp.float32).reshape(
        model_width, 3, -1
    )
    grad_qkv_b = jnp.sum(grad_projected.astype(jnp.float32), axis=0).reshape(3, -1)
    grad_normed_part = jnp.dot(
        grad_projected, back_qkv.T, preferred_element_type=jnp.float32
    ) + jnp.dot(grad_hidden, back_up.T, preferred_element_type=jnp.float32)
    grad_normed = lax.psum_scatter(
        grad_normed_part.astype(jnp.bfloat16), "mp", scatter_dimension=1, tiled=True
    ).astype(jnp.float32)
    gained = grad_normed * norm_gain
    row_terms = lax.psum((jnp.sum(gained, axis=1), jnp.sum(gained * normalized, axis=1)), "mp")
    local_grad = cotangent.astype(jnp.float32) * is_valid[:, None]
    input_grad = local_grad + inv_std * (
        gained
        - row_terms[0][:, None] / model_width
        - normalized * row_terms[1][:, None] / model_width
    )
    grad_norm = jnp.stack([jnp.sum(grad_normed * normalized, axis=0), jnp.sum(grad_normed, axis=0)])
    bias_total = jnp.sum(local_grad, axis=0)
    grad_obias = jnp.stack([bias_total, bias_total])
    reduced = (
        lax.psum_scatter(
            grad_qkv_w.astype(jnp.bfloat16), "dp", scatter_dimension=0, tiled=True
        ).astype(jnp.float32),
        lax.psum_scatter(
            grad_out_w.astype(jnp.bfloat16), "dp", scatter_dimension=1, tiled=True
        ).astype(jnp.float32),
        lax.psum_scatter(
            grad_up_w.astype(jnp.bfloat16), "dp", scatter_dimension=0, tiled=True
        ).astype(jnp.float32),
        lax.psum_scatter(
            grad_down_w.astype(jnp.bfloat16), "dp", scatter_dimension=1, tiled=True
        ).astype(jnp.float32),
        lax.psum_scatter(
            grad_qkv_b.astype(jnp.bfloat16), "dp", scatter_dimension=1, tiled=True
        ).astype(jnp.float32),
        lax.psum_scatter(
            grad_up_b.astype(jnp.bfloat16), "dp", scatter_dimension=0, tiled=True
        ).astype(jnp.float32),
        lax.psum_scatter(
            grad_norm.astype(jnp.bfloat16), "dp", scatter_dimension=1, tiled=True
        ).astype(jnp.float32),
        lax.psum_scatter(
            grad_obias.astype(jnp.bfloat16), "dp", scatter_dimension=1, tiled=True
        ).astype(jnp.float32),
    )
    owned_qkv, owned_out, owned_up, owned_down, owned_bqkv, owned_bup, owned_norm, owned_obias = (
        reduced
    )
    qkv_rows = w_qkv.shape[0]
    new_qkv_block, qkv_left_new, qkv_right_new = shampoo(
        w_qkv.reshape(qkv_rows, -1), owned_qkv.reshape(qkv_rows, -1), qkv_left, qkv_right
    )
    new_w_qkv = new_qkv_block.reshape(w_qkv.shape)
    new_w_out, out_left_new, out_right_new = shampoo(w_out, owned_out, out_left, out_right)
    new_w_up, up_left_new, up_right_new = shampoo(w_up, owned_up, up_left, up_right)
    new_w_down, down_left_new, down_right_new = shampoo(w_down, owned_down, down_left, down_right)
    qkv_params, qkv_stats = vector_update(qkv_bias_state, owned_bqkv)
    obias_params, obias_stats = vector_update(out_bias_state, owned_obias)
    norm_new_params, norm_new_stats = vector_update(ln_state, owned_norm)
    new_up_bias, new_up_stat = vector_update(up_bias_state, owned_bup)
    new_vector_params = jnp.concatenate([qkv_params, obias_params, norm_new_params], axis=0)
    new_vector_stats = jnp.concatenate([qkv_stats, obias_stats, norm_new_stats], axis=0)
    return (
        output,
        input_grad,
        new_w_qkv,
        new_w_out,
        new_w_up,
        new_w_down,
        new_vector_params,
        new_vector_stats,
        new_up_bias,
        new_up_stat,
        qkv_left_new,
        qkv_right_new,
        out_left_new,
        out_right_new,
        up_left_new,
        up_right_new,
        down_left_new,
        down_right_new,
    )


def solution(mesh):
    return jax.shard_map(
        local,
        mesh=mesh,
        in_specs=(
            P("dp", "mp"),
            P("dp", "mp"),
            P("dp", None),
            P("dp", None, "mp"),
            P(None, None, ("mp", "dp")),
            P("mp", "dp"),
            P(None, None, ("mp", "dp")),
            P("dp", "mp"),
            P(None, ("mp", "dp")),
            P("mp", "dp"),
            P(None, None, ("mp", "dp")),
            P(None, "mp", "dp", None, None),
            P(None, "mp", "dp", None, None),
            P(None, "mp", "dp", None, None),
            P(None, "mp", "dp", None, None),
            P(None, "mp", "dp", None, None),
            P(None, "mp", "dp", None, None),
            P(None, "mp", "dp", None, None),
            P(None, "mp", "dp", None, None),
        ),
        out_specs=(
            P("dp", "mp"),
            P("dp", "mp"),
            P("dp", None, "mp"),
            P("mp", "dp"),
            P("dp", "mp"),
            P("mp", "dp"),
            P(None, ("mp", "dp")),
            P(None, ("mp", "dp")),
            P(("mp", "dp")),
            P(("mp", "dp")),
            P("mp", "dp", None, None),
            P("mp", "dp", None, None),
            P("mp", "dp", None, None),
            P("mp", "dp", None, None),
            P("mp", "dp", None, None),
            P("mp", "dp", None, None),
            P("mp", "dp", None, None),
            P("mp", "dp", None, None),
        ),
        check_vma=False,
    )
```

profile of v0, /device:TPU:0, one launch (start us, length us, event | category | flops | bytes accessed | tf_op | source)
XLA Modules:
  0.0 989.2 jit_solution(17249354589565544944)
XLA Ops:
  9.6 13.4 %all-gather = bf16[8,64,2]{1,2,0:T(2,128)(2,1)S(1)} all-gather(bf16[1,64,2]{1,2,0:T(2,128)(2,1)S(1)} %fusion.152), channel_id=1, replica_groups=mesh['mp'=4,'dp'=8] {'dp'}, dimensions={0}, use_global_device_ids=true | all-gather | bytes 2304 | tf_op jit(solution)/shard_map/all_gather | solution.py:259
  23.0 10.1 %all-reduce.2 = (f32[1024]{0:T(1024)S(1)}, f32[1024]{0:T(1024)S(1)}) all-reduce(f32[1024]{0:T(1024)S(1)} %get-tuple-element.180, f32[1024]{0:T(1024)S(1)} %get-tuple-element.179), channel_id=1, replica_groups=mesh['mp'=4,'dp'=8] {'mp'}, use_global_device_ids=true, to_apply=%region_3.0 | all-reduce | flops 2048 | bytes 16384 | tf_op jit(solution)/shard_map/psum | solution.py:263
  61.4 10.4 %all-gather.2 = bf16[8,1,256]{2,1,0:T(2,128)(2,1)S(1)} all-gather(bf16[1,1,256]{2,1,0:T(2,128)(2,1)S(1)} %reshape.462), channel_id=1, replica_groups=mesh['mp'=4,'dp'=8] {'dp'}, dimensions={0}, use_global_device_ids=true | all-gather | bytes 4608 | tf_op jit(solution)/shard_map/all_gather | solution.py:258
  72.5 13.0 %all-gather.11.cloned.1.call-done = bf16[1024,2048]{1,0:T(8,128)(2,1)} async-done(((bf16[1024,512]{1,0:T(8,128)(2,1)}), bf16[1024,2048]{1,0:T(8,128)(2,1)}) %all-gather.11.cloned.1.call-update) | async-done | bytes 4194320 | tf_op jit(solution)/shard_map/all_gather | solution.py:272
  85.5 67.4 %all-gather.13.cloned.1.call-done = bf16[2048,3,512]{0,2,1:T(8,128)(2,1)} async-done(((bf16[256,3,512]{0,2,1:T(8,128)(2,1)}), bf16[2048,3,512]{0,2,1:T(8,128)(2,1)}) %all-gather.13.cloned.1.call-update) | async-done | bytes 6291472 | tf_op jit(solution)/shard_map/all_gather | solution.py:253
  152.9 11.7 %convolution_add_fusion.1 = f32[1024,1536]{1,0:T(8,128)} fusion(bf16[1024,2048]{1,0:T(8,128)(2,1)} %all-gather.11.cloned.1.call-done, bf16[2048,1536]{0,1:T(8,128)(2,1)} %bitcast.317, f32[1536]{0:T(1024)S(1)} %reshape.455), kind=kOutput, calls=%fused_computation.92 | convolution fusion | flops 6444023808 | bytes 16783360 | tf_op jit(solution)/shard_map/dot_general | solution.py:278
  212.3 25.1 %all-gather.21.cloned.1.call-done = bf16[1024,2048]{1,0:T(8,128)(2,1)} async-done(((bf16[1024,512]{1,0:T(8,128)(2,1)}), bf16[1024,2048]{1,0:T(8,128)(2,1)}) %all-gather.21.cloned.1.call-update) | async-done | bytes 4194320 | tf_op jit(solution)/shard_map/all_gather | solution.py:273
  245.0 12.3 %conditional.5 = (f32[512,8,64]{0,2,1:T(8,128)S(1)}, f32[512,8,64]{0,2,1:T(8,128)S(1)}, f32[512,8,64]{0,2,1:T(8,128)S(1)}) conditional(s32[]{:T(128)} %bitcast.22, () %tuple.34, (s32[1024]{0:T(1024)S(1)}, bf16[1024,8,64]{0,2,1:T(8,128)(2,1)S(1)}, bf16[1024,8,64]{0,2,1:T(8,128)(2,1)S(1)}, f32[8,512]{1,0:T(8,128)S(1)}, ...), branch_computations={%region_19.20_spmd, %region_20.21_spmd} | conditional | flops 1364460032 | bytes 45449240 | solution.py:73
  287.9 33.6 %all-gather.17.cloned.1.call-done = bf16[2048,2048]{1,0:T(8,128)(2,1)} async-done(((bf16[256,2048]{1,0:T(8,128)(2,1)}), bf16[2048,2048]{1,0:T(8,128)(2,1)}) %all-gather.17.cloned.1.call-update) | async-done | bytes 8388624 | tf_op jit(solution)/shard_map/all_gather | solution.py:255
  321.6 14.5 %fusion.172 = f32[1024,2048]{1,0:T(8,128)} fusion(bf16[1024,2048]{1,0:T(8,128)(2,1)} %all-gather.11.cloned.1.call-done, bf16[2048,2048]{1,0:T(8,128)(2,1)} %all-gather.17.cloned.1.call-done), kind=kOutput, calls=%fused_computation.285 | convolution fusion | flops 8589934592 | bytes 20971520 | tf_op jit(solution)/shard_map/dot_general | solution.py:287
  336.0 68.6 %all-gather.19.cloned.1.call-done = bf16[2048,2048]{1,0:T(8,128)(2,1)} async-done(((bf16[2048,256]{1,0:T(8,128)(2,1)}), bf16[2048,2048]{1,0:T(8,128)(2,1)}) %all-gather.19.cloned.1.call-update) | async-done | bytes 8388624 | tf_op jit(solution)/shard_map/all_gather | solution.py:256
  404.7 18.8 %fusion.171 = (bf16[2048]{0:T(1024)(128)(2,1)S(1)}, bf16[1024,2048]{1,0:T(8,128)(2,1)S(1)}) fusion(f32[1024,2048]{1,0:T(8,128)} %fusion.172, f32[2048]{0:T(1024)S(1)} %bitcast.308, bf16[2048,2048]{1,0:T(8,128)(2,1)} %all-gather.19.cloned.1.call-done, bf16[1024,2048]{1,0:T(8,128)(2,1)} %all-gather.21.cloned.1.call-done, f32[1024]{0:T(1024)S(1)} %fusion.136), kind=kOutput, calls=%fused_computation.284 | convolution fusion | flops 8642361344 | bytes 25182208 | tf_op jit(solution)/shard_map/dot_general | solution.py:302
  423.5 12.8 %fusion.173 = f32[1024,2048]{1,0:T(8,128)S(1)} fusion(bf16[1024,2048]{1,0:T(8,128)(2,1)S(1)} %get-tuple-element.254, bf16[2048,2048]{1,0:T(8,128)(2,1)} %all-gather.17.cloned.1.call-done), kind=kOutput, calls=%fused_computation.286 | convolution fusion | flops 8589934592 | bytes 20971520 | tf_op jit(solution)/shard_map/dot_general | solution.py:327
  436.4 11.8 %add_convert_fusion = bf16[1024,2048]{1,0:T(8,128)(2,1)} fusion(f32[1024,2048]{1,0:T(8,128)S(1)} %fusion.173, bf16[1024,1536]{0,1:T(8,128)(2,1)S(1)} %bitcast.287, bf16[2048,1536]{0,1:T(8,128)(2,1)} %bitcast.318), kind=kOutput, calls=%fused_computation.74 | convolution fusion | flops 6446645248 | bytes 22020096 | tf_op jit(solution)/shard_map/dot_general | solution.py:325
  448.4 15.7 %fusion.159 = f32[1024,2048]{1,0:T(8,128)S(1)} fusion(bf16[2048,2048]{1,0:T(8,128)(2,1)} %all-gather.19.cloned.1.call-done, f32[1024,2048]{1,0:T(8,128)} %fusion.172, f32[2048]{0:T(1024)S(1)} %bitcast.309), kind=kOutput, calls=%fused_computation.273 | convolution fusion | flops 8610906112 | bytes 25174016 | tf_op jit(solution)/shard_map/dot_general | solution.py:292
  475.8 9.7 all-gather.3
  485.6 13.6 %reduce-scatter.18.cloned.1.call-done = bf16[1024,512]{1,0:T(8,128)(2,1)} async-done(((bf16[1024,2048]{1,0:T(8,128)(2,1)}), bf16[1024,512]{1,0:T(8,128)(2,1)}) %reduce-scatter.18.cloned.1.call-update) | async-done | bytes 1048592 | tf_op jit(solution)/shard_map/reduce_scatter | solution.py:328
  513.2 42.5 %reduce-scatter.16.cloned.1.call-done = bf16[1024,512]{1,0:T(8,128)(2,1)} async-done(((bf16[1024,2048]{1,0:T(8,128)(2,1)}), bf16[1024,512]{1,0:T(8,128)(2,1)}) %reduce-scatter.16.cloned.1.call-update) | async-done | bytes 1048592 | tf_op jit(solution)/shard_map/reduce_scatter | solution.py:295
  560.6 11.5 %convolution_convert_fusion.2 = bf16[2048,3,512]{2,0,1:T(8,128)(2,1)} fusion(bf16[3,512,1024]{2,1,0:T(8,128)(2,1)} %bitcast.286, bf16[1024,2048]{1,0:T(8,128)(2,1)} %all-gather.11.cloned.1.call-done), kind=kOutput, calls=%fused_computation.91 | convolution fusion | flops 6445596672 | bytes 13631488 | tf_op jit(solution)/shard_map/dot_general | solution.py:321
  572.2 14.0 %convolution_convert_fusion.1 = bf16[2048,2048]{1,0:T(8,128)(2,1)} fusion(bf16[1024,2048]{1,0:T(8,128)(2,1)} %all-gather.11.cloned.1.call-done, bf16[1024,2048]{1,0:T(8,128)(2,1)} %copy-done.51), kind=kOutput, calls=%fused_computation.87 | convolution fusion | flops 8594128896 | bytes 16777216 | tf_op jit(solution)/shard_map/dot_general | solution.py:305
  586.5 19.8 %convolution_convert_fusion = bf16[2048,2048]{1,0:T(8,128)(2,1)} fusion(bf16[1024,2048]{1,0:T(8,128)(2,1)} %all-gather.21.cloned.1.call-done, f32[1024]{0:T(1024)S(1)} %fusion.136, f32[1024,2048]{1,0:T(8,128)} %fusion.172, f32[2048]{0:T(1024)S(1)} %bitcast.310), kind=kOutput, calls=%fused_computation.86 | convolution fusion | flops 8621391872 | bytes 20983808 | tf_op jit(solution)/shard_map/dot_general | solution.py:304
  610.3 16.4 %all-reduce = bf16[2048]{0:T(1024)(128)(2,1)S(1)} all-reduce(bf16[2048]{0:T(1024)(128)(2,1)S(1)} %get-tuple-element.253), channel_id=11, replica_groups=mesh['mp'=4,'dp'=8] {'dp'}, use_global_device_ids=true, to_apply=%region_38.39.clone | all-reduce | flops 2048 | bytes 8192
  637.1 20.2 %reduce-scatter.32.cloned.1.call-done = bf16[64,2]{1,0:T(8,128)(2,1)} async-done(((bf16[512,2]{1,0:T(8,128)(2,1)}), bf16[64,2]{1,0:T(8,128)(2,1)}) %reduce-scatter.32.cloned.1.call-update) | async-done | bytes 272
  658.1 30.2 %reduce-scatter.30.cloned.1.call-done = bf16[64,2]{1,0:T(8,128)(2,1)} async-done(((bf16[512,2]{1,0:T(8,128)(2,1)}), bf16[64,2]{1,0:T(8,128)(2,1)}) %reduce-scatter.30.cloned.1.call-update) | async-done | bytes 272
  690.4 68.4 %reduce-scatter.20.cloned.1.call-done = bf16[256,3,512]{2,0,1:T(8,128)(2,1)} async-done(((bf16[2048,3,512]{2,0,1:T(8,128)(2,1)}), bf16[256,3,512]{2,0,1:T(8,128)(2,1)}) %reduce-scatter.20.cloned.1.call-update) | async-done | bytes 786448 | tf_op jit(solution)/shard_map/reduce_scatter | solution.py:343
  761.1 12.5 %fusion.63 = f32[256,1536]{1,0:T(8,128)} fusion(f32[256,1536]{1,0:T(8,128)S(1)} %copy.152, f32[1536,256]{1,0:T(8,128)S(1)} %fusion.130, f32[2,1,1,1536,1536]{4,3,2,1,0:T(8,128)} %param.37), kind=kOutput, calls=%fused_computation.100 | convolution fusion | flops 7248150528 | bytes 14155776 | tf_op jit(solution)/shard_map/dot_general | solution.py:205
  788.2 61.4 %reduce-scatter.24.cloned.1.call-done = bf16[256,2048]{1,0:T(8,128)(2,1)} async-done(((bf16[2048,2048]{1,0:T(8,128)(2,1)}), bf16[256,2048]{1,0:T(8,128)(2,1)}) %reduce-scatter.24.cloned.1.call-update) | async-done | bytes 1048592 | tf_op jit(solution)/shard_map/reduce_scatter | solution.py:349
  852.1 17.7 %fusion.69 = f32[256,2048]{1,0:T(8,128)} fusion(f32[256,2048]{1,0:T(8,128)S(1)} %copy-done.8, f32[2048,256]{1,0:T(8,128)S(1)} %fusion.127, f32[2,1,1,2048,2048]{4,3,2,1,0:T(8,128)} %param.41), kind=kOutput, calls=%fused_computation.106 | convolution fusion | flops 12885426176 | bytes 23068672 | tf_op jit(solution)/shard_map/dot_general | solution.py:205
  869.8 70.7 %reduce-scatter.26.cloned.1.call-done = bf16[2048,256]{1,0:T(8,128)(2,1)} async-done(((bf16[2048,2048]{1,0:T(8,128)(2,1)}), bf16[2048,256]{1,0:T(8,128)(2,1)}) %reduce-scatter.26.cloned.1.call-update) | async-done | bytes 1048592 | tf_op jit(solution)/shard_map/reduce_scatter | solution.py:352
  940.4 13.0 %fusion.42 = f32[256,2048]{1,0:T(8,128)S(1)} fusion(bf16[2048,256]{1,0:T(8,128)(2,1)} %reduce-scatter.26.cloned.1.call-done, f32[2,1,1,2048,2048]{4,3,2,1,0:T(8,128)} %param.42), kind=kOutput, calls=%fused_computation.53 | convolution fusion | flops 12884901888 | bytes 19922944 | tf_op jit(solution)/shard_map/dot_general | solution.py:206
  958.2 11.0 %fusion.41 = f32[1,1,2048,2048]{3,2,1,0:T(8,128)} fusion(f32[2,1,1,2048,2048]{4,3,2,1,0:T(8,128)} %param.41, bf16[256,2048]{1,0:T(8,128)(2,1)S(1)} %copy-done.4), kind=kOutput, calls=%fused_computation.52 | convolution fusion | flops 2155872256 | bytes 35651584 | tf_op jit(solution)/shard_map/dot_general | solution.py:204
  970.4 10.9 %fusion.39 = f32[1,1,2048,2048]{3,2,1,0:T(8,128)} fusion(f32[2,1,1,2048,2048]{4,3,2,1,0:T(8,128)} %param.42, bf16[2048,256]{1,0:T(8,128)(2,1)S(1)} %copy-done.1), kind=kOutput, calls=%fused_computation.49 | convolution fusion | flops 2155872256 | bytes 35651584 | tf_op jit(solution)/shard_map/dot_general | solution.py:203
  (288 shorter events, 212.0 us)
Async XLA Ops:
  7.2 32.3 %copy-start.18 = (f32[512,256]{1,0:T(8,128)S(1)}, f32[512,256]{1,0:T(8,128)}, u32[]{:S(2)}) copy-start(f32[512,256]{1,0:T(8,128)} %param.30) | copy-start | bytes 1572868
  7.2 78.3 %all-gather.11.cloned.1.call-start = ((), (), s32[]{:S(2)}) async-start(), calls=%async_computation.9 | async-start | bytes 5242880 | tf_op jit(solution)/shard_map/all_gather | solution.py:272
  36.4 23.8 %copy-start.45 = (f32[2,256]{1,0:T(2,128)S(1)}, f32[2,256]{1,0:T(2,128)}, u32[]{:S(2)}) copy-start(f32[2,256]{1,0:T(2,128)} %param.33) | copy-start | bytes 6148
  36.4 116.4 %all-gather.13.cloned.1.call-start = ((), (), s32[]{:S(2)}) async-start(), calls=%async_computation.10 | async-start | bytes 7077888 | tf_op jit(solution)/shard_map/all_gather | solution.py:253
  38.4 126.2 %copy-start.6 = (f32[256,3,512]{0,2,1:T(8,128)}, f32[256,3,512]{0,2,1:T(8,128)S(1)}, u32[]{:S(2)}) copy-start(f32[256,3,512]{0,2,1:T(8,128)S(1)} %copy.133) | copy-start | bytes 4718596
  39.4 172.9 %all-gather.15.cloned.1.call-start = ((), (), s32[]{:S(2)}) async-start(), calls=%async_computation.11 | async-start | bytes 2359296 | tf_op jit(solution)/shard_map/all_gather | solution.py:254
  40.3 197.2 %all-gather.21.cloned.1.call-start = ((), (), s32[]{:S(2)}) async-start(), calls=%async_computation.15 | async-start | bytes 5242880 | tf_op jit(solution)/shard_map/all_gather | solution.py:273
  40.8 280.7 %all-gather.17.cloned.1.call-start = ((), (), s32[]{:S(2)}) async-start(), calls=%async_computation.12 | async-start | bytes 9437184 | tf_op jit(solution)/shard_map/all_gather | solution.py:255
  43.7 360.9 %all-gather.19.cloned.1.call-start = ((), (), s32[]{:S(2)}) async-start(), calls=%async_computation.13 | async-start | bytes 9437184 | tf_op jit(solution)/shard_map/all_gather | solution.py:256
  46.5 452.7 %reduce-scatter.18.cloned.1.call-start = ((), (), s32[]{:S(2)}) async-start(), calls=%async_computation.16 | async-start | bytes 5242880 | tf_op jit(solution)/shard_map/reduce_scatter | solution.py:328
  72.5 192.3 %copy-start.17 = (pred[512,512]{0,1:T(8,128)(4,1)}, pred[512,512]{0,1:T(8,128)(4,1)S(1)}, u32[]{:S(2)}) copy-start(pred[512,512]{0,1:T(8,128)(4,1)S(1)} %get-tuple-element.257) | copy-start | bytes 786436
  190.4 69.0 %copy-start.35 = (f32[8,512]{1,0:T(8,128)}, f32[8,512]{1,0:T(8,128)S(1)}, u32[]{:S(2)}) copy-start(f32[8,512]{1,0:T(8,128)S(1)} %log_add_fusion) | copy-start | bytes 49156
  202.4 62.5 %copy-start.37 = (f32[8,512]{1,0:T(8,128)}, f32[8,512]{1,0:T(8,128)S(1)}, u32[]{:S(2)}) copy-start(f32[8,512]{1,0:T(8,128)S(1)} %log_add_fusion.1) | copy-start | bytes 49156
  448.2 107.6 %reduce-scatter.16.cloned.1.call-start = ((), (), s32[]{:S(2)}) async-start(), calls=%async_computation.14 | async-start | bytes 5242880 | tf_op jit(solution)/shard_map/reduce_scatter | solution.py:295
  468.6 30.6 %copy-start.5 = (bf16[1024,512]{1,0:T(8,128)(2,1)S(1)}, bf16[1024,512]{1,0:T(8,128)(2,1)}, u32[]{:S(2)}) copy-start(bf16[1024,512]{1,0:T(8,128)(2,1)} %param.25) | copy-start | bytes 3145732
  468.6 30.6 %copy-start.30 = (f32[1024]{0:T(1024)S(1)}, f32[1024]{0:T(1024)}, u32[]{:S(2)}) copy-start(f32[1024]{0:T(1024)} %copy-done.29) | copy-start | bytes 12292
  468.6 30.6 %copy-start.32 = (f32[1024]{0:T(1024)S(1)}, f32[1024]{0:T(1024)}, u32[]{:S(2)}) copy-start(f32[1024]{0:T(1024)} %copy-done.31) | copy-start | bytes 12292
  468.6 30.5 %copy-start.34 = (f32[1,512]{1,0:T(1,128)S(1)}, f32[1,512]{1,0:T(1,128)}, u32[]{:S(2)}) copy-start(f32[1,512]{1,0:T(1,128)} %copy-done.33) | copy-start | bytes 6148
  468.6 140.8 %reduce-scatter.28.cloned.1.call-start = ((), (), s32[]{:S(2)}) async-start(), calls=%async_computation.21 | async-start | bytes 147456
  469.5 86.2 %copy-start.11 = (bf16[1024,512]{1,0:T(8,128)(2,1)S(1)}, bf16[1024,512]{1,0:T(8,128)(2,1)}, u32[]{:S(2)}) copy-start(bf16[1024,512]{1,0:T(8,128)(2,1)} %param.26) | copy-start | bytes 3145732
  469.5 157.8 %reduce-scatter.22.cloned.1.call-start = ((), (), s32[]{:S(2)}) async-start(), calls=%async_computation.18 | async-start | bytes 2359296 | tf_op jit(solution)/shard_map/reduce_scatter | solution.py:346
  475.7 181.6 %reduce-scatter.32.cloned.1.call-start = ((), (), s32[]{:S(2)}) async-start(), calls=%async_computation.23 | async-start | bytes 147456
  559.6 128.7 %reduce-scatter.30.cloned.1.call-start = ((), (), s32[]{:S(2)}) async-start(), calls=%async_computation.22 | async-start | bytes 147456
  560.5 198.2 %reduce-scatter.20.cloned.1.call-start = ((), (), s32[]{:S(2)}) async-start(), calls=%async_computation.17 | async-start | bytes 7077888 | tf_op jit(solution)/shard_map/reduce_scatter | solution.py:343
  572.2 277.5 %reduce-scatter.24.cloned.1.call-start = ((), (), s32[]{:S(2)}) async-start(), calls=%async_computation.19 | async-start | bytes 9437184 | tf_op jit(solution)/shard_map/reduce_scatter | solution.py:349
  586.3 354.2 %reduce-scatter.26.cloned.1.call-start = ((), (), s32[]{:S(2)}) async-start(), calls=%async_computation.20 | async-start | bytes 9437184 | tf_op jit(solution)/shard_map/reduce_scatter | solution.py:352
  606.3 82.8 %copy-start.46 = (f32[2,2,64]{2,1,0:T(2,128)S(1)}, f32[2,2,64]{2,1,0:T(2,128)}, u32[]{:S(2)}) copy-start(f32[2,2,64]{2,1,0:T(2,128)} %param.35) | copy-start | bytes 3076
  608.2 152.0 %copy-start.26 = (f32[2,1,1,256,256]{4,3,2,1,0:T(8,128)S(1)}, f32[2,1,1,256,256]{4,3,2,1,0:T(8,128)}, u32[]{:S(2)}) copy-start(f32[2,1,1,256,256]{4,3,2,1,0:T(8,128)} %param.36) | copy-start | bytes 1572868
  779.1 70.5 %copy-start.27 = (f32[2,1,1,256,256]{4,3,2,1,0:T(8,128)S(1)}, f32[2,1,1,256,256]{4,3,2,1,0:T(8,128)}, u32[]{:S(2)}) copy-start(f32[2,1,1,256,256]{4,3,2,1,0:T(8,128)} %param.40) | copy-start | bytes 1572868
  779.1 72.9 %copy-start.8 = (f32[256,2048]{1,0:T(8,128)S(1)}, f32[256,2048]{1,0:T(8,128)}, u32[]{:S(2)}) copy-start(f32[256,2048]{1,0:T(8,128)} %param.32) | copy-start | bytes 6291460
  869.8 83.7 %copy-start.9 = (f32[2048,256]{1,0:T(8,128)S(1)}, f32[2048,256]{1,0:T(8,128)}, u32[]{:S(2)}) copy-start(f32[2048,256]{1,0:T(8,128)} %param.34) | copy-start | bytes 6291460
  869.8 88.5 %copy-start.4 = (bf16[256,2048]{1,0:T(8,128)(2,1)S(1)}, bf16[256,2048]{1,0:T(8,128)(2,1)}, u32[]{:S(2)}) copy-start(bf16[256,2048]{1,0:T(8,128)(2,1)} %reduce-scatter.24.cloned.1.call-done) | copy-start | bytes 3145732
  (41 other events, 317.4 us)
Sparse Core Ops, SparseCore 0:
  36.5 48.9 all-gather.10
  87.7 65.1 all-gather.12
  155.0 29.0 all-gather.14
  185.8 51.6 all-gather.20
  239.5 82.0 all-gather.16
  323.6 81.0 all-gather.18
  448.3 50.8 reduce-scatter.17
  503.0 52.6 reduce-scatter.15
  558.5 30.1 reduce-scatter.27
  591.5 34.0 reduce-scatter.21
  628.5 28.7 reduce-scatter.31
  660.0 28.2 reduce-scatter.29
  690.7 68.0 reduce-scatter.19
  761.6 87.9 reduce-scatter.23
  852.4 87.9 reduce-scatter.25
where the time goes:
time: 999 us; the launch traced here: 989 us
  waiting for transfers between devices  515 us (52%)
  matrix products  300 us (30%)
  blocking collectives  77.4 us (8%)
  other arithmetic  42.7 us (4%)
  local copies, waits for them, and re-layouts  34.5 us (3%)
  between operations  17.2 us (2%)
    reduce_scatter x1, waiting for transfers between devices, local(): lax.psum_scatter(grad_down_w.astype(jnp.bfloat16), 'dp', scatter_dimensio...  70.7 us
    all_gather x1, waiting for transfers between devices, local(): lax.all_gather(sent[3], 'dp', axis=1, tiled=True)  68.6 us
    reduce_scatter x1, waiting for transfers between devices, local(): lax.psum_scatter(grad_qkv_w.astype(jnp.bfloat16), 'dp', scatter_dimension...  68.4 us
    all_gather x1, waiting for transfers between devices, local(): lax.all_gather(sent[0], 'dp', axis=0, tiled=True)  67.4 us
    reduce_scatter x1, waiting for transfers between devices, local(): lax.psum_scatter(grad_up_w.astype(jnp.bfloat16), 'dp', scatter_dimension=...  61.4 us
    unnamed x18, waiting for transfers between devices  51.1 us
    reduce_scatter x1, waiting for transfers between devices, local(): lax.psum_scatter(partial_sum.astype(jnp.bfloat16), 'mp', scatter_dimensio...  42.5 us
    dot_general x4, matrix products, shampoo(): jnp.dot(jnp.dot(left[1, 0, 0], grad_block, precision=highest), right[1, 0...  37.9 us
  transfers between devices with their start and end apart: 15, of which 12 were waited for; matrix products, arithmetic and copies ran while one was open for 28% of the time, Pallas kernels for 0%

commit v1 on v0

v1 whole, which is shorter than its diff:
```python
import functools
import math

import jax
import jax.numpy as jnp
from jax import lax
from jax.experimental import pallas as pl
from jax.experimental.pallas import tpu as pltpu
from jax.sharding import PartitionSpec as P

HEAD_DIM = 64
ROT_DIM = 32
LANES = 128
ROW_TILE = 256


norm_eps = 1e-05
matrix_rate = 1.0
vector_rate = 0.4
masked_score = -1e30


def segment_layout(lengths, row_count):
    positions = jnp.arange(row_count, dtype=jnp.int32)
    seq_ends = jnp.cumsum(lengths)
    finished = seq_ends[None, :] <= positions[:, None]
    segment = jnp.sum(finished.astype(jnp.int32), axis=1)
    starting = jnp.max(jnp.where(finished, seq_ends[None, :], 0), axis=1)
    is_valid = positions < seq_ends[-1]
    segment = jnp.where(is_valid, segment, lengths.shape[0] + positions)
    offsets = (positions - starting).astype(jnp.float32)
    return (segment, offsets, is_valid.astype(jnp.float32))


def rope_tables(offsets):
    half_rot = ROT_DIM // 2
    freq_index = jnp.arange(half_rot, dtype=jnp.float32)
    inverse = jnp.exp(-(2.0 * freq_index / ROT_DIM) * math.log(10000.0))
    angles = offsets[:, None] * inverse[None, :]
    return (jnp.cos(angles), jnp.sin(angles))


def gelu_pair(values):
    square = values * values
    inner = math.sqrt(2.0 / math.pi) * values * (1.0 + 0.044715 * square)
    bent = jnp.tanh(inner)
    half = 0.5 * (1.0 + bent)
    slope = half + 0.5 * values * (1.0 - bent * bent) * math.sqrt(2.0 / math.pi) * (
        1.0 + 3.0 * 0.044715 * square
    )
    return (values * half, slope)


def take(array, index, axis=0):
    return lax.dynamic_index_in_dim(array, index, axis, keepdims=False)


def mp_pairs(bit):
    return [(source, source ^ bit) for source in range(lax.axis_size("mp"))]


def mp_gather(share):
    if lax.axis_size("mp") != 4:
        return lax.all_gather(share, "mp", axis=1, tiled=True)
    place = lax.axis_index("mp")
    rows, width = share.shape
    half = rows // 2
    over_x = lax.ppermute(share, "mp", mp_pairs(1))
    over_y = lax.ppermute(share, "mp", mp_pairs(2))
    top = lax.ppermute(over_y[:half], "mp", mp_pairs(1))
    bottom = lax.ppermute(over_x[half:], "mp", mp_pairs(2))
    whole = jnp.zeros((rows, 4 * width), share.dtype)
    whole = lax.dynamic_update_slice(whole, share, (0, place * width))
    whole = lax.dynamic_update_slice(whole, over_x, (0, (place ^ 1) * width))
    whole = lax.dynamic_update_slice(whole, over_y, (0, (place ^ 2) * width))
    whole = lax.dynamic_update_slice(whole, top, (0, (place ^ 3) * width))
    return lax.dynamic_update_slice(whole, bottom, (half, (place ^ 3) * width))


def summed(*terms):
    total = terms[0].astype(jnp.float32)
    for term in terms[1:]:
        total = total + term.astype(jnp.float32)
    return total


def mp_scatter(partial):
    if lax.axis_size("mp") != 4:
        return lax.psum_scatter(partial, "mp", scatter_dimension=1, tiled=True).astype(jnp.float32)
    place = lax.axis_index("mp")
    rows = partial.shape[0]
    width = partial.shape[1] // 4
    half = rows // 2

    def part(start, bits):
        return lax.dynamic_slice(partial, (start, (place ^ bits) * width), (half, width))

    top_far = lax.ppermute(part(0, 3), "mp", mp_pairs(1))
    bottom_far = lax.ppermute(part(half, 3), "mp", mp_pairs(2))
    top_near = lax.ppermute(part(0, 1), "mp", mp_pairs(1))
    bottom_near = lax.ppermute(part(half, 2), "mp", mp_pairs(2))
    top_send = summed(part(0, 2), top_far).astype(jnp.bfloat16)
    bottom_send = summed(part(half, 1), bottom_far).astype(jnp.bfloat16)
    top_last = lax.ppermute(top_send, "mp", mp_pairs(2))
    bottom_last = lax.ppermute(bottom_send, "mp", mp_pairs(1))
    top = summed(part(0, 0), top_near, top_last)
    bottom = summed(part(half, 0), bottom_near, bottom_last)
    return jnp.concatenate([top, bottom], axis=0)


def parity_columns(rows, parity):
    size = lax.axis_size("dp")
    width = rows.shape[1] // size
    pieces = [
        lax.dynamic_slice_in_dim(rows, (2 * chip + parity) * width, width, 1)
        for chip in range(size // 2)
    ]
    return jnp.concatenate(pieces, axis=1)


def over_rows(left, right):
    return lax.dot_general(left, right, (((0,), (0,)), ((), ())), preferred_element_type=jnp.float32)


def tie(value, *others):
    return lax.optimization_barrier((value,) + others)[0]


class OwnerSum:
    def __init__(self, far_product):
        self.size = lax.axis_size("dp")
        self.count = self.size // 2
        self.spot = lax.axis_index("dp") // 2
        self.step = 0
        self.sent = 0
        self.rising = None
        self.falling = None
        self.from_sibling = lax.ppermute(
            far_product.astype(jnp.bfloat16), "dp", [(at, at ^ 1) for at in range(self.size)]
        )

    def add_near(self, near_product):
        blocks = summed(near_product, self.from_sibling).astype(jnp.bfloat16)
        self.blocks = blocks.reshape(self.count, -1, blocks.shape[1])
        return self.ready()

    def ready(self):
        self.step += 1
        last = self.count - 1
        up_block = take(self.blocks, jnp.clip(self.count + self.spot - self.step, 0, last))
        down_block = take(self.blocks, jnp.clip(self.spot - self.count + self.step, 0, last))
        if self.rising is not None:
            up_block = summed(up_block, self.rising).astype(jnp.bfloat16)
            down_block = summed(down_block, self.falling).astype(jnp.bfloat16)
        self.sends = (up_block, down_block)
        return self.sends

    def send(self):
        up_pairs = [
            (2 * chip + core, 2 * chip + 2 + core)
            for chip in range(self.step)
            for core in range(2)
        ]
        down_pairs = [
            (2 * chip + core, 2 * chip - 2 + core)
            for chip in range(self.count - self.step, self.count)
            for core in range(2)
        ]
        self.sent += 1
        self.rising = lax.ppermute(self.sends[0], "dp", up_pairs)
        self.falling = lax.ppermute(self.sends[1], "dp", down_pairs)

    def advance(self):
        self.send()
        if self.step < self.count - 1:
            return self.ready()
        return (self.rising, self.falling)

    def rest(self):
        while self.sent < self.count - 1:
            self.advance()
        return self

    def total(self):
        return summed(take(self.blocks, self.spot), self.rising, self.falling)


def exchange_kernel(axes, count, same, in_ref, out_ref, send_sems, recv_sems):
    sizes = [lax.axis_size(axis) for axis in axes]
    place = lax.axis_index(axes[0])
    for axis, size in zip(axes[1:], sizes[1:]):
        place = place * size + lax.axis_index(axis)

    def device(peer):
        if len(axes) == 1:
            return {axes[0]: peer}
        return {axes[0]: peer // sizes[1], axes[1]: lax.rem(peer, sizes[1])}

    barrier = pltpu.get_barrier_semaphore()

    def greet(step, carry):
        peer = lax.rem(place + step, count)
        pl.semaphore_signal(
            barrier, inc=1, device_id=device(peer), device_id_type=pl.DeviceIdType.MESH
        )
        return carry

    lax.fori_loop(1, count, greet, 0)
    pl.semaphore_wait(barrier, count - 1)

    def copy_to(step):
        peer = lax.rem(place + step, count)
        source = in_ref.at[0] if same else in_ref.at[peer]
        return pltpu.make_async_remote_copy(
            src_ref=source,
            dst_ref=out_ref.at[place],
            send_sem=send_sems.at[step],
            recv_sem=recv_sems.at[step],
            device_id=device(peer),
            device_id_type=pl.DeviceIdType.MESH,
        )

    def begin(step, carry):
        copy_to(step).start()
        return carry

    def finish(step, carry):
        copy_to(step).wait()
        return carry

    lax.fori_loop(1, count, begin, 0)
    out_ref[place] = in_ref[0] if same else in_ref[place]
    lax.fori_loop(1, count, finish, 0)


def exchange(values, axes, collective_id, same):
    count = 1
    for axis in axes:
        count *= lax.axis_size(axis)
    return pl.pallas_call(
        functools.partial(exchange_kernel, axes, count, same),
        out_shape=jax.ShapeDtypeStruct((count,) + values.shape[1:], values.dtype),
        in_specs=[pl.BlockSpec(memory_space=pltpu.VMEM)],
        out_specs=pl.BlockSpec(memory_space=pltpu.VMEM),
        scratch_shapes=[pltpu.SemaphoreType.DMA((count,)), pltpu.SemaphoreType.DMA((count,))],
        compiler_params=pltpu.CompilerParams(collective_id=collective_id, has_side_effects=True),
        name="exchange",
    )(values)


def contract(left, right, left_axis, right_axis):
    return lax.dot_general(
        left, right, (((left_axis,), (right_axis,)), ((), ())), preferred_element_type=jnp.float32
    )


def attention_kernel(
    head_cols,
    q_ref,
    k_ref,
    v_ref,
    go_ref,
    seg_col_ref,
    seg_row_ref,
    keep_ref,
    ahead_ref,
    behind_ref,
    or_ref,
    grad_ref,
    bias_ref,
    q_low,
    k_low,
    v_low,
    dq_acc,
    dk_acc,
    dv_acc,
):
    rows = q_ref.shape[0]
    tiles = rows // ROW_TILE
    pair = pl.program_id(0)
    scale = HEAD_DIM ** (-0.5)

    @pl.when(pair == 0)
    def _():
        for tile in range(tiles):
            here = pl.ds(tile * ROW_TILE, ROW_TILE)
            shape = (ROW_TILE, rows)
            row_ids = lax.broadcasted_iota(jnp.int32, shape, 0) + tile * ROW_TILE
            key_ids = lax.broadcasted_iota(jnp.int32, shape, 1)
            allowed = (seg_col_ref[here, :] == seg_row_ref[...]) & (key_ids <= row_ids)
            bias_ref[here, :] = jnp.where(allowed, 0.0, masked_score)

    def turned(values, here, direction):
        ahead = pltpu.roll(values, LANES - ROT_DIM // 2, 1)
        behind = pltpu.roll(values, ROT_DIM // 2, 1)
        return values * keep_ref[here, :] + direction * (
            ahead * ahead_ref[here, :] + behind * behind_ref[here, :]
        )

    for tile in range(tiles):
        here = pl.ds(tile * ROW_TILE, ROW_TILE)
        q_low[here, :] = (turned(q_ref[here, :], here, 1.0).astype(jnp.bfloat16)) * scale
        k_low[here, :] = turned(k_ref[here, :], here, 1.0).astype(jnp.bfloat16)
        v_low[here, :] = v_ref[here, :].astype(jnp.bfloat16)
    dk_acc[...] = jnp.zeros_like(dk_acc)
    dv_acc[...] = jnp.zeros_like(dv_acc)

    lane = lax.broadcasted_iota(jnp.int32, (ROW_TILE, LANES), 1)
    for tile in range(tiles):
        here = pl.ds(tile * ROW_TILE, ROW_TILE)
        reach = (tile + 1) * ROW_TILE
        keys = pl.ds(0, reach)
        outs = []
        query_grads = []
        for head in range(LANES // HEAD_DIM):
            mine = (lane >= head * HEAD_DIM) & (lane < (head + 1) * HEAD_DIM)
            none = jnp.zeros((ROW_TILE, LANES), jnp.bfloat16)
            query = jnp.where(mine, q_low[here, :], none)
            grad_out = jnp.where(mine, go_ref[here, :], none)
            scores = contract(query, k_low[keys, :], 1, 1) + bias_ref[here, keys]
            peak = jnp.max(scores, axis=1, keepdims=True)
            weights = jnp.exp(scores - peak)
            share = 1.0 / jnp.sum(weights, axis=1, keepdims=True)
            probs = weights * share
            probs_low = probs.astype(jnp.bfloat16)
            outs.append(contract(probs_low, v_low[keys, :], 1, 0))
            grad_probs = contract(grad_out, v_low[keys, :], 1, 1)
            delta = jnp.sum(probs * grad_probs, axis=1, keepdims=True)
            grad_scores = (probs * (grad_probs - delta)).astype(jnp.bfloat16)
            query_grads.append(contract(grad_scores, k_low[keys, :], 1, 0))
            dk_acc[keys, :] += contract(grad_scores, query, 0, 0)
            dv_acc[keys, :] += contract(probs_low, grad_out, 0, 0)
        first = lane < HEAD_DIM
        or_ref[here, :] = jnp.where(first, outs[0], outs[1]).astype(jnp.bfloat16)
        dq_acc[here, :] = jnp.where(first, query_grads[0], query_grads[1])
    column = pl.multiple_of(pair * LANES, LANES)
    for tile in range(tiles):
        here = pl.ds(tile * ROW_TILE, ROW_TILE)
        query_grad = turned(dq_acc[here, :], here, -1.0) * scale
        grad_ref[here, pl.ds(column, LANES)] = query_grad.astype(jnp.bfloat16)
        key_grad = turned(dk_acc[here, :], here, -1.0)
        grad_ref[here, pl.ds(head_cols + column, LANES)] = key_grad.astype(jnp.bfloat16)
        grad_ref[here, pl.ds(2 * head_cols + column, LANES)] = dv_acc[here, :].astype(jnp.bfloat16)


def attention(projected, grad_attended, segment, cosine, sine):
    rows, columns = projected.shape
    head_cols = columns // 3
    pairs = head_cols // LANES
    still = jnp.ones((rows, HEAD_DIM - ROT_DIM), jnp.float32)
    zero = jnp.zeros((rows, ROT_DIM // 2), jnp.float32)
    repeat = (1, LANES // HEAD_DIM)
    keep = jnp.tile(jnp.concatenate([cosine, cosine, still], axis=1), repeat)
    ahead = jnp.tile(jnp.concatenate([-sine, zero, 0.0 * still], axis=1), repeat)
    behind = jnp.tile(jnp.concatenate([zero, sine, 0.0 * still], axis=1), repeat)
    whole = lambda pair: (0, 0)
    table = pl.BlockSpec((rows, LANES), whole)
    flops = 12 * rows * rows * LANES * 2 * pairs
    return pl.pallas_call(
        functools.partial(attention_kernel, head_cols),
        grid=(pairs,),
        in_specs=[
            pl.BlockSpec((rows, LANES), lambda pair: (0, pair)),
            pl.BlockSpec((rows, LANES), lambda pair: (0, pairs + pair)),
            pl.BlockSpec((rows, LANES), lambda pair: (0, 2 * pairs + pair)),
            pl.BlockSpec((rows, LANES), lambda pair: (0, pair)),
            pl.BlockSpec((rows, 1), whole),
            pl.BlockSpec((1, rows), whole),
            table,
            table,
            table,
        ],
        out_specs=[
            pl.BlockSpec((rows, LANES), lambda pair: (0, pair)),
            pl.BlockSpec((rows, columns), whole),
        ],
        out_shape=[
            jax.ShapeDtypeStruct((rows, head_cols), jnp.bfloat16),
            jax.ShapeDtypeStruct((rows, columns), jnp.bfloat16),
        ],
        scratch_shapes=[
            pltpu.VMEM((rows, rows), jnp.float32),
            pltpu.VMEM((rows, LANES), jnp.bfloat16),
            pltpu.VMEM((rows, LANES), jnp.bfloat16),
            pltpu.VMEM((rows, LANES), jnp.bfloat16),
            pltpu.VMEM((rows, LANES), jnp.float32),
            pltpu.VMEM((rows, LANES), jnp.float32),
            pltpu.VMEM((rows, LANES), jnp.float32),
        ],
        compiler_params=pltpu.CompilerParams(vmem_limit_bytes=40 * 1024 * 1024),
        cost_estimate=pl.CostEstimate(
            flops=flops, bytes_accessed=rows * columns * 8, transcendentals=rows * rows * pairs
        ),
        name="attention",
    )(
        projected,
        projected,
        projected,
        grad_attended,
        segment[:, None],
        segment[None, :],
        keep,
        ahead,
        behind,
    )


def dot_f32(left, right, left_axis, right_axis):
    return lax.dot_general(
        left.astype(jnp.bfloat16),
        right.astype(jnp.bfloat16),
        (((left_axis,), (right_axis,)), ((), ())),
        preferred_element_type=jnp.float32,
    )


def shampoo(weight_block, grad_block, left, right):
    left_new = 0.5 * left[0, 0, 0] + 0.5 * dot_f32(grad_block, grad_block, 1, 1)
    right_new = 0.5 * right[0, 0, 0] + 0.5 * dot_f32(grad_block, grad_block, 0, 0)
    step_block = dot_f32(dot_f32(left[1, 0, 0], grad_block, 1, 0), right[1, 0, 0], 1, 0)
    return (weight_block - matrix_rate * step_block, left_new[None, None], right_new[None, None])


def shampoo_turned(weight_block, turned_grad, left, right):
    left_new = 0.5 * left[0, 0, 0] + 0.5 * dot_f32(turned_grad, turned_grad, 0, 0)
    right_new = 0.5 * right[0, 0, 0] + 0.5 * dot_f32(turned_grad, turned_grad, 1, 1)
    step_block = dot_f32(dot_f32(left[1, 0, 0], turned_grad, 1, 1), right[1, 0, 0], 1, 0)
    return (weight_block - matrix_rate * step_block, left_new[None, None], right_new[None, None])


def vector_update(state, grad):
    stat_new = 0.5 * state[1] + 0.5 * grad * grad
    param_new = state[0] - vector_rate * grad * lax.rsqrt(stat_new)
    return (param_new, stat_new)


def local(
    tokens,
    cotangent,
    seq_lengths,
    w_qkv,
    qkv_bias_state,
    w_out,
    out_bias_state,
    w_up,
    up_bias_state,
    w_down,
    ln_state,
    qkv_left,
    qkv_right,
    out_left,
    out_right,
    up_left,
    up_right,
    down_left,
    down_right,
):
    row_count, share_width = tokens.shape
    mp_size = lax.axis_size("mp")
    dp_size = lax.axis_size("dp")
    model_width = share_width * mp_size
    own_width = w_qkv.shape[2]
    mp_place = lax.axis_index("mp")
    core = lax.axis_index("dp") % 2

    flat_master = jnp.concatenate([w_qkv[:, kind] for kind in range(3)], axis=1)
    block_qkvo = jnp.concatenate([flat_master, w_out.T], axis=1).astype(jnp.bfloat16)
    full_qkvo = lax.all_gather(block_qkvo, "dp", axis=0, tiled=True)
    full_up = lax.all_gather(w_up.astype(jnp.bfloat16), "dp", axis=0, tiled=True)
    turned_down = lax.all_gather(w_down.T.astype(jnp.bfloat16), "dp", axis=0, tiled=True)
    full_qkv = full_qkvo[:, : 3 * own_width]
    turned_out = full_qkvo[:, 3 * own_width :]

    piece = ln_state.shape[2]
    small = jnp.concatenate(
        [
            ln_state[0].reshape(-1),
            qkv_bias_state[0].reshape(-1),
            out_bias_state[0].reshape(-1),
            up_bias_state[0].reshape(-1),
        ]
    )
    small = small.astype(jnp.bfloat16).astype(jnp.float32)
    filled = small.shape[0]
    small = jnp.pad(small, (0, -filled % 1024)).reshape(1, 8, -1)
    spread = exchange(small, ("mp", "dp"), 1, True).reshape(mp_size * dp_size, -1)[:, :filled]
    x_full = mp_gather(tie(tokens, spread))
    upstream = mp_gather(tie(cotangent, spread))
    norm_all = spread[:, : 2 * piece].reshape(-1, 2, piece).transpose(1, 0, 2).reshape(2, -1)
    here = take(spread.reshape(mp_size, dp_size, -1), mp_place)
    bias_qkv = here[:, 2 * piece : 5 * piece].reshape(dp_size, 3, piece)
    bias_qkv = bias_qkv.transpose(1, 0, 2).reshape(-1)
    bias_out = here[:, 5 * piece : 7 * piece].reshape(dp_size, 2, piece)
    bias_out = bias_out.transpose(1, 0, 2).reshape(2, -1)
    bias_up = here[:, 7 * piece :].reshape(-1)

    segment, offsets, is_valid = segment_layout(seq_lengths[0], row_count)
    cosine, sine = rope_tables(offsets)

    inputs = x_full.astype(jnp.float32)
    row_mean = jnp.mean(inputs, axis=1, keepdims=True)
    row_var = jnp.mean(inputs * inputs, axis=1, keepdims=True) - row_mean * row_mean
    inv_std = lax.rsqrt(row_var + norm_eps)
    normed = ((inputs - row_mean) * inv_std * norm_all[0] + norm_all[1]).astype(jnp.bfloat16)
    grad_rows = (upstream.astype(jnp.float32) * is_valid[:, None]).astype(jnp.bfloat16)
    gy_near, gy_far = (parity_columns(grad_rows, core), parity_columns(grad_rows, 1 - core))
    xn_near, xn_far = (parity_columns(normed, core), parity_columns(normed, 1 - core))

    projected = jnp.dot(normed, full_qkv, preferred_element_type=jnp.float32) + bias_qkv
    grad_attended = jnp.dot(grad_rows, turned_out, preferred_element_type=jnp.float32)
    attended, grad_projected = attention(
        projected, grad_attended.astype(jnp.bfloat16), segment, cosine, sine
    )
    sum_qkvo = OwnerSum(
        jnp.concatenate([over_rows(xn_far, grad_projected), over_rows(gy_far, attended)], axis=1)
    )
    sends = sum_qkvo.add_near(
        jnp.concatenate([over_rows(xn_near, grad_projected), over_rows(gy_near, attended)], axis=1)
    )

    normed_up = tie(normed, *sends)
    hidden = jnp.dot(normed_up, full_up, preferred_element_type=jnp.float32) + bias_up
    activated, slope = gelu_pair(hidden)
    activated = activated.astype(jnp.bfloat16)
    slope = slope.astype(jnp.bfloat16)
    sends = sum_qkvo.advance()
    sum_down = OwnerSum(over_rows(gy_far, activated))
    gy_near = tie(gy_near, *sends)
    sends = sum_down.add_near(over_rows(gy_near, activated))
    more = sum_qkvo.advance()
    grad_rows_down = tie(grad_rows, *sends, *more)

    grad_act = jnp.dot(grad_rows_down, turned_down, preferred_element_type=jnp.float32)
    grad_hidden = (grad_act * slope.astype(jnp.float32)).astype(jnp.bfloat16)
    sends = sum_down.advance()
    xn_far, xn_near = lax.optimization_barrier((xn_far, xn_near) + tuple(sends))[:2]
    sum_up = OwnerSum(over_rows(xn_far, grad_hidden))
    sends_up = sum_up.add_near(over_rows(xn_near, grad_hidden))
    attended_late = tie(attended, *sends_up)

    partial_sum = contract(attended_late, turned_out, 1, 1) + contract(activated, turned_down, 1, 1)
    branches = mp_scatter(partial_sum.astype(jnp.bfloat16))
    grad_projected_late = tie(grad_projected, partial_sum)
    grad_normed_part = contract(grad_projected_late, full_qkv, 1, 1) + contract(grad_hidden, full_up, 1, 1)
    gained_part = grad_normed_part * norm_all[0]
    row_terms = jnp.stack(
        [
            jnp.sum(gained_part, axis=1),
            jnp.sum(gained_part * ((inputs - row_mean) * inv_std), axis=1),
        ]
    )
    row_terms = jnp.sum(exchange(row_terms.reshape(1, 16, -1), ("mp",), 2, True), axis=0)
    row_terms = row_terms.reshape(2, -1)
    grad_normed = mp_scatter(grad_normed_part.astype(jnp.bfloat16))

    own_inputs = tokens.astype(jnp.float32)
    output = (own_inputs + branches + bias_out[0] + bias_out[1]).astype(jnp.bfloat16)

    normalized = (own_inputs - row_mean) * inv_std
    norm_here = lax.dynamic_slice_in_dim(norm_all, mp_place * share_width, share_width, 1)
    gained = grad_normed * norm_here[0]
    local_grad = cotangent.astype(jnp.float32) * is_valid[:, None]
    input_grad = local_grad + inv_std * (
        gained
        - row_terms[0][:, None] / model_width
        - normalized * row_terms[1][:, None] / model_width
    )

    def owner_rows(values, count):
        return values.reshape(count, dp_size, -1).transpose(1, 0, 2).reshape(dp_size, -1)

    vector_grads = jnp.concatenate(
        [
            owner_rows(jnp.sum(grad_normed * normalized, axis=0), 1),
            owner_rows(jnp.sum(grad_normed, axis=0), 1),
            owner_rows(jnp.sum(grad_projected.astype(jnp.float32), axis=0), 3),
            owner_rows(jnp.sum(local_grad, axis=0), 1),
            owner_rows(jnp.sum(grad_hidden.astype(jnp.float32), axis=0), 1),
        ],
        axis=1,
    )
    width = vector_grads.shape[1]
    vector_grads = jnp.pad(vector_grads, ((0, 0), (0, -width % 1024))).reshape(dp_size, 8, -1)
    vector_sums = jnp.sum(exchange(vector_grads, ("dp",), 3, False), axis=0).reshape(-1)[:width]
    owned_norm = vector_sums[: 2 * piece].reshape(2, piece)
    owned_bqkv = vector_sums[2 * piece : 5 * piece].reshape(3, piece)
    bias_total = vector_sums[5 * piece : 6 * piece]
    owned_obias = jnp.stack([bias_total, bias_total])
    owned_bup = vector_sums[6 * piece :]

    owned_qkvo = sum_qkvo.rest().total()
    owned_down = sum_down.rest().total()
    owned_up = sum_up.rest().total()
    owned_qkv = owned_qkvo[:, : 3 * own_width]
    owned_out = owned_qkvo[:, 3 * own_width :]
    new_w_down, down_left_new, down_right_new = shampoo_turned(
        w_down, owned_down, down_left, down_right
    )
    new_w_out, out_left_new, out_right_new = shampoo_turned(w_out, owned_out, out_left, out_right)
    new_qkv_block, qkv_left_new, qkv_right_new = shampoo(
        flat_master, owned_qkv, qkv_left, qkv_right
    )
    new_w_qkv = jnp.stack(
        [new_qkv_block[:, kind * own_width : (kind + 1) * own_width] for kind in range(3)], axis=1
    )
    new_w_up, up_left_new, up_right_new = shampoo(w_up, owned_up, up_left, up_right)
    qkv_params, qkv_stats = vector_update(qkv_bias_state, owned_bqkv)
    obias_params, obias_stats = vector_update(out_bias_state, owned_obias)
    norm_new_params, norm_new_stats = vector_update(ln_state, owned_norm)
    new_up_bias, new_up_stat = vector_update(up_bias_state, owned_bup)
    new_vector_params = jnp.concatenate([qkv_params, obias_params, norm_new_params], axis=0)
    new_vector_stats = jnp.concatenate([qkv_stats, obias_stats, norm_new_stats], axis=0)
    return (
        output,
        input_grad,
        new_w_qkv,
        new_w_out,
        new_w_up,
        new_w_down,
        new_vector_params,
        new_vector_stats,
        new_up_bias,
        new_up_stat,
        qkv_left_new,
        qkv_right_new,
        out_left_new,
        out_right_new,
        up_left_new,
        up_right_new,
        down_left_new,
        down_right_new,
    )


def solution(mesh):
    return jax.shard_map(
        local,
        mesh=mesh,
        in_specs=(
            P("dp", "mp"),
            P("dp", "mp"),
            P("dp", None),
            P("dp", None, "mp"),
            P(None, None, ("mp", "dp")),
            P("mp", "dp"),
            P(None, None, ("mp", "dp")),
            P("dp", "mp"),
            P(None, ("mp", "dp")),
            P("mp", "dp"),
            P(None, None, ("mp", "dp")),
            P(None, "mp", "dp", None, None),
            P(None, "mp", "dp", None, None),
            P(None, "mp", "dp", None, None),
            P(None, "mp", "dp", None, None),
            P(None, "mp", "dp", None, None),
            P(None, "mp", "dp", None, None),
            P(None, "mp", "dp", None, None),
            P(None, "mp", "dp", None, None),
        ),
        out_specs=(
            P("dp", "mp"),
            P("dp", "mp"),
            P("dp", None, "mp"),
            P("mp", "dp"),
            P("dp", "mp"),
            P("mp", "dp"),
            P(None, ("mp", "dp")),
            P(None, ("mp", "dp")),
            P(("mp", "dp")),
            P(("mp", "dp")),
            P("mp", "dp", None, None),
            P("mp", "dp", None, None),
            P("mp", "dp", None, None),
            P("mp", "dp", None, None),
            P("mp", "dp", None, None),
            P("mp", "dp", None, None),
            P("mp", "dp", None, None),
            P("mp", "dp", None, None),
        ),
        check_vma=False,
    )
```

time: 999 us -> 685 us (0.69)
  waiting for transfers between devices: 515 us -> 178 us
  matrix products: 300 us -> 201 us
  starting transfers between devices: 0.83 us -> 87.5 us
  blocking collectives: 77.4 us -> 0 us
  Pallas kernels: 0 us -> 76.1 us
  other arithmetic: 42.7 us -> 67.6 us
  local copies, waits for them, and re-layouts: 34.5 us -> 51.7 us
    reduce_scatter x6 -> x0, waiting for transfers between devices: 257 us -> none  [the longest x1 70.7 us: local(): lax.psum_scatter(grad_down_w.astype(jnp.bfloat16), 'dp', scatter_dimensio...]
    all_gather x6 -> x3, waiting for transfers between devices: 208 us -> 0.01 us  [the longest x1 0.01 us: local(): full_qkvo = lax.all_gather(block_qkvo, 'dp', axis=0, tiled=True)]
    ppermute x0 -> x41, waiting for transfers between devices: none -> 178 us  [the longest x9 88.4 us: send(): self.rising = lax.ppermute(self.sends[0], 'dp', up_pairs)]
    dot_general x47 -> x28, matrix products: 300 us -> 201 us  [the longest x12 66.3 us: dot_f32(): lax.dot_general(left.astype(jnp.bfloat16), right.astype(jnp.bfloat16), ((...]
    ppermute x0 -> x41, starting transfers between devices: none -> 87.3 us  [the longest x9 50.2 us: send(): self.rising = lax.ppermute(self.sends[0], 'dp', up_pairs)]
    pallas_call x0 -> x4, Pallas kernels: none -> 76.1 us  [the longest x3 38.7 us: exchange(): pl.pallas_call(functools.partial(exchange_kernel, axes, count, same), out...]
    unnamed x18 -> x3, waiting for transfers between devices: 51.1 us -> 0.05 us
    all_gather x4 -> x0, blocking collectives: 41.8 us -> none  [the longest x1 13.4 us: local(): lax.all_gather(sent[6], 'dp', axis=1, tiled=True)]
  transfers between devices with their start and end apart: 15 -> 44, of which waited for: 12 -> 20; matrix products, arithmetic and copies ran while one was open for 28% -> 37% of each run, Pallas kernels for 0% -> 11%
where the time goes in v1:
time: 685 us; the launch traced here: 678 us
  matrix products  201 us (29%)
  waiting for transfers between devices  178 us (26%)
  starting transfers between devices  87.5 us (13%)
  Pallas kernels  76.1 us (11%)
  other arithmetic  67.6 us (10%)
  local copies, waits for them, and re-layouts  51.7 us (8%)
  between operations  15.6 us (2%)
    ppermute x9, waiting for transfers between devices, send(): self.rising = lax.ppermute(self.sends[0], 'dp', up_pairs)  88.4 us
    dot_general x12, matrix products, dot_f32(): lax.dot_general(left.astype(jnp.bfloat16), right.astype(jnp.bfloat16), ((...  66.3 us
    ppermute x9, starting transfers between devices, send(): self.rising = lax.ppermute(self.sends[0], 'dp', up_pairs)  50.2 us
    dot_general x4, matrix products, contract(): lax.dot_general(left, right, (((left_axis,), (right_axis,)), ((), ())), p...  48.3 us
    pallas_call x3, Pallas kernels, exchange(): pl.pallas_call(functools.partial(exchange_kernel, axes, count, same), out...  38.7 us
    dot_general x8, matrix products, over_rows(): lax.dot_general(left, right, (((0,), (0,)), ((), ())), preferred_element_...  38.3 us
    pallas_call x1, Pallas kernels, attention(): pl.pallas_call(functools.partial(attention_kernel, head_cols), grid=(pair...  37.4 us
    ppermute x2, waiting for transfers between devices, mp_gather(): over_y = lax.ppermute(share, 'mp', mp_pairs(2))  30.7 us
  transfers between devices with their start and end apart: 44, of which 20 were waited for; matrix products, arithmetic and copies ran while one was open for 37% of the time, Pallas kernels for 11%

profile of v1, /device:TPU:0, one launch (start us, length us, event | category | flops | bytes accessed | tf_op | source)
XLA Modules:
  0.0 677.8 jit_solution(8824905148252725624)
XLA Ops:
  18.6 16.0 %exchange.3 = f32[32,8,128]{2,1,0:T(8,128)} custom-call(f32[1,8,128]{2,1,0:T(8,128)} %fusion.124.in_ref), custom_call_target="tpu_custom_call" | custom-call | tf_op jit(solution)/shard_map/exchange/pallas_call | solution.py:240
  51.0 12.3 %collective-permute-done.1 = bf16[1024,512]{1,0:T(8,128)(2,1)} collective-permute-done((bf16[1024,512]{1,0:T(8,128)(2,1)S(1)}, bf16[1024,512]{1,0:T(8,128)(2,1)}, u32[]{:S(2)}, u32[]{:S(2)}) %collective-permute-start.1) | collective-permute-done | bytes 1048608 | tf_op jit(solution)/shard_map/ppermute | solution.py:69
  67.4 18.4 %collective-permute-done.5 = bf16[1024,512]{1,0:T(8,128)(2,1)} collective-permute-done((bf16[1024,512]{1,0:T(8,128)(2,1)}, bf16[1024,512]{1,0:T(8,128)(2,1)}, u32[]{:S(2)}, u32[]{:S(2)}) %collective-permute-start.5) | collective-permute-done | bytes 1048608 | tf_op jit(solution)/shard_map/ppermute | solution.py:69
  97.0 8.8 %collective-permute-done.6 = bf16[512,512]{1,0:T(8,128)(2,1)S(1)} collective-permute-done((bf16[512,512]{1,0:T(8,128)(2,1)S(1)}, bf16[512,512]{1,0:T(8,128)(2,1)S(1)}, u32[]{:S(2)}, u32[]{:S(2)}) %collective-permute-start.6) | collective-permute-done | bytes 524320 | tf_op jit(solution)/shard_map/ppermute | solution.py:70
  122.5 6.7 fusion.27.q_ref.k_ref.v_ref
  129.3 37.4 %attention.1 = (bf16[1024,512]{1,0:T(8,128)(2,1)S(1)}, bf16[1024,1536]{1,0:T(8,128)(2,1)S(1)}) custom-call(f32[1024,1536]{1,0:T(8,128)S(1)} %fusion.27.q_ref.k_ref.v_ref, f32[1024,1536]{1,0:T(8,128)S(1)} %fusion.27.q_ref.k_ref.v_ref, f32[1024,1536]{1,0:T(8,128)S(1)} %fusion.27.q_ref.k_ref.v_ref, bf16[1024,512]{1,0:T(8,128)(2,1)S(1)} %fusion.75.go_ref, ...), custom_call_target="tpu_custom_call" | custom-call | flops 12884901888 | bytes 12582912 | tf_op jit(solution)/shard_map/attention/pallas_call | solution.py:359
  206.1 35.4 %collective-permute-done.9 = bf16[256,2048]{1,0:T(8,128)(2,1)} collective-permute-done((bf16[256,2048]{1,0:T(8,128)(2,1)}, bf16[256,2048]{1,0:T(8,128)(2,1)}, u32[]{:S(2)}, u32[]{:S(2)}) %collective-permute-start.9) | collective-permute-done | bytes 1048608 | tf_op jit(solution)/shard_map/ppermute | solution.py:170
  251.3 16.6 %multiply_convert_fusion.1 = (bf16[1024,2048]{1,0:T(8,128)(2,1)S(1)}, f32[1024,2048]{1,0:T(8,128)}) fusion(f32[2048]{0:T(1024)S(1)} %bitcast.296, bf16[1024,2048]{1,0:T(8,128)(2,1)} %copy-done.13, bf16[2048,2048]{1,0:T(8,128)(2,1)} %all-gather.6.cloned.1.call-done), kind=kOutput, calls=%fused_computation.33 | convolution fusion | flops 8610906112 | bytes 25174016 | tf_op jit(solution)/shard_map/dot_general | solution.py:522
  268.0 6.6 convolution_convert_fusion.2
  274.6 21.2 %collective-permute-done.14 = bf16[256,2048]{1,0:T(8,128)(2,1)} collective-permute-done((bf16[256,2048]{1,0:T(8,128)(2,1)S(1)}, bf16[256,2048]{1,0:T(8,128)(2,1)}, u32[]{:S(2)}, u32[]{:S(2)}) %collective-permute-start.14) | collective-permute-done | bytes 1048608 | tf_op jit(solution)/shard_map/ppermute | solution.py:170
  300.4 13.6 %collective-permute-start.29 = (bf16[256,2048]{1,0:T(8,128)(2,1)}, bf16[256,2048]{1,0:T(8,128)(2,1)}, u32[]{:S(2)}, u32[]{:S(2)}) collective-permute-start(bf16[256,2048]{1,0:T(8,128)(2,1)} %get-tuple-element.77), channel_id=1, source_target_pairs={{0,2},{1,3},{2,4},{3,5},{4,6},{5,7},{8,10},{9,11},{10,12},{11,13},... | collective-permute-start | bytes 3145736 | tf_op jit(solution)/shard_map/ppermute | solution.py:170
  314.0 14.6 %fusion.144 = f32[1024,2048]{1,0:T(8,128)} fusion(bf16[1024,2048]{1,0:T(8,128)(2,1)} %copy-done.83, bf16[2048,2048]{0,1:T(8,128)(2,1)} %all-gather.8.cloned.1.call-done), kind=kOutput, calls=%fused_computation.288 | convolution fusion | flops 8589934592 | bytes 20971520 | tf_op jit(solution)/shard_map/dot_general | solution.py:252
  348.8 9.0 %fusion.5 = f32[1,1,1536,1536]{3,2,1,0:T(8,128)} fusion(f32[2,1,1,1536,1536]{4,3,2,1,0:T(8,128)} %param.31, bf16[256,2048]{1,0:T(8,128)(2,1)S(1)} %fusion.64), kind=kOutput, calls=%fused_computation.14 | convolution fusion | flops 1212678144 | bytes 19660800 | tf_op jit(solution)/shard_map/dot_general | solution.py:409
  357.9 6.5 add_convert_fusion.2
  370.4 19.1 %convert_reduce_fusion.1 = (f32[2048]{0:T(1024)S(1)}, bf16[1024,2048]{1,0:T(8,128)(2,1)}) fusion(f32[1024,2048]{1,0:T(8,128)} %get-tuple-element.135, f32[2048]{0:T(1024)S(1)} %bitcast.297, bf16[1024,2048]{1,0:T(8,128)(2,1)S(1)} %copy-done.16, bf16[2048,2048]{0,1:T(8,128)(2,1)} %all-gather.8.cloned.1.call-done), kind=kOutput, calls=%fused_computation.28 | convolution fusion | flops 8638167040 | bytes 25182208 | tf_op jit(solution)/shard_map/dot_general | solution.py:533
  398.6 6.3 convolution_convert_fusion.1
  406.2 10.4 %collective-permute-done.37 = bf16[256,2048]{1,0:T(8,128)(2,1)S(1)} collective-permute-done((bf16[256,2048]{1,0:T(8,128)(2,1)}, bf16[256,2048]{1,0:T(8,128)(2,1)S(1)}, u32[]{:S(2)}, u32[]{:S(2)}) %collective-permute-start.37) | collective-permute-done | bytes 1048608 | tf_op jit(solution)/shard_map/ppermute | solution.py:170
  420.6 8.2 %collective-permute-start.38 = (bf16[256,2048]{1,0:T(8,128)(2,1)S(1)}, bf16[256,2048]{1,0:T(8,128)(2,1)S(1)}, u32[]{:S(2)}, u32[]{:S(2)}) collective-permute-start(bf16[256,2048]{1,0:T(8,128)(2,1)S(1)} %get-tuple-element.59), channel_id=1, source_target_pairs={{0,2},{1,3},{2,4},{3,5},{4,6},{5,7},{8,10},{9,11},{10,12},{11,13},... | collective-permute-start | bytes 3145736 | tf_op jit(solution)/shard_map/ppermute | solution.py:170
  428.8 13.7 %fusion.145 = f32[1024,2048]{1,0:T(8,128)} fusion(bf16[1024,2048]{1,0:T(8,128)(2,1)S(1)} %copy-done.82, bf16[2048,2048]{1,0:T(8,128)(2,1)} %all-gather.6.cloned.1.call-done), kind=kOutput, calls=%fused_computation.289 | convolution fusion | flops 8589934592 | bytes 20971520 | tf_op jit(solution)/shard_map/dot_general | solution.py:252
  448.8 9.8 %convolution_subtract_fusion = f32[2048,256]{1,0:T(8,128)} fusion(f32[2048,256]{1,0:T(8,128)S(1)} %copy-done.21, bf16[256,2048]{1,0:T(8,128)(2,1)S(1)} %fusion.56, f32[2,1,1,2048,2048]{4,3,2,1,0:T(8,128)} %param.36, f32[2,1,1,256,256]{4,3,2,1,0:T(8,128)} %param.37), kind=kOutput, calls=%fused_computation.52 | convolution fusion | flops 2416967680 | bytes 13762560 | tf_op jit(solution)/shard_map/dot_general | solution.py:409
  458.6 8.6 %add_convert_fusion = bf16[1024,2048]{1,0:T(8,128)(2,1)S(1)} fusion(bf16[1024,2048]{1,0:T(8,128)(2,1)} %collective-permute-done.16, bf16[1024,1024]{1,0:T(8,128)(2,1)} %get-tuple-element.35, bf16[1024,2048]{1,0:T(8,128)(2,1)} %get-tuple-element.138), kind=kOutput, calls=%fused_computation.29 | convolution fusion | flops 4301258752 | bytes 14680064 | tf_op jit(solution)/shard_map/dot_general | solution.py:122
  469.2 6.5 convolution_add_fusion.1
  483.6 13.5 %multiply_reduce_fusion = (f32[1024]{0:T(1024)S(1)}, f32[1024]{0:T(1024)S(1)}, bf16[1024,2048]{1,0:T(8,128)(2,1)}) fusion(f32[2048]{0:T(1024)S(1)} %copy-done.64, f32[1024]{0:T(1024)S(1)} %copy-done.60, f32[1024]{0:T(1024)S(1)} %copy-done.58, bf16[1024,2048]{1,0:T(8,128)(2,1)S(1)} %copy-done.10, f32[1024,2048]{1,0:T(8,128)} %fusion.145, ...), kind=kOutput, calls=%fused_computation.37 | convolution fusion | flops 6461323264 | bytes 26238976 | tf_op jit(solution)/shard_map/dot_general | solution.py:252
  501.8 10.9 %fusion.1 = f32[1,1,2048,2048]{3,2,1,0:T(8,128)} fusion(f32[2,1,1,2048,2048]{4,3,2,1,0:T(8,128)} %param.36, bf16[256,2048]{1,0:T(8,128)(2,1)S(1)} %fusion.56), kind=kOutput, calls=%fused_computation.4 | convolution fusion | flops 2155872256 | bytes 35651584 | tf_op jit(solution)/shard_map/dot_general | solution.py:409
  530.0 6.6 collective-permute-done.23
  547.4 6.6 collective-permute-done.21
  554.8 10.5 %collective-permute-done.19 = bf16[512,512]{1,0:T(8,128)(2,1)S(1)} collective-permute-done((bf16[512,512]{1,0:T(8,128)(2,1)S(1)}, bf16[512,512]{1,0:T(8,128)(2,1)S(1)}, u32[]{:S(2)}, u32[]{:S(2)}) %collective-permute-start.19) | collective-permute-done | bytes 524320 | tf_op jit(solution)/shard_map/ppermute | solution.py:104
  577.7 10.3 %exchange.4 = f32[4,16,128]{2,1,0:T(8,128)} custom-call(f32[1,16,128]{2,1,0:T(8,128)} %reshape.274.in_ref), custom_call_target="tpu_custom_call" | custom-call | tf_op jit(solution)/shard_map/exchange/pallas_call | solution.py:240
  601.2 12.4 %exchange.5 = f32[8,8,128]{2,1,0:T(8,128)} custom-call(f32[8,8,128]{2,1,0:T(8,128)} %bitcast.290), custom_call_target="tpu_custom_call" | custom-call | tf_op jit(solution)/shard_map/exchange/pallas_call | solution.py:240
  622.5 17.8 %collective-permute-done.33 = bf16[256,2048]{1,0:T(8,128)(2,1)S(1)} collective-permute-done((bf16[256,2048]{1,0:T(8,128)(2,1)}, bf16[256,2048]{1,0:T(8,128)(2,1)S(1)}, u32[]{:S(2)}, u32[]{:S(2)}) %collective-permute-start.33) | collective-permute-done | bytes 1048608 | tf_op jit(solution)/shard_map/ppermute | solution.py:170
  649.7 10.4 %fusion.36 = f32[256,2048]{1,0:T(8,128)} fusion(f32[256,2048]{1,0:T(8,128)S(1)} %copy-done.22, f32[2,1,1,2048,2048]{4,3,2,1,0:T(8,128)} %param.35, bf16[256,2048]{1,0:T(8,128)(2,1)S(1)} %fusion.62, f32[2,1,1,256,256]{4,3,2,1,0:T(8,128)} %param.34), kind=kOutput, calls=%fused_computation.56 | convolution fusion | flops 2416967680 | bytes 13762560 | tf_op jit(solution)/shard_map/dot_general | solution.py:409
  660.2 10.8 %fusion.3 = f32[1,1,2048,2048]{3,2,1,0:T(8,128)} fusion(f32[2,1,1,2048,2048]{4,3,2,1,0:T(8,128)} %param.35, bf16[256,2048]{1,0:T(8,128)(2,1)S(1)} %fusion.62), kind=kOutput, calls=%fused_computation.7 | convolution fusion | flops 2155872256 | bytes 35651584 | tf_op jit(solution)/shard_map/dot_general | solution.py:409
  (401 shorter events, 246.2 us)
Async XLA Ops:
  7.2 108.6 %all-gather.4.cloned.1.call-start = ((), (), s32[]{:S(2)}) async-start(), calls=%async_computation | async-start | bytes 9437184 | tf_op jit(solution)/shard_map/all_gather | solution.py:468
  11.1 240.2 %all-gather.6.cloned.1.call-start = ((), (), s32[]{:S(2)}) async-start(), calls=%async_computation.1 | async-start | bytes 9437184 | tf_op jit(solution)/shard_map/all_gather | solution.py:469
  14.0 300.0 %all-gather.8.cloned.1.call-start = ((), (), s32[]{:S(2)}) async-start(), calls=%async_computation.2 | async-start | bytes 9437184 | tf_op jit(solution)/shard_map/all_gather | solution.py:470
  35.6 29.4 %collective-permute-start = (bf16[1024,512]{1,0:T(8,128)(2,1)S(1)}, bf16[1024,512]{1,0:T(8,128)(2,1)}, u32[]{:S(2)}, u32[]{:S(2)}) collective-permute-start(bf16[1024,512]{1,0:T(8,128)(2,1)S(1)} %copy-done.24), channel_id=1, source_target_pairs={{0,8},{8,0},{16,24},{24,16},{1,9},{9,1},{17,25},{25,17},{2,10},{10... | collective-permute-start | bytes 3145736 | tf_op jit(solution)/shard_map/ppermute | solution.py:68
  37.1 26.2 %collective-permute-start.1 = (bf16[1024,512]{1,0:T(8,128)(2,1)S(1)}, bf16[1024,512]{1,0:T(8,128)(2,1)}, u32[]{:S(2)}, u32[]{:S(2)}) collective-permute-start(bf16[1024,512]{1,0:T(8,128)(2,1)S(1)} %copy-done.24), channel_id=1, source_target_pairs={{0,16},{8,24},{16,0},{24,8},{1,17},{9,25},{17,1},{25,9},{2,18},{10... | collective-permute-start | bytes 3145736 | tf_op jit(solution)/shard_map/ppermute | solution.py:69
  37.9 49.6 %collective-permute-start.4 = (bf16[1024,512]{1,0:T(8,128)(2,1)}, bf16[1024,512]{1,0:T(8,128)(2,1)}, u32[]{:S(2)}, u32[]{:S(2)}) collective-permute-start(bf16[1024,512]{1,0:T(8,128)(2,1)} %param.20), channel_id=1, source_target_pairs={{0,8},{8,0},{16,24},{24,16},{1,9},{9,1},{17,25},{25,17},{2,10},{10... | collective-permute-start | bytes 3145736 | tf_op jit(solution)/shard_map/ppermute | solution.py:68
  38.9 46.8 %collective-permute-start.5 = (bf16[1024,512]{1,0:T(8,128)(2,1)}, bf16[1024,512]{1,0:T(8,128)(2,1)}, u32[]{:S(2)}, u32[]{:S(2)}) collective-permute-start(bf16[1024,512]{1,0:T(8,128)(2,1)} %param.20), channel_id=1, source_target_pairs={{0,16},{8,24},{16,0},{24,8},{1,17},{9,25},{17,1},{25,9},{2,18},{10... | collective-permute-start | bytes 3145736 | tf_op jit(solution)/shard_map/ppermute | solution.py:69
  64.4 31.0 %collective-permute-start.2 = (bf16[512,512]{1,0:T(8,128)(2,1)S(1)}, bf16[512,512]{1,0:T(8,128)(2,1)S(1)}, u32[]{:S(2)}, u32[]{:S(2)}) collective-permute-start(bf16[512,512]{1,0:T(8,128)(2,1)S(1)} %slice.263), channel_id=1, source_target_pairs={{0,8},{8,0},{16,24},{24,16},{1,9},{9,1},{17,25},{25,17},{2,10},{10... | collective-permute-start | bytes 1572872 | tf_op jit(solution)/shard_map/ppermute | solution.py:70
  66.1 30.8 %collective-permute-start.3 = (bf16[512,512]{1,0:T(8,128)(2,1)S(1)}, bf16[512,512]{1,0:T(8,128)(2,1)S(1)}, u32[]{:S(2)}, u32[]{:S(2)}) collective-permute-start(bf16[512,512]{1,0:T(8,128)(2,1)S(1)} %slice.264), channel_id=1, source_target_pairs={{0,16},{8,24},{16,0},{24,8},{1,17},{9,25},{17,1},{25,9},{2,18},{10... | collective-permute-start | bytes 1572872 | tf_op jit(solution)/shard_map/ppermute | solution.py:71
  192.7 48.8 %collective-permute-start.9 = (bf16[256,2048]{1,0:T(8,128)(2,1)}, bf16[256,2048]{1,0:T(8,128)(2,1)}, u32[]{:S(2)}, u32[]{:S(2)}) collective-permute-start(bf16[256,2048]{1,0:T(8,128)(2,1)} %get-tuple-element.85), channel_id=1, source_target_pairs={{0,2},{1,3},{8,10},{9,11},{16,18},{17,19},{24,26},{25,27}} | collective-permute-start | bytes 3145736 | tf_op jit(solution)/shard_map/ppermute | solution.py:170
  244.5 30.0 %collective-permute-start.15 = (bf16[256,2048]{1,0:T(8,128)(2,1)S(1)}, bf16[256,2048]{1,0:T(8,128)(2,1)S(1)}, u32[]{:S(2)}, u32[]{:S(2)}) collective-permute-start(bf16[256,2048]{1,0:T(8,128)(2,1)S(1)} %get-tuple-element.82), channel_id=1, source_target_pairs={{4,2},{5,3},{6,4},{7,5},{12,10},{13,11},{14,12},{15,13},{20,18},{2... | collective-permute-start | bytes 3145736 | tf_op jit(solution)/shard_map/ppermute | solution.py:171
  245.3 50.5 %collective-permute-start.14 = (bf16[256,2048]{1,0:T(8,128)(2,1)S(1)}, bf16[256,2048]{1,0:T(8,128)(2,1)}, u32[]{:S(2)}, u32[]{:S(2)}) collective-permute-start(bf16[256,2048]{1,0:T(8,128)(2,1)S(1)} %get-tuple-element.83), channel_id=1, source_target_pairs={{0,2},{1,3},{2,4},{3,5},{8,10},{9,11},{10,12},{11,13},{16,18},{17,... | collective-permute-start | bytes 3145736 | tf_op jit(solution)/shard_map/ppermute | solution.py:170
  274.6 83.3 %collective-permute-start.11 = (bf16[1024,2048]{1,0:T(8,128)(2,1)}, bf16[1024,2048]{1,0:T(8,128)(2,1)}, u32[]{:S(2)}, u32[]{:S(2)}) collective-permute-start(bf16[1024,2048]{1,0:T(8,128)(2,1)} %convolution_convert_fusion.2), channel_id=1, source_target_pairs={{0,1},{1,0},{2,3},{3,2},{4,5},{5,4},{6,7},{7,6},{8,9},{9,8},{10,11... | collective-permute-start | bytes 12582920 | tf_op jit(solution)/shard_map/ppermute | solution.py:138
  299.1 34.2 %collective-permute-start.30 = (bf16[256,2048]{1,0:T(8,128)(2,1)}, bf16[256,2048]{1,0:T(8,128)(2,1)S(1)}, u32[]{:S(2)}, u32[]{:S(2)}) collective-permute-start(bf16[256,2048]{1,0:T(8,128)(2,1)} %get-tuple-element.76), channel_id=1, source_target_pairs={{2,0},{3,1},{4,2},{5,3},{6,4},{7,5},{10,8},{11,9},{12,10},{13,11},... | collective-permute-start | bytes 3145736 | tf_op jit(solution)/shard_map/ppermute | solution.py:171
  300.4 34.2 %collective-permute-start.29 = (bf16[256,2048]{1,0:T(8,128)(2,1)}, bf16[256,2048]{1,0:T(8,128)(2,1)}, u32[]{:S(2)}, u32[]{:S(2)}) collective-permute-start(bf16[256,2048]{1,0:T(8,128)(2,1)} %get-tuple-element.77), channel_id=1, source_target_pairs={{0,2},{1,3},{2,4},{3,5},{4,6},{5,7},{8,10},{9,11},{10,12},{11,13},... | collective-permute-start | bytes 3145736 | tf_op jit(solution)/shard_map/ppermute | solution.py:170
  364.7 24.9 %collective-permute-start.13 = (bf16[256,2048]{1,0:T(8,128)(2,1)S(1)}, bf16[256,2048]{1,0:T(8,128)(2,1)S(1)}, u32[]{:S(2)}, u32[]{:S(2)}) collective-permute-start(bf16[256,2048]{1,0:T(8,128)(2,1)S(1)} %get-tuple-element.80), channel_id=1, source_target_pairs={{6,4},{7,5},{14,12},{15,13},{22,20},{23,21},{30,28},{31,29}} | collective-permute-start | bytes 3145736 | tf_op jit(solution)/shard_map/ppermute | solution.py:171
  365.6 25.2 %collective-permute-start.12 = (bf16[256,2048]{1,0:T(8,128)(2,1)S(1)}, bf16[256,2048]{1,0:T(8,128)(2,1)S(1)}, u32[]{:S(2)}, u32[]{:S(2)}) collective-permute-start(bf16[256,2048]{1,0:T(8,128)(2,1)S(1)} %get-tuple-element.81), channel_id=1, source_target_pairs={{0,2},{1,3},{8,10},{9,11},{16,18},{17,19},{24,26},{25,27}} | collective-permute-start | bytes 3145736 | tf_op jit(solution)/shard_map/ppermute | solution.py:170
  392.5 24.2 %collective-permute-start.37 = (bf16[256,2048]{1,0:T(8,128)(2,1)}, bf16[256,2048]{1,0:T(8,128)(2,1)S(1)}, u32[]{:S(2)}, u32[]{:S(2)}) collective-permute-start(bf16[256,2048]{1,0:T(8,128)(2,1)} %get-tuple-element.79), channel_id=1, source_target_pairs={{0,2},{1,3},{2,4},{3,5},{8,10},{9,11},{10,12},{11,13},{16,18},{17,... | collective-permute-start | bytes 3145736 | tf_op jit(solution)/shard_map/ppermute | solution.py:170
  404.9 53.7 %collective-permute-start.16 = (bf16[1024,2048]{1,0:T(8,128)(2,1)}, bf16[1024,2048]{1,0:T(8,128)(2,1)}, u32[]{:S(2)}, u32[]{:S(2)}) collective-permute-start(bf16[1024,2048]{1,0:T(8,128)(2,1)} %convolution_convert_fusion.1), channel_id=1, source_target_pairs={{0,1},{1,0},{2,3},{3,2},{4,5},{5,4},{6,7},{7,6},{8,9},{9,8},{10,11... | collective-permute-start | bytes 12582920 | tf_op jit(solution)/shard_map/ppermute | solution.py:138
  419.3 26.6 %collective-permute-start.40 = (bf16[256,2048]{1,0:T(8,128)(2,1)S(1)}, bf16[256,2048]{1,0:T(8,128)(2,1)S(1)}, u32[]{:S(2)}, u32[]{:S(2)}) collective-permute-start(bf16[256,2048]{1,0:T(8,128)(2,1)S(1)} %get-tuple-element.60), channel_id=1, source_target_pairs={{2,0},{3,1},{4,2},{5,3},{6,4},{7,5},{10,8},{11,9},{12,10},{13,11},... | collective-permute-start | bytes 3145736 | tf_op jit(solution)/shard_map/ppermute | solution.py:171
  420.6 26.5 %collective-permute-start.38 = (bf16[256,2048]{1,0:T(8,128)(2,1)S(1)}, bf16[256,2048]{1,0:T(8,128)(2,1)S(1)}, u32[]{:S(2)}, u32[]{:S(2)}) collective-permute-start(bf16[256,2048]{1,0:T(8,128)(2,1)S(1)} %get-tuple-element.59), channel_id=1, source_target_pairs={{0,2},{1,3},{2,4},{3,5},{4,6},{5,7},{8,10},{9,11},{10,12},{11,13},... | collective-permute-start | bytes 3145736 | tf_op jit(solution)/shard_map/ppermute | solution.py:170
  479.0 61.0 %collective-permute-start.31 = (bf16[256,2048]{1,0:T(8,128)(2,1)S(1)}, bf16[256,2048]{1,0:T(8,128)(2,1)S(1)}, u32[]{:S(2)}, u32[]{:S(2)}) collective-permute-start(bf16[256,2048]{1,0:T(8,128)(2,1)S(1)} %get-tuple-element.75), channel_id=1, source_target_pairs={{0,2},{1,3},{8,10},{9,11},{16,18},{17,19},{24,26},{25,27}} | collective-permute-start | bytes 3145736 | tf_op jit(solution)/shard_map/ppermute | solution.py:170
  515.7 25.7 %collective-permute-start.27 = (bf16[512,512]{1,0:T(8,128)(2,1)S(1)}, bf16[512,512]{1,0:T(8,128)(2,1)S(1)}, u32[]{:S(2)}, u32[]{:S(2)}) collective-permute-start(bf16[512,512]{1,0:T(8,128)(2,1)S(1)} %get-tuple-element.65), channel_id=1, source_target_pairs={{0,16},{8,24},{16,0},{24,8},{1,17},{9,25},{17,1},{25,9},{2,18},{10... | collective-permute-start | bytes 1572872 | tf_op jit(solution)/shard_map/ppermute | solution.py:99
  518.8 28.7 %collective-permute-start.17 = (bf16[512,512]{1,0:T(8,128)(2,1)S(1)}, bf16[512,512]{1,0:T(8,128)(2,1)S(1)}, u32[]{:S(2)}, u32[]{:S(2)}) collective-permute-start(bf16[512,512]{1,0:T(8,128)(2,1)S(1)} %copy-done.45), channel_id=1, source_target_pairs={{0,8},{8,0},{16,24},{24,16},{1,9},{9,1},{17,25},{25,17},{2,10},{10... | collective-permute-start | bytes 1572872 | tf_op jit(solution)/shard_map/ppermute | solution.py:100
  540.0 25.3 %collective-permute-start.19 = (bf16[512,512]{1,0:T(8,128)(2,1)S(1)}, bf16[512,512]{1,0:T(8,128)(2,1)S(1)}, u32[]{:S(2)}, u32[]{:S(2)}) collective-permute-start(bf16[512,512]{1,0:T(8,128)(2,1)S(1)} %add_convert_fusion.6), channel_id=1, source_target_pairs={{0,16},{8,24},{16,0},{24,8},{1,17},{9,25},{17,1},{25,9},{2,18},{10... | collective-permute-start | bytes 1572872 | tf_op jit(solution)/shard_map/ppermute | solution.py:104
  541.4 50.9 %collective-permute-start.34 = (bf16[256,2048]{1,0:T(8,128)(2,1)S(1)}, bf16[256,2048]{1,0:T(8,128)(2,1)}, u32[]{:S(2)}, u32[]{:S(2)}) collective-permute-start(bf16[256,2048]{1,0:T(8,128)(2,1)S(1)} %get-tuple-element.74), channel_id=1, source_target_pairs={{6,4},{7,5},{14,12},{15,13},{22,20},{23,21},{30,28},{31,29}} | collective-permute-start | bytes 3145736 | tf_op jit(solution)/shard_map/ppermute | solution.py:171
  543.0 32.8 %collective-permute-start.26 = (bf16[512,512]{1,0:T(8,128)(2,1)S(1)}, bf16[512,512]{1,0:T(8,128)(2,1)S(1)}, u32[]{:S(2)}, u32[]{:S(2)}) collective-permute-start(bf16[512,512]{1,0:T(8,128)(2,1)S(1)} %get-tuple-element.66), channel_id=1, source_target_pairs={{0,16},{8,24},{16,0},{24,8},{1,17},{9,25},{17,1},{25,9},{2,18},{10... | collective-permute-start | bytes 1572872 | tf_op jit(solution)/shard_map/ppermute | solution.py:101
  547.4 43.2 %collective-permute-start.20 = (bf16[512,512]{1,0:T(8,128)(2,1)}, bf16[512,512]{1,0:T(8,128)(2,1)}, u32[]{:S(2)}, u32[]{:S(2)}) collective-permute-start(bf16[512,512]{1,0:T(8,128)(2,1)} %get-tuple-element.71), channel_id=1, source_target_pairs={{0,16},{8,24},{16,0},{24,8},{1,17},{9,25},{17,1},{25,9},{2,18},{10... | collective-permute-start | bytes 1572872 | tf_op jit(solution)/shard_map/ppermute | solution.py:101
  554.1 34.7 %collective-permute-start.28 = (bf16[512,512]{1,0:T(8,128)(2,1)}, bf16[512,512]{1,0:T(8,128)(2,1)}, u32[]{:S(2)}, u32[]{:S(2)}) collective-permute-start(bf16[512,512]{1,0:T(8,128)(2,1)} %get-tuple-element.63), channel_id=1, source_target_pairs={{0,8},{8,0},{16,24},{24,16},{1,9},{9,1},{17,25},{25,17},{2,10},{10... | collective-permute-start | bytes 1572872 | tf_op jit(solution)/shard_map/ppermute | solution.py:105
  565.3 27.0 %collective-permute-start.32 = (bf16[256,2048]{1,0:T(8,128)(2,1)}, bf16[256,2048]{1,0:T(8,128)(2,1)}, u32[]{:S(2)}, u32[]{:S(2)}) collective-permute-start(bf16[256,2048]{1,0:T(8,128)(2,1)} %fusion.59), channel_id=1, source_target_pairs={{0,2},{1,3},{2,4},{3,5},{8,10},{9,11},{10,12},{11,13},{16,18},{17,... | collective-permute-start | bytes 3145736 | tf_op jit(solution)/shard_map/ppermute | solution.py:170
  614.7 25.5 %collective-permute-start.33 = (bf16[256,2048]{1,0:T(8,128)(2,1)}, bf16[256,2048]{1,0:T(8,128)(2,1)S(1)}, u32[]{:S(2)}, u32[]{:S(2)}) collective-permute-start(bf16[256,2048]{1,0:T(8,128)(2,1)} %get-tuple-element.61), channel_id=1, source_target_pairs={{0,2},{1,3},{2,4},{3,5},{4,6},{5,7},{8,10},{9,11},{10,12},{11,13},... | collective-permute-start | bytes 3145736 | tf_op jit(solution)/shard_map/ppermute | solution.py:170
  618.9 26.9 %collective-permute-start.36 = (bf16[256,2048]{1,0:T(8,128)(2,1)S(1)}, bf16[256,2048]{1,0:T(8,128)(2,1)S(1)}, u32[]{:S(2)}, u32[]{:S(2)}) collective-permute-start(bf16[256,2048]{1,0:T(8,128)(2,1)S(1)} %fusion.58), channel_id=1, source_target_pairs={{2,0},{3,1},{4,2},{5,3},{6,4},{7,5},{10,8},{11,9},{12,10},{13,11},... | collective-permute-start | bytes 3145736 | tf_op jit(solution)/shard_map/ppermute | solution.py:171
  (97 other events, 1317.1 us)
Sparse Core Ops, SparseCore 0:
  11.2 87.5 all-gather.3
  100.9 83.1 all-gather.5
  186.2 124.7 all-gather.7

commit v2 on v1

v2 whole, which is shorter than its diff:
```python
import functools
import math

import jax
import jax.numpy as jnp
from jax import lax
from jax.experimental import pallas as pl
from jax.experimental.pallas import tpu as pltpu
from jax.sharding import PartitionSpec as P

HEAD_DIM = 64
ROT_DIM = 32
LANES = 128
ROW_TILE = 256


norm_eps = 1e-05
matrix_rate = 1.0
vector_rate = 0.4
masked_score = -1e30


def segment_layout(lengths, row_count):
    positions = jnp.arange(row_count, dtype=jnp.int32)
    seq_ends = jnp.cumsum(lengths)
    finished = seq_ends[None, :] <= positions[:, None]
    segment = jnp.sum(finished.astype(jnp.int32), axis=1)
    starting = jnp.max(jnp.where(finished, seq_ends[None, :], 0), axis=1)
    is_valid = positions < seq_ends[-1]
    segment = jnp.where(is_valid, segment, lengths.shape[0] + positions)
    offsets = (positions - starting).astype(jnp.float32)
    return (segment, offsets, is_valid.astype(jnp.float32))


def rope_tables(offsets):
    half_rot = ROT_DIM // 2
    freq_index = jnp.arange(half_rot, dtype=jnp.float32)
    inverse = jnp.exp(-(2.0 * freq_index / ROT_DIM) * math.log(10000.0))
    angles = offsets[:, None] * inverse[None, :]
    return (jnp.cos(angles), jnp.sin(angles))


def gelu_pair(values):
    square = values * values
    inner = math.sqrt(2.0 / math.pi) * values * (1.0 + 0.044715 * square)
    bent = jnp.tanh(inner)
    half = 0.5 * (1.0 + bent)
    slope = half + 0.5 * values * (1.0 - bent * bent) * math.sqrt(2.0 / math.pi) * (
        1.0 + 3.0 * 0.044715 * square
    )
    return (values * half, slope)


def take(array, index, axis=0):
    return lax.dynamic_index_in_dim(array, index, axis, keepdims=False)


def summed(*terms):
    total = terms[0].astype(jnp.float32)
    for term in terms[1:]:
        total = total + term.astype(jnp.float32)
    return total


def exchange_kernel(axes, count, same, in_ref, out_ref, send_sems, recv_sems):
    sizes = [lax.axis_size(axis) for axis in axes]
    place = lax.axis_index(axes[0])
    for axis, size in zip(axes[1:], sizes[1:]):
        place = place * size + lax.axis_index(axis)

    def device(peer):
        if len(axes) == 1:
            return {axes[0]: peer}
        return {axes[0]: peer // sizes[1], axes[1]: lax.rem(peer, sizes[1])}

    barrier = pltpu.get_barrier_semaphore()

    def greet(step, carry):
        peer = lax.rem(place + step, count)
        pl.semaphore_signal(
            barrier, inc=1, device_id=device(peer), device_id_type=pl.DeviceIdType.MESH
        )
        return carry

    lax.fori_loop(1, count, greet, 0)
    pl.semaphore_wait(barrier, count - 1)

    def copy_to(step):
        peer = lax.rem(place + step, count)
        source = in_ref.at[0] if same else in_ref.at[peer]
        return pltpu.make_async_remote_copy(
            src_ref=source,
            dst_ref=out_ref.at[place],
            send_sem=send_sems.at[step],
            recv_sem=recv_sems.at[step],
            device_id=device(peer),
            device_id_type=pl.DeviceIdType.MESH,
        )

    def begin(step, carry):
        copy_to(step).start()
        return carry

    def finish(step, carry):
        copy_to(step).wait()
        return carry

    lax.fori_loop(1, count, begin, 0)
    out_ref[place] = in_ref[0] if same else in_ref[place]
    lax.fori_loop(1, count, finish, 0)


def exchange(values, axes, collective_id, same):
    count = 1
    for axis in axes:
        count *= lax.axis_size(axis)
    return pl.pallas_call(
        functools.partial(exchange_kernel, axes, count, same),
        out_shape=jax.ShapeDtypeStruct((count,) + values.shape[1:], values.dtype),
        in_specs=[pl.BlockSpec(memory_space=pltpu.VMEM)],
        out_specs=pl.BlockSpec(memory_space=pltpu.VMEM),
        scratch_shapes=[pltpu.SemaphoreType.DMA((count,)), pltpu.SemaphoreType.DMA((count,))],
        compiler_params=pltpu.CompilerParams(collective_id=collective_id, has_side_effects=True),
        name="exchange",
    )(values)


def contract(left, right, left_axis, right_axis):
    return lax.dot_general(
        left, right, (((left_axis,), (right_axis,)), ((), ())), preferred_element_type=jnp.float32
    )


MESH_ID = pl.DeviceIdType.MESH


def remote(source, target, send_sem, recv_sem, axis, peer):
    return pltpu.make_async_remote_copy(
        src_ref=source,
        dst_ref=target,
        send_sem=send_sem,
        recv_sem=recv_sem,
        device_id={axis: peer},
        device_id_type=MESH_ID,
    )


def greet_line():
    size = lax.axis_size("dp")
    place = lax.axis_index("dp")
    barrier = pltpu.get_barrier_semaphore()
    core = lax.rem(place, 2)
    peers = [place + 1 - 2 * core, lax.rem(place + 2, size), lax.rem(place + size - 2, size)]
    for peer in peers:
        pl.semaphore_signal(barrier, inc=1, device_id={"dp": peer}, device_id_type=MESH_ID)
    return (barrier, len(peers))


class LineGather:
    def __init__(self, own, full, send, recv):
        self.count = lax.axis_size("dp") // 2
        self.place = lax.axis_index("dp")
        self.spot = self.place // 2
        self.core = lax.rem(self.place, 2)
        self.own, self.full, self.send, self.recv = own, full, send, recv
        self.rows = own.shape[0]

    def block(self, chip, core):
        start = pl.multiple_of((2 * chip + core) * self.rows, self.rows)
        return self.full.at[pl.ds(start, self.rows), :]

    def copy(self, kind, step, chip, peer, from_own=False):
        block = self.block(chip, self.core)
        source = self.own if from_own else block
        return remote(
            source, block, self.send.at[kind, step], self.recv.at[kind, step], "dp", peer
        )

    def rise(self, step):
        return self.copy(0, step, self.spot - step + 1, self.place + 2, step == 1)

    def fall(self, step):
        return self.copy(1, step, self.spot + step - 1, self.place - 2, step == 1)

    def show(self, kind, step):
        chip = self.spot - step if kind == 2 else self.spot + step
        return self.copy(kind, step, chip, self.place + 1 - 2 * self.core, step == 0)

    def keep(self):
        return pltpu.make_async_copy(
            self.own, self.block(self.spot, self.core), self.send.at[3, 0]
        )

    def start(self):
        pl.when(self.spot + 1 < self.count)(lambda: self.rise(1).start())
        pl.when(self.spot > 0)(lambda: self.fall(1).start())
        self.show(2, 0).start()
        self.keep().start()

    def advance(self, step):
        @pl.when(self.spot >= step)
        def _():
            self.rise(step).wait_recv()
            pl.when(self.spot + 1 < self.count)(lambda: self.rise(step + 1).start())
            self.show(2, step).start()

        @pl.when(self.spot + step < self.count)
        def _():
            self.fall(step).wait_recv()
            pl.when(self.spot > 0)(lambda: self.fall(step + 1).start())
            self.show(3, step).start()

    def finish(self):
        self.keep().wait()
        self.show(2, 0).wait()
        for step in range(1, self.count):
            rises = (self.spot + 1 < self.count) & (self.spot >= step - 1)
            falls = (self.spot > 0) & (self.spot + step - 1 < self.count)
            pl.when(rises)(lambda step=step: self.rise(step).wait_send())
            pl.when(falls)(lambda step=step: self.fall(step).wait_send())
            pl.when(self.spot >= step)(lambda step=step: self.show(2, step).wait())
            pl.when(self.spot + step < self.count)(lambda step=step: self.show(3, step).wait())


def gather_sems():
    count = lax.axis_size("dp") // 2
    return [pltpu.SemaphoreType.DMA((4, count + 1)), pltpu.SemaphoreType.DMA((4, count + 1))]


def by_rows(rows, step, body):
    def once(index, carry):
        body(pl.ds(pl.multiple_of(index * step, step), step))
        return carry

    lax.fori_loop(0, rows // step, once, 0)


class LineSum:
    def __init__(self, blocks, from_below, from_above, send, recv):
        self.count = lax.axis_size("dp") // 2
        self.place = lax.axis_index("dp")
        self.spot = self.place // 2
        self.blocks, self.below, self.above = blocks, from_below, from_above
        self.send, self.recv = send, recv

    def rise(self, step, source):
        target = self.below.at[step - 1]
        sems = (self.send.at[0, step], self.recv.at[0, step])
        return remote(source, target, *sems, "dp", self.place + 2)

    def fall(self, step, source):
        target = self.above.at[step - 1]
        sems = (self.send.at[1, step], self.recv.at[1, step])
        return remote(source, target, *sems, "dp", self.place - 2)

    def add(self, slot, block):
        def body(rows):
            total = slot[rows, :].astype(jnp.float32) + self.blocks[block, rows, :].astype(jnp.float32)
            slot[rows, :] = total.astype(jnp.bfloat16)

        by_rows(slot.shape[0], 32, body)

    def advance(self, step):
        last = self.count - 1
        up_block = self.count + self.spot - step
        down_block = self.spot - self.count + step
        mirrored = last - self.spot

        @pl.when(self.spot == 0)
        def _():
            self.rise(step, self.blocks.at[self.count - step]).start()

        @pl.when(mirrored == 0)
        def _():
            self.fall(step, self.blocks.at[step - 1]).start()

        if step > 1:

            @pl.when((self.spot > 0) & (self.spot < last) & (self.spot < step))
            def _():
                slot = self.below.at[step - 2]
                self.rise(step - 1, slot).wait_recv()
                self.add(slot, up_block)
                self.rise(step, slot).start()

            @pl.when((mirrored > 0) & (mirrored < last) & (mirrored < step))
            def _():
                slot = self.above.at[step - 2]
                self.fall(step - 1, slot).wait_recv()
                self.add(slot, down_block)
                self.fall(step, slot).start()

    def finish(self, out):
        last = self.count - 1

        def body(rows):
            out[rows, :] = self.blocks[self.spot, rows, :].astype(jnp.float32)

        by_rows(out.shape[0], 32, body)

        def gain(slot):
            def body(rows):
                out[rows, :] = out[rows, :] + slot[rows, :].astype(jnp.float32)

            by_rows(out.shape[0], 32, body)

        @pl.when(self.spot > 0)
        def _():
            slot = self.below.at[last - 1]
            self.rise(last, slot).wait_recv()
            gain(slot)

        @pl.when(self.spot < last)
        def _():
            slot = self.above.at[last - 1]
            self.fall(last, slot).wait_recv()
            gain(slot)

        for step in range(1, self.count):
            block = self.blocks.at[0]
            mirrored = last - self.spot
            rises = (self.spot < step) & (self.spot < last)
            falls = (mirrored < step) & (mirrored < last)
            pl.when(rises)(lambda step=step, block=block: self.rise(step, block).wait_send())
            pl.when(falls)(lambda step=step, block=block: self.fall(step, block).wait_send())


def sum_scratch(rows, columns):
    count = lax.axis_size("dp") // 2
    return [
        pltpu.VMEM((count - 1, rows, columns), jnp.bfloat16),
        pltpu.VMEM((count - 1, rows, columns), jnp.bfloat16),
        pltpu.SemaphoreType.DMA((2, count)),
        pltpu.SemaphoreType.DMA((2, count)),
    ]


class PairProducts:
    def __init__(self, lefts, rights, parcel, sums, send, recv):
        self.count = lax.axis_size("dp") // 2
        self.place = lax.axis_index("dp")
        self.core = lax.rem(self.place, 2)
        self.lefts, self.rights = lefts, rights
        self.parcel, self.sums, self.send, self.recv = parcel, sums, send, recv

    def copy(self, chip):
        return remote(
            self.parcel.at[chip],
            self.sums.at[chip],
            self.send.at[chip],
            self.recv.at[chip],
            "dp",
            self.place + 1 - 2 * self.core,
        )

    def product(self, chip, core, quarter):
        rows = self.sums.shape[1]
        width = self.sums.shape[2] // 4
        start = pl.multiple_of((2 * chip + core) * rows, rows)
        left = self.lefts[quarter][:, pl.ds(start, rows)]
        ref, first = self.rights[quarter]
        return contract(left, ref[:, pl.ds(first, width)], 0, 0)

    def far(self):
        width = self.sums.shape[2] // 4

        def once(chip, carry):
            for quarter in range(4):
                piece = self.product(chip, 1 - self.core, quarter)
                self.parcel[chip, :, pl.ds(quarter * width, width)] = piece.astype(jnp.bfloat16)
            self.copy(chip).start()
            return carry

        lax.fori_loop(0, self.count, once, 0)

    def near(self):
        width = self.sums.shape[2] // 4

        def once(chip, carry):
            self.copy(chip).wait()
            for quarter in range(4):
                columns = pl.ds(quarter * width, width)
                piece = self.product(chip, self.core, quarter)
                total = piece + self.sums[chip, :, columns].astype(jnp.float32)
                self.sums[chip, :, columns] = total.astype(jnp.bfloat16)
            return carry

        lax.fori_loop(0, self.count, once, 0)


def pair_scratch(rows, columns):
    count = lax.axis_size("dp") // 2
    return [
        pltpu.VMEM((count, rows, columns), jnp.bfloat16),
        pltpu.SemaphoreType.DMA((count,)),
        pltpu.SemaphoreType.DMA((count,)),
    ]


class BlockGather:
    def __init__(self, own, full, send, recv):
        self.size = lax.axis_size("mp")
        self.place = lax.axis_index("mp")
        self.own, self.full, self.send, self.recv = own, full, send, recv
        self.rows, self.width = own.shape

    def spread(self, index, rows, owner, peer, first):
        start = pl.multiple_of(owner * self.width, self.width)
        target = self.full.at[rows, pl.ds(start, self.width)]
        source = self.own if first else target
        return remote(source, target, self.send.at[index], self.recv.at[index], "mp", peer)

    def copies(self):
        every = pl.ds(0, self.rows)
        if self.size != 4:
            peers = [lax.rem(self.place + step, self.size) for step in range(1, self.size)]
            return [
                self.spread(index, every, self.place, peer, True)
                for index, peer in enumerate(peers)
            ]
        beside = self.place + 1 - 2 * lax.rem(self.place, 2)
        above = lax.rem(self.place + 2, 4)
        half = self.rows // 2
        return [
            self.spread(0, every, self.place, beside, True),
            self.spread(1, every, self.place, above, True),
            self.spread(2, pl.ds(0, half), above, beside, False),
            self.spread(3, pl.ds(half, half), beside, above, False),
        ]

    def keep(self):
        start = pl.multiple_of(self.place * self.width, self.width)
        target = self.full.at[:, pl.ds(start, self.width)]
        return pltpu.make_async_copy(self.own, target, self.send.at[self.size])

    def start(self):
        copies = self.copies()
        for copy in copies[:2] if self.size == 4 else copies:
            copy.start()
        self.keep().start()

    def forward(self):
        copies = self.copies()
        if self.size == 4:
            copies[1].wait_recv()
            copies[2].start()
            copies[0].wait_recv()
            copies[3].start()

    def finish(self):
        copies = self.copies()
        self.keep().wait()
        for index, copy in enumerate(copies):
            copy.wait_send()
            if index > 1 or self.size != 4:
                copy.wait_recv()


def block_sems():
    size = lax.axis_size("mp") + 1
    return [pltpu.SemaphoreType.DMA((size,)), pltpu.SemaphoreType.DMA((size,))]


def first_kernel(
    block_ref,
    x_ref,
    gy_ref,
    small_ref,
    full_ref,
    x_full,
    gy_full,
    spread_ref,
    gather_send,
    gather_recv,
    x_send,
    x_recv,
    gy_send,
    gy_recv,
    small_send,
    small_recv,
):
    columns = lax.axis_size("dp")
    total = columns * lax.axis_size("mp")
    place = lax.axis_index("mp") * columns + lax.axis_index("dp")
    barrier = pltpu.get_barrier_semaphore()

    def device(step):
        peer = lax.rem(place + step, total)
        return {"mp": peer // columns, "dp": lax.rem(peer, columns)}

    def greet(step, carry):
        pl.semaphore_signal(barrier, inc=1, device_id=device(step), device_id_type=MESH_ID)
        return carry

    lax.fori_loop(1, total, greet, 0)
    pl.semaphore_wait(barrier, total - 1)

    def small_copy(step):
        return pltpu.make_async_remote_copy(
            src_ref=small_ref.at[0],
            dst_ref=spread_ref.at[place],
            send_sem=small_send.at[step],
            recv_sem=small_recv.at[step],
            device_id=device(step),
            device_id_type=MESH_ID,
        )

    def begin(step, carry):
        small_copy(step).start()
        return carry

    def end(step, carry):
        small_copy(step).wait()
        return carry

    weight = LineGather(block_ref, full_ref, gather_send, gather_recv)
    rows_x = BlockGather(x_ref, x_full, x_send, x_recv)
    rows_gy = BlockGather(gy_ref, gy_full, gy_send, gy_recv)
    lax.fori_loop(1, total, begin, 0)
    weight.start()
    rows_x.start()
    spread_ref[place] = small_ref[0]
    lax.fori_loop(1, total, end, 0)
    weight.advance(1)
    rows_x.forward()
    rows_gy.start()
    for step in range(2, weight.count):
        weight.advance(step)
        if step == 2:
            rows_gy.forward()
    weight.finish()
    rows_x.finish()
    rows_gy.finish()


def first_gathers(block, tokens, cotangent, small):
    hbm = pl.BlockSpec(memory_space=pl.ANY)
    vmem = pl.BlockSpec(memory_space=pltpu.VMEM)
    mp_size, dp_size = (lax.axis_size("mp"), lax.axis_size("dp"))
    wide = (tokens.shape[0], tokens.shape[1] * mp_size)
    total = mp_size * dp_size
    return pl.pallas_call(
        first_kernel,
        in_specs=[hbm, hbm, hbm, vmem],
        out_specs=[hbm, hbm, hbm, vmem],
        out_shape=[
            jax.ShapeDtypeStruct((block.shape[0] * dp_size, block.shape[1]), block.dtype),
            jax.ShapeDtypeStruct(wide, tokens.dtype),
            jax.ShapeDtypeStruct(wide, cotangent.dtype),
            jax.ShapeDtypeStruct((total,) + small.shape[1:], small.dtype),
        ],
        scratch_shapes=gather_sems()
        + block_sems()
        + block_sems()
        + [pltpu.SemaphoreType.DMA((total,)), pltpu.SemaphoreType.DMA((total,))],
        compiler_params=pltpu.CompilerParams(collective_id=1, has_side_effects=True),
        name="first_gathers",
    )(block, tokens, cotangent, small)


def greet_and_wait():
    barrier, count = greet_line()
    pl.semaphore_wait(barrier, count)


def second_kernel(
    block_ref,
    xn_ref,
    gy_ref,
    up_ref,
    bias_ref,
    full_ref,
    act_ref,
    slope_ref,
    sums_ref,
    gather_send,
    gather_recv,
    parcel,
    pair_send,
    pair_recv,
):
    weight = LineGather(block_ref, full_ref, gather_send, gather_recv)
    products = PairProducts(
        [gy_ref] * 4, quarters(act_ref), parcel, sums_ref, pair_send, pair_recv
    )
    greet_and_wait()
    weight.start()
    width = up_ref.shape[1] // 4

    def tile(rows):
        for quarter in range(4):
            columns = pl.ds(quarter * width, width)
            hidden = contract(xn_ref[rows, :], up_ref[:, columns], 1, 0) + bias_ref[:, columns]
            activated, slope = gelu_pair(hidden)
            act_ref[rows, columns] = activated.astype(jnp.bfloat16)
            slope_ref[rows, columns] = slope.astype(jnp.bfloat16)

    by_rows(xn_ref.shape[0], ROW_TILE, tile)
    products.far()
    weight.advance(1)
    products.near()
    for step in range(2, weight.count):
        weight.advance(step)
    weight.finish()


def quarters(ref):
    width = ref.shape[1] // 4
    return [(ref, quarter * width) for quarter in range(4)]


VMEM_LIMIT = 60 * 1024 * 1024


def carrying(kernel, collective_id, operands, in_places, outs, out_places, scratch, flops, name):
    spaces = {"h": pl.BlockSpec(memory_space=pl.ANY), "v": pl.BlockSpec(memory_space=pltpu.VMEM)}
    return pl.pallas_call(
        kernel,
        in_specs=[spaces[place] for place in in_places],
        out_specs=[spaces[place] for place in out_places],
        out_shape=[jax.ShapeDtypeStruct(shape, dtype) for shape, dtype in outs],
        scratch_shapes=scratch,
        compiler_params=pltpu.CompilerParams(
            collective_id=collective_id, has_side_effects=True, vmem_limit_bytes=VMEM_LIMIT
        ),
        cost_estimate=pl.CostEstimate(flops=flops, bytes_accessed=1 << 25, transcendentals=0),
        name=name,
    )(*operands)


def second_step(block, normed, grad_rows, full_up, bias_up):
    rows, width = normed.shape
    count = lax.axis_size("dp") // 2
    columns = full_up.shape[1]
    low = jnp.bfloat16
    return carrying(
        second_kernel,
        4,
        (block, normed, grad_rows, full_up, bias_up[None, :]),
        "hvvvv",
        [
            ((width, block.shape[1]), low),
            ((rows, columns), low),
            ((rows, columns), low),
            ((count, width // (2 * count), columns), low),
        ],
        "hvvv",
        gather_sems() + pair_scratch(width // (2 * count), columns),
        4 * rows * width * columns,
        "gather_beside_hidden",
    )


def third_kernel(
    head_cols,
    block_ref,
    ready_ref,
    xn_ref,
    gy_ref,
    weight_ref,
    bias_ref,
    seg_col_ref,
    seg_row_ref,
    keep_ref,
    ahead_ref,
    behind_ref,
    full_ref,
    grad_ref,
    or_ref,
    sums_ref,
    owned_ref,
    gather_send,
    gather_recv,
    below,
    above,
    line_send,
    line_recv,
    parcel,
    pair_send,
    pair_recv,
    mask_ref,
    low_ref,
    go_ref,
    dq_acc,
    dk_acc,
    dv_acc,
):
    weight = LineGather(block_ref, full_ref, gather_send, gather_recv)
    line = LineSum(ready_ref, below, above, line_send, line_recv)
    rights = [(grad_ref, kind * head_cols) for kind in range(3)] + [(or_ref, 0)]
    products = PairProducts(
        [xn_ref] * 3 + [gy_ref], rights, parcel, sums_ref, pair_send, pair_recv
    )
    greet_and_wait()
    weight.start()
    line.advance(1)

    rows = xn_ref.shape[0]
    tiles = rows // ROW_TILE
    scale = HEAD_DIM ** (-0.5)
    for tile in range(tiles):
        here = pl.ds(tile * ROW_TILE, ROW_TILE)
        reach = (tile + 1) * ROW_TILE
        shape = (ROW_TILE, reach)
        row_ids = lax.broadcasted_iota(jnp.int32, shape, 0) + tile * ROW_TILE
        key_ids = lax.broadcasted_iota(jnp.int32, shape, 1)
        allowed = (seg_col_ref[here, :] == seg_row_ref[:, pl.ds(0, reach)]) & (key_ids <= row_ids)
        mask_ref[here, pl.ds(0, reach)] = jnp.where(allowed, 0.0, masked_score)

    def turned(values, here, direction):
        ahead = pltpu.roll(values, LANES - ROT_DIM // 2, 1)
        behind = pltpu.roll(values, ROT_DIM // 2, 1)
        return values * keep_ref[here, :] + direction * (
            ahead * ahead_ref[here, :] + behind * behind_ref[here, :]
        )

    def project(here):
        for kind in range(3):
            columns = pl.ds(kind * head_cols, head_cols)
            values = contract(xn_ref[here, :], weight_ref[:, columns], 1, 0) + bias_ref[:, columns]
            if kind == 2:
                low_ref[here, columns] = values.astype(jnp.bfloat16)
                continue
            for first in range(0, head_cols, LANES):
                part = turned(values[:, first : first + LANES], here, 1.0).astype(jnp.bfloat16)
                if kind == 0:
                    part = part * scale
                low_ref[here, pl.ds(kind * head_cols + first, LANES)] = part
        columns = pl.ds(3 * head_cols, head_cols)
        values = contract(gy_ref[here, :], weight_ref[:, columns], 1, 0)
        go_ref[here, :] = values.astype(jnp.bfloat16)

    by_rows(rows, ROW_TILE, project)

    lane = lax.broadcasted_iota(jnp.int32, (ROW_TILE, LANES), 1)
    first_head = lane < HEAD_DIM

    def one_pair(pair, carry):
        column = pl.multiple_of(pair * LANES, LANES)
        q_lanes = pl.ds(column, LANES)
        k_lanes = pl.ds(pl.multiple_of(head_cols + column, LANES), LANES)
        v_lanes = pl.ds(pl.multiple_of(2 * head_cols + column, LANES), LANES)
        dk_acc[...] = jnp.zeros_like(dk_acc)
        dv_acc[...] = jnp.zeros_like(dv_acc)
        for tile in range(tiles):
            here = pl.ds(tile * ROW_TILE, ROW_TILE)
            keys = pl.ds(0, (tile + 1) * ROW_TILE)
            outs = []
            query_grads = []
            for head in range(LANES // HEAD_DIM):
                mine = first_head if head == 0 else jnp.logical_not(first_head)
                none = jnp.zeros((ROW_TILE, LANES), jnp.bfloat16)
                query = jnp.where(mine, low_ref[here, q_lanes], none)
                grad_out = jnp.where(mine, go_ref[here, q_lanes], none)
                scores = contract(query, low_ref[keys, k_lanes], 1, 1) + mask_ref[here, keys]
                peak = jnp.max(scores, axis=1, keepdims=True)
                weights = jnp.exp(scores - peak)
                share = 1.0 / jnp.sum(weights, axis=1, keepdims=True)
                probs = weights * share
                probs_low = probs.astype(jnp.bfloat16)
                outs.append(contract(probs_low, low_ref[keys, v_lanes], 1, 0))
                grad_probs = contract(grad_out, low_ref[keys, v_lanes], 1, 1)
                delta = jnp.sum(probs * grad_probs, axis=1, keepdims=True)
                grad_scores = (probs * (grad_probs - delta)).astype(jnp.bfloat16)
                query_grads.append(contract(grad_scores, low_ref[keys, k_lanes], 1, 0))
                dk_acc[keys, :] += contract(grad_scores, query, 0, 0)
                dv_acc[keys, :] += contract(probs_low, grad_out, 0, 0)
            or_ref[here, q_lanes] = jnp.where(first_head, outs[0], outs[1]).astype(jnp.bfloat16)
            dq_acc[here, :] = jnp.where(first_head, query_grads[0], query_grads[1])
        for tile in range(tiles):
            here = pl.ds(tile * ROW_TILE, ROW_TILE)
            query_grad = turned(dq_acc[here, :], here, -1.0) * scale
            grad_ref[here, q_lanes] = query_grad.astype(jnp.bfloat16)
            key_grad = turned(dk_acc[here, :], here, -1.0)
            grad_ref[here, k_lanes] = key_grad.astype(jnp.bfloat16)
            grad_ref[here, v_lanes] = dv_acc[here, :].astype(jnp.bfloat16)

        @pl.when(pair == 0)
        def _():
            weight.advance(1)
            line.advance(2)

        return carry

    lax.fori_loop(0, head_cols // LANES, one_pair, 0)
    weight.advance(2)
    line.advance(3)
    products.far()
    products.near()
    for step in range(3, weight.count):
        weight.advance(step)
    for step in range(4, weight.count):
        line.advance(step)
    line.finish(owned_ref)
    weight.finish()


def third_step(block, ready, normed, grad_rows, full_qkvo, bias_qkv, segment, cosine, sine):
    rows, width = normed.shape
    count = lax.axis_size("dp") // 2
    columns = full_qkvo.shape[1]
    head_cols = columns // 4
    part = width // (2 * count)
    low = jnp.bfloat16
    still = jnp.ones((rows, HEAD_DIM - ROT_DIM), jnp.float32)
    zero = jnp.zeros((rows, ROT_DIM // 2), jnp.float32)
    repeat = (1, LANES // HEAD_DIM)
    keep = jnp.tile(jnp.concatenate([cosine, cosine, still], axis=1), repeat)
    ahead = jnp.tile(jnp.concatenate([-sine, zero, 0.0 * still], axis=1), repeat)
    behind = jnp.tile(jnp.concatenate([zero, sine, 0.0 * still], axis=1), repeat)
    return carrying(
        functools.partial(third_kernel, head_cols),
        5,
        (
            block,
            ready,
            normed,
            grad_rows,
            full_qkvo,
            bias_qkv[None, :],
            segment[:, None],
            segment[None, :],
            keep,
            ahead,
            behind,
        ),
        "hvvvvvvvvvv",
        [
            ((width, block.shape[1]), low),
            ((rows, 3 * head_cols), low),
            ((rows, head_cols), low),
            ((count, part, columns), low),
            ((part, ready.shape[2]), jnp.float32),
        ],
        "hvvvv",
        gather_sems()
        + sum_scratch(part, ready.shape[2])
        + pair_scratch(part, columns)
        + [
            pltpu.VMEM((rows, rows), jnp.float32),
            pltpu.VMEM((rows, 3 * head_cols), low),
            pltpu.VMEM((rows, head_cols), low),
            pltpu.VMEM((rows, LANES), jnp.float32),
            pltpu.VMEM((rows, LANES), jnp.float32),
            pltpu.VMEM((rows, LANES), jnp.float32),
        ],
        4 * rows * width * columns + 12 * rows * rows * head_cols,
        "lines_beside_attention",
    )


def fourth_kernel(
    ready_ref,
    xn_ref,
    gy_ref,
    down_ref,
    slope_ref,
    gh_ref,
    sums_ref,
    owned_ref,
    below,
    above,
    line_send,
    line_recv,
    parcel,
    pair_send,
    pair_recv,
):
    line = LineSum(ready_ref, below, above, line_send, line_recv)
    products = PairProducts(
        [xn_ref] * 4, quarters(gh_ref), parcel, sums_ref, pair_send, pair_recv
    )
    greet_and_wait()
    line.advance(1)
    width = down_ref.shape[1] // 4

    def tile(rows):
        for quarter in range(4):
            columns = pl.ds(quarter * width, width)
            grad_act = contract(gy_ref[rows, :], down_ref[:, columns], 1, 0)
            grad_hidden = grad_act * slope_ref[rows, columns].astype(jnp.float32)
            gh_ref[rows, columns] = grad_hidden.astype(jnp.bfloat16)

    by_rows(gy_ref.shape[0], ROW_TILE, tile)
    products.far()
    line.advance(2)
    products.near()
    for step in range(3, line.count):
        line.advance(step)
    line.finish(owned_ref)


def fourth_step(ready, normed, grad_rows, turned_down, slope):
    rows, width = normed.shape
    count = lax.axis_size("dp") // 2
    columns = turned_down.shape[1]
    part = width // (2 * count)
    low = jnp.bfloat16
    return carrying(
        fourth_kernel,
        6,
        (ready, normed, grad_rows, turned_down, slope),
        "vvvvv",
        [
            ((rows, columns), low),
            ((count, part, columns), low),
            ((part, ready.shape[2]), jnp.float32),
        ],
        "vvv",
        sum_scratch(part, ready.shape[2]) + pair_scratch(part, columns),
        4 * rows * width * columns,
        "line_beside_hidden_grad",
    )


def greet_block():
    size = lax.axis_size("mp")
    place = lax.axis_index("mp")
    barrier = pltpu.get_barrier_semaphore()
    for step in range(1, size):
        peer = lax.rem(place + step, size)
        pl.semaphore_signal(barrier, inc=1, device_id={"mp": peer}, device_id_type=MESH_ID)
    return size - 1


class BlockScatter:
    def __init__(self, parts, got, send, recv):
        self.size = lax.axis_size("mp")
        self.place = lax.axis_index("mp")
        self.parts, self.got, self.send, self.recv = parts, got, send, recv
        self.half = parts.shape[1] // 2
        self.beside = self.place + 1 - 2 * lax.rem(self.place, 2)
        self.above = lax.rem(self.place + 2, 4)

    def owner(self, index):
        if self.size == 4:
            return [lax.rem(self.beside + 2, 4), self.beside, self.above, self.place][index]
        return lax.rem(self.place + 1 + index, self.size)

    def copy(self, index):
        if self.size == 4:
            part, bottom, peer = [
                (0, 0, self.beside),
                (0, 1, self.above),
                (1, 0, self.beside),
                (2, 1, self.above),
                (2, 0, self.above),
                (1, 1, self.beside),
            ][index]
            source = self.parts.at[part, pl.ds(bottom * self.half, self.half), :]
        else:
            source = self.parts.at[index]
            peer = self.owner(index)
        sems = (self.send.at[index], self.recv.at[index])
        return remote(source, self.got.at[index], *sems, "mp", peer)

    def after(self, index):
        if self.size != 4:
            if index < self.size - 1:
                self.copy(index).start()
            return
        for number in ((0, 1), (2,), (3,), ())[index]:
            self.copy(number).start()

    def second(self):
        if self.size != 4:
            return
        for number, part, bottom in ((0, 2, 0), (1, 1, 1)):
            self.copy(number).wait_recv()

            def body(rows, number=number, part=part, bottom=bottom):
                here = pl.ds(bottom * self.half + rows.start, rows.size)
                total = summed(self.parts[part, here, :], self.got[number, rows, :])
                self.parts[part, here, :] = total.astype(jnp.bfloat16)

            by_rows(self.half, 64, body)
            self.copy(number + 4).start()

    def finish(self):
        if self.size != 4:
            for index in range(self.size - 1):
                self.copy(index).wait()
            return
        for index in range(6):
            if index > 1:
                self.copy(index).wait_recv()
            self.copy(index).wait_send()

    def total(self, tile, rows):
        here = pl.ds(tile * rows, rows)
        own = self.parts[self.size - 1, here, :]
        if self.size != 4:
            return summed(own, *[self.got[index, here, :] for index in range(self.size - 1)])
        bottom = (tile * rows) // self.half
        there = pl.ds(tile * rows - bottom * self.half, rows)
        return summed(own, self.got[2 + bottom, there, :], self.got[4 + bottom, there, :])


def scatter_scratch(rows, width):
    size = lax.axis_size("mp")
    slots = (6, rows // 2, width) if size == 4 else (size - 1, rows, width)
    return [
        pltpu.VMEM((size, rows, width), jnp.bfloat16),
        pltpu.VMEM(slots, jnp.bfloat16),
        pltpu.SemaphoreType.DMA((slots[0],)),
        pltpu.SemaphoreType.DMA((slots[0],)),
    ]


def fifth_kernel(
    head_cols,
    ready_ref,
    act_ref,
    gh_ref,
    grad_ref,
    or_ref,
    down_ref,
    qkvo_ref,
    up_ref,
    x_ref,
    gy_ref,
    stats_ref,
    vectors_ref,
    out_ref,
    dx_ref,
    owned_ref,
    sums_ref,
    below,
    above,
    line_send,
    line_recv,
    g_parts,
    g_got,
    g_send,
    g_recv,
    t_parts,
    t_got,
    t_send,
    t_recv,
    one_ref,
    two_ref,
    load_sems,
    terms_ref,
    terms_got,
    terms_send,
    terms_recv,
):
    line = LineSum(ready_ref, below, above, line_send, line_recv)
    from_norm = BlockScatter(g_parts, g_got, g_send, g_recv)
    branches = BlockScatter(t_parts, t_got, t_send, t_recv)
    mp_size = from_norm.size
    mp_place = from_norm.place
    rows, width = x_ref.shape
    model_width = width * mp_size
    tiles = rows // ROW_TILE

    def load(index):
        late, share = divmod(index, mp_size)
        start = pl.multiple_of(from_norm.owner(share) * width, width)
        slot = index % 2
        where = pl.ds(start, width)
        source = down_ref if late else up_ref
        return [
            pltpu.make_async_copy(qkvo_ref.at[where, :], one_ref.at[slot], load_sems.at[0, slot]),
            pltpu.make_async_copy(source.at[where, :], two_ref.at[slot], load_sems.at[1, slot]),
        ]

    for copy in load(0):
        copy.start()
    barrier, count = greet_line()
    count += greet_block()
    pl.semaphore_wait(barrier, count)
    line.advance(1)

    for index in range(2 * mp_size):
        late, share = divmod(index, mp_size)
        slot = index % 2
        for copy in load(index):
            copy.wait()
        if index + 1 < 2 * mp_size:
            for copy in load(index + 1):
                copy.start()

        def tile(here, late=late, share=share, slot=slot):
            if late:
                part = contract(or_ref[here, :], one_ref[slot, :, pl.ds(3 * head_cols, head_cols)], 1, 1)
                part = part + contract(act_ref[here, :], two_ref[slot], 1, 1)
                t_parts[share, here, :] = part.astype(jnp.bfloat16)
            else:
                part = contract(grad_ref[here, :], one_ref[slot, :, pl.ds(0, 3 * head_cols)], 1, 1)
                part = part + contract(gh_ref[here, :], two_ref[slot], 1, 1)
                g_parts[share, here, :] = part.astype(jnp.bfloat16)

        by_rows(rows, ROW_TILE, tile)
        (branches if late else from_norm).after(share)
        if index == mp_size:
            from_norm.second()
        if index == mp_size + 1:
            line.advance(2)
    branches.second()
    from_norm.finish()

    def lane_pair(first, second):
        lane = lax.broadcasted_iota(jnp.int32, (ROW_TILE, LANES), 1)
        return jnp.where(lane == 0, first, jnp.where(lane == 1, second, 0.0))

    gain = vectors_ref[0:1, :]
    columns = [jnp.zeros((1, width), jnp.float32) for _ in range(3)]
    for tile in range(tiles):
        here = pl.ds(tile * ROW_TILE, ROW_TILE)
        normalized = (x_ref[here, :].astype(jnp.float32) - stats_ref[here, 0:1]) * stats_ref[here, 1:2]
        grad = from_norm.total(tile, ROW_TILE)
        gained = grad * gain
        terms = lane_pair(
            jnp.sum(gained, axis=1, keepdims=True),
            jnp.sum(gained * normalized, axis=1, keepdims=True),
        )
        terms_ref[:, here] = jnp.transpose(terms)[:8, :]
        upstream = gy_ref[here, :].astype(jnp.float32) * stats_ref[here, 2:3]
        columns[0] += jnp.sum(grad * normalized, axis=0, keepdims=True)
        columns[1] += jnp.sum(grad, axis=0, keepdims=True)
        columns[2] += jnp.sum(upstream, axis=0, keepdims=True)
    sums_ref[...] = jnp.concatenate(columns + [jnp.zeros((5, width), jnp.float32)], axis=0)

    def terms_copy(step):
        peer = lax.rem(mp_place + step, mp_size)
        slot = step - 1
        sems = (terms_send.at[slot], terms_recv.at[slot])
        return remote(terms_ref, terms_got.at[slot], *sems, "mp", peer)

    for step in range(1, mp_size):
        terms_copy(step).start()
    for step in range(3, line.count):
        line.advance(step)
    for step in range(1, mp_size):
        terms_copy(step).wait()
    for tile in range(tiles):
        here = pl.ds(tile * ROW_TILE, ROW_TILE)
        terms = terms_ref[:, here]
        for slot in range(mp_size - 1):
            terms = terms + terms_got[slot, :, here]
        wide = jnp.concatenate([terms, jnp.zeros((LANES - 8, ROW_TILE), jnp.float32)], axis=0)
        terms = jnp.transpose(wide) * (1.0 / model_width)
        inv_std = stats_ref[here, 1:2]
        normalized = (x_ref[here, :].astype(jnp.float32) - stats_ref[here, 0:1]) * inv_std
        gained = from_norm.total(tile, ROW_TILE) * gain
        upstream = gy_ref[here, :].astype(jnp.float32) * stats_ref[here, 2:3]
        dx_ref[here, :] = upstream + inv_std * (gained - terms[:, 0:1] - normalized * terms[:, 1:2])
    branches.finish()
    for tile in range(tiles):
        here = pl.ds(tile * ROW_TILE, ROW_TILE)
        total = x_ref[here, :].astype(jnp.float32) + branches.total(tile, ROW_TILE)
        total = total + vectors_ref[1:2, :] + vectors_ref[2:3, :]
        out_ref[here, :] = total.astype(jnp.bfloat16)
    line.finish(owned_ref)


def fifth_step(
    ready,
    activated,
    grad_hidden,
    grad_projected,
    attended,
    turned_down,
    full_qkvo,
    full_up,
    tokens,
    cotangent,
    stats,
    vectors,
):
    rows, width = tokens.shape
    head_cols = attended.shape[1]
    count, part, columns = ready.shape
    mp_size = lax.axis_size("mp")
    low = jnp.bfloat16
    return carrying(
        functools.partial(fifth_kernel, head_cols),
        7,
        (
            ready,
            activated,
            grad_hidden,
            grad_projected,
            attended,
            turned_down,
            full_qkvo,
            full_up,
            tokens,
            cotangent,
            stats,
            vectors,
        ),
        "vvvvvhhhvvvv",
        [
            ((rows, width), low),
            ((rows, width), jnp.float32),
            ((part, columns), jnp.float32),
            ((8, width), jnp.float32),
        ],
        "vvvv",
        sum_scratch(part, columns)
        + scatter_scratch(rows, width)
        + scatter_scratch(rows, width)
        + [
            pltpu.VMEM((2, width, columns), low),
            pltpu.VMEM((2, width, columns), low),
            pltpu.SemaphoreType.DMA((2, 2)),
            pltpu.VMEM((8, rows), jnp.float32),
            pltpu.VMEM((mp_size - 1, 8, rows), jnp.float32),
            pltpu.SemaphoreType.DMA((mp_size - 1,)),
            pltpu.SemaphoreType.DMA((mp_size - 1,)),
        ],
        4 * rows * width * mp_size * columns,
        "line_beside_norm_grad",
    )


def dot_f32(left, right, left_axis, right_axis):
    return lax.dot_general(
        left.astype(jnp.bfloat16),
        right.astype(jnp.bfloat16),
        (((left_axis,), (right_axis,)), ((), ())),
        preferred_element_type=jnp.float32,
    )


def shampoo(weight_block, grad_block, left, right):
    left_new = 0.5 * left[0, 0, 0] + 0.5 * dot_f32(grad_block, grad_block, 1, 1)
    right_new = 0.5 * right[0, 0, 0] + 0.5 * dot_f32(grad_block, grad_block, 0, 0)
    step_block = dot_f32(dot_f32(left[1, 0, 0], grad_block, 1, 0), right[1, 0, 0], 1, 0)
    return (weight_block - matrix_rate * step_block, left_new[None, None], right_new[None, None])


def shampoo_turned(weight_block, turned_grad, left, right):
    left_new = 0.5 * left[0, 0, 0] + 0.5 * dot_f32(turned_grad, turned_grad, 0, 0)
    right_new = 0.5 * right[0, 0, 0] + 0.5 * dot_f32(turned_grad, turned_grad, 1, 1)
    step_block = dot_f32(dot_f32(left[1, 0, 0], turned_grad, 1, 1), right[1, 0, 0], 1, 0)
    return (weight_block - matrix_rate * step_block, left_new[None, None], right_new[None, None])


def vector_update(state, grad):
    stat_new = 0.5 * state[1] + 0.5 * grad * grad
    param_new = state[0] - vector_rate * grad * lax.rsqrt(stat_new)
    return (param_new, stat_new)


def local(
    tokens,
    cotangent,
    seq_lengths,
    w_qkv,
    qkv_bias_state,
    w_out,
    out_bias_state,
    w_up,
    up_bias_state,
    w_down,
    ln_state,
    qkv_left,
    qkv_right,
    out_left,
    out_right,
    up_left,
    up_right,
    down_left,
    down_right,
):
    row_count, share_width = tokens.shape
    mp_size = lax.axis_size("mp")
    dp_size = lax.axis_size("dp")
    model_width = share_width * mp_size
    own_width = w_qkv.shape[2]
    mp_place = lax.axis_index("mp")

    flat_master = jnp.concatenate([w_qkv[:, kind] for kind in range(3)], axis=1)
    block_qkvo = jnp.concatenate([flat_master, w_out.T], axis=1).astype(jnp.bfloat16)
    piece = ln_state.shape[2]
    small = jnp.concatenate(
        [
            ln_state[0].reshape(-1),
            qkv_bias_state[0].reshape(-1),
            out_bias_state[0].reshape(-1),
            up_bias_state[0].reshape(-1),
        ]
    )
    small = small.astype(jnp.bfloat16).astype(jnp.float32)
    filled = small.shape[0]
    small = jnp.pad(small, (0, -filled % 1024)).reshape(1, 8, -1)
    full_up, x_full, upstream, spread = first_gathers(
        w_up.astype(jnp.bfloat16), tokens, cotangent, small
    )
    spread = spread.reshape(mp_size * dp_size, -1)[:, :filled]
    norm_all = spread[:, : 2 * piece].reshape(-1, 2, piece).transpose(1, 0, 2).reshape(2, -1)
    here = take(spread.reshape(mp_size, dp_size, -1), mp_place)
    bias_qkv = here[:, 2 * piece : 5 * piece].reshape(dp_size, 3, piece)
    bias_qkv = bias_qkv.transpose(1, 0, 2).reshape(-1)
    bias_out = here[:, 5 * piece : 7 * piece].reshape(dp_size, 2, piece)
    bias_out = bias_out.transpose(1, 0, 2).reshape(2, -1)
    bias_up = here[:, 7 * piece :].reshape(-1)

    segment, offsets, is_valid = segment_layout(seq_lengths[0], row_count)
    cosine, sine = rope_tables(offsets)

    inputs = x_full.astype(jnp.float32)
    row_mean = jnp.mean(inputs, axis=1, keepdims=True)
    row_var = jnp.mean(inputs * inputs, axis=1, keepdims=True) - row_mean * row_mean
    inv_std = lax.rsqrt(row_var + norm_eps)
    normed = ((inputs - row_mean) * inv_std * norm_all[0] + norm_all[1]).astype(jnp.bfloat16)
    grad_rows = (upstream.astype(jnp.float32) * is_valid[:, None]).astype(jnp.bfloat16)
    full_qkvo, activated, slope, ready_down = second_step(
        block_qkvo, normed, grad_rows, full_up, bias_up
    )
    turned_down, grad_projected, attended, ready_qkvo, owned_down = third_step(
        w_down.T.astype(jnp.bfloat16),
        ready_down,
        normed,
        grad_rows,
        full_qkvo,
        bias_qkv,
        segment,
        cosine,
        sine,
    )
    grad_hidden, ready_up, owned_qkvo = fourth_step(
        ready_qkvo, normed, grad_rows, turned_down, slope
    )
    norm_here = lax.dynamic_slice_in_dim(norm_all, mp_place * share_width, share_width, 1)
    vectors = jnp.concatenate(
        [norm_here[:1], bias_out, jnp.zeros((5, share_width), jnp.float32)], axis=0
    )
    stats = jnp.concatenate([row_mean, inv_std, is_valid[:, None]], axis=1)
    output, input_grad, owned_up, column_sums = fifth_step(
        ready_up,
        activated,
        grad_hidden,
        grad_projected,
        attended,
        turned_down,
        full_qkvo,
        full_up,
        tokens,
        cotangent,
        stats,
        vectors,
    )

    def owner_rows(values, count):
        return values.reshape(count, dp_size, -1).transpose(1, 0, 2).reshape(dp_size, -1)

    vector_grads = jnp.concatenate(
        [
            owner_rows(column_sums[0], 1),
            owner_rows(column_sums[1], 1),
            owner_rows(jnp.sum(grad_projected.astype(jnp.float32), axis=0), 3),
            owner_rows(column_sums[2], 1),
            owner_rows(jnp.sum(grad_hidden.astype(jnp.float32), axis=0), 1),
        ],
        axis=1,
    )
    width = vector_grads.shape[1]
    vector_grads = jnp.pad(vector_grads, ((0, 0), (0, -width % 1024))).reshape(dp_size, 8, -1)
    vector_sums = jnp.sum(exchange(vector_grads, ("dp",), 3, False), axis=0).reshape(-1)[:width]
    owned_norm = vector_sums[: 2 * piece].reshape(2, piece)
    owned_bqkv = vector_sums[2 * piece : 5 * piece].reshape(3, piece)
    bias_total = vector_sums[5 * piece : 6 * piece]
    owned_obias = jnp.stack([bias_total, bias_total])
    owned_bup = vector_sums[6 * piece :]

    owned_qkv = owned_qkvo[:, : 3 * own_width]
    owned_out = owned_qkvo[:, 3 * own_width :]
    new_w_down, down_left_new, down_right_new = shampoo_turned(
        w_down, owned_down, down_left, down_right
    )
    new_w_out, out_left_new, out_right_new = shampoo_turned(w_out, owned_out, out_left, out_right)
    new_qkv_block, qkv_left_new, qkv_right_new = shampoo(
        flat_master, owned_qkv, qkv_left, qkv_right
    )
    new_w_qkv = jnp.stack(
        [new_qkv_block[:, kind * own_width : (kind + 1) * own_width] for kind in range(3)], axis=1
    )
    new_w_up, up_left_new, up_right_new = shampoo(w_up, owned_up, up_left, up_right)
    qkv_params, qkv_stats = vector_update(qkv_bias_state, owned_bqkv)
    obias_params, obias_stats = vector_update(out_bias_state, owned_obias)
    norm_new_params, norm_new_stats = vector_update(ln_state, owned_norm)
    new_up_bias, new_up_stat = vector_update(up_bias_state, owned_bup)
    new_vector_params = jnp.concatenate([qkv_params, obias_params, norm_new_params], axis=0)
    new_vector_stats = jnp.concatenate([qkv_stats, obias_stats, norm_new_stats], axis=0)
    return (
        output,
        input_grad,
        new_w_qkv,
        new_w_out,
        new_w_up,
        new_w_down,
        new_vector_params,
        new_vector_stats,
        new_up_bias,
        new_up_stat,
        qkv_left_new,
        qkv_right_new,
        out_left_new,
        out_right_new,
        up_left_new,
        up_right_new,
        down_left_new,
        down_right_new,
    )


def solution(mesh):
    return jax.shard_map(
        local,
        mesh=mesh,
        in_specs=(
            P("dp", "mp"),
            P("dp", "mp"),
            P("dp", None),
            P("dp", None, "mp"),
            P(None, None, ("mp", "dp")),
            P("mp", "dp"),
            P(None, None, ("mp", "dp")),
            P("dp", "mp"),
            P(None, ("mp", "dp")),
            P("mp", "dp"),
            P(None, None, ("mp", "dp")),
            P(None, "mp", "dp", None, None),
            P(None, "mp", "dp", None, None),
            P(None, "mp", "dp", None, None),
            P(None, "mp", "dp", None, None),
            P(None, "mp", "dp", None, None),
            P(None, "mp", "dp", None, None),
            P(None, "mp", "dp", None, None),
            P(None, "mp", "dp", None, None),
        ),
        out_specs=(
            P("dp", "mp"),
            P("dp", "mp"),
            P("dp", None, "mp"),
            P("mp", "dp"),
            P("dp", "mp"),
            P("mp", "dp"),
            P(None, ("mp", "dp")),
            P(None, ("mp", "dp")),
            P(("mp", "dp")),
            P(("mp", "dp")),
            P("mp", "dp", None, None),
            P("mp", "dp", None, None),
            P("mp", "dp", None, None),
            P("mp", "dp", None, None),
            P("mp", "dp", None, None),
            P("mp", "dp", None, None),
            P("mp", "dp", None, None),
            P("mp", "dp", None, None),
        ),
        check_vma=False,
    )
```

time: 685 us -> 642 us (0.937)
  Pallas kernels: 76.1 us -> 506 us
  waiting for transfers between devices: 178 us -> 0 us
  matrix products: 201 us -> 77.4 us
  starting transfers between devices: 87.5 us -> 0 us
  other arithmetic: 67.6 us -> 32.2 us
  local copies, waits for them, and re-layouts: 51.7 us -> 17.3 us
  between operations: 15.6 us -> 1.53 us
    pallas_call x1 -> x5, Pallas kernels: 37.4 us -> 498 us  [the longest x4 392 us: carrying(): pl.pallas_call(kernel, in_specs=[spaces[place] for place in in_places], o...]
    ppermute x41 -> x0, waiting for transfers between devices: 178 us -> none  [the longest x9 88.4 us: send(): self.rising = lax.ppermute(self.sends[0], 'dp', up_pairs)]
    dot_general x16 -> x0, matrix products: 134 us -> none  [the longest x4 48.3 us: contract(): lax.dot_general(left, right, (((left_axis,), (right_axis,)), ((), ())), p...]
    ppermute x41 -> x0, starting transfers between devices: 87.3 us -> none  [the longest x9 50.2 us: send(): self.rising = lax.ppermute(self.sends[0], 'dp', up_pairs)]
    pallas_call x3 -> x1, Pallas kernels: 38.7 us -> 7.25 us  [exchange(): pl.pallas_call(functools.partial(exchange_kernel, axes, count, same), out...]
    convert_element_type x14 -> x0, other arithmetic: 28.1 us -> none  [the longest x4 9.65 us: ready(): down_block = summed(down_block, self.falling).astype(jnp.bfloat16)]
    dot_general x12, matrix products: 66.3 us -> 77.4 us  [dot_f32(): lax.dot_general(left.astype(jnp.bfloat16), right.astype(jnp.bfloat16), ((...]
    unnamed x177 -> x36, local copies, waits for them, and re-layouts: 16 us -> 5.19 us
  transfers between devices with their start and end apart: 44 -> 0, of which waited for: 20 -> 0; matrix products, arithmetic and copies ran while one was open for 37% -> 0% of each run, Pallas kernels for 11% -> 0%
where the time goes in v2:
time: 642 us; the launch traced here: 634 us
  Pallas kernels  506 us (79%)
  matrix products  77.4 us (12%)
  other arithmetic  32.2 us (5%)
  local copies, waits for them, and re-layouts  17.3 us (3%)
    pallas_call x4, Pallas kernels, carrying(): pl.pallas_call(kernel, in_specs=[spaces[place] for place in in_places], o...  392 us
    pallas_call x1, Pallas kernels, first_gathers(): pl.pallas_call(first_kernel, in_specs=[hbm, hbm, hbm, vmem], out_specs=[h...  106 us
    dot_general x12, matrix products, dot_f32(): lax.dot_general(left.astype(jnp.bfloat16), right.astype(jnp.bfloat16), ((...  77.4 us

profile of v2, /device:TPU:0, one launch (start us, length us, event | category | flops | bytes accessed | tf_op | source)
XLA Modules:
  0.0 634.0 jit_solution(4574808761323745683)
XLA Ops:
  4.5 2.7 convert_element_type.130.block_ref
  7.2 106.1 %first_gathers.1 = (bf16[2048,2048]{1,0:T(8,128)(2,1)}, bf16[1024,2048]{1,0:T(8,128)(2,1)}, bf16[1024,2048]{1,0:T(8,128)(2,1)}, f32[32,8,128]{2,1,0:T(8,128)}) custom-call(bf16[256,2048]{1,0:T(8,128)(2,1)} %convert_element_type.130.block_ref, bf16[1024,512]{1,0:T(8,128)(2,1)} %x_ref.3, bf16[1024,512]{1,0:T(8,128)(2,1)} %gy_ref.3, f32[1,8,128]{2,1,0:T(8,128)} %fusion.74.small_ref), custom_call_target="tpu_custom_call" | custom-call | tf_op jit(solution)/shard_map/first_gathers/pallas_call | solution.py:542
  114.6 5.7 fusion.10
  120.7 4.8 fusion.9.xn_ref
  126.4 1.1 pad_maximum_fusion.1.block_ref
  127.6 87.1 %gather_beside_hidden.1 = (bf16[2048,2048]{1,0:T(8,128)(2,1)}, bf16[1024,2048]{1,0:T(8,128)(2,1)}, bf16[1024,2048]{1,0:T(8,128)(2,1)}, bf16[4,256,2048]{2,1,0:T(8,128)(2,1)}) custom-call(bf16[256,2048]{1,0:T(8,128)(2,1)} %pad_maximum_fusion.1.block_ref, bf16[1024,2048]{1,0:T(8,128)(2,1)} %fusion.9.xn_ref, bf16[1024,2048]{1,0:T(8,128)(2,1)} %get-tuple-element.98.gy_ref, ...), custom_call_target="tpu_custom_call" | custom-call | flops 17179869184 | bytes 33554432 | tf_op jit(solution)/shard_map/gather_beside_hidden/pallas_call | solution.py:617
  219.7 1.5 add_select_fusion.seg_col_ref
  221.2 1.2 compare_select_fusion.seg_row_ref
  222.4 1.4 copy.74
  223.8 133.2 %lines_beside_attention.1 = (bf16[2048,2048]{1,0:T(8,128)(2,1)}, bf16[1024,1536]{1,0:T(8,128)(2,1)}, bf16[1024,512]{1,0:T(8,128)(2,1)}, bf16[4,256,2048]{2,1,0:T(8,128)(2,1)}, f32[256,2048]{1,0:T(8,128)}) custom-call(bf16[256,2048]{1,0:T(8,128)(2,1)} %bitcast.174, bf16[4,256,2048]{2,1,0:T(8,128)(2,1)} %get-tuple-element.42.ready_ref, ...), custom_call_target="tpu_custom_call" | custom-call | flops 23622320128 | bytes 33554432 | tf_op jit(solution)/shard_map/lines_beside_attention/pallas_call | solution.py:617
  357.0 84.2 %line_beside_hidden_grad.1 = (bf16[1024,2048]{1,0:T(8,128)(2,1)}, bf16[4,256,2048]{2,1,0:T(8,128)(2,1)}, f32[256,2048]{1,0:T(8,128)}) custom-call(bf16[4,256,2048]{2,1,0:T(8,128)(2,1)} %get-tuple-element.44.ready_ref, bf16[1024,2048]{1,0:T(8,128)(2,1)} %fusion.9.xn_ref, bf16[1024,2048]{1,0:T(8,128)(2,1)} %get-tuple-element.98.gy_ref, ...), custom_call_target="tpu_custom_call" | custom-call | flops 17179869184 | bytes 33554432 | tf_op jit(solution)/shard_map/line_beside_hidden_grad/pallas_call | solution.py:617
  442.2 1.0 copy.86.stats_ref
  444.4 87.8 %line_beside_norm_grad.1 = (bf16[1024,512]{1,0:T(8,128)(2,1)}, f32[1024,512]{1,0:T(8,128)}, f32[256,2048]{1,0:T(8,128)}, f32[8,512]{1,0:T(8,128)}) custom-call(bf16[4,256,2048]{2,1,0:T(8,128)(2,1)} %get-tuple-element.47.ready_ref, bf16[1024,2048]{1,0:T(8,128)(2,1)} %get-tuple-element.48.act_ref, bf16[1024,2048]{1,0:T(8,128)(2,1)} %get-tuple-element.49.gh_ref, ...), custom_call_target="tpu_custom_call" | custom-call | flops 17179869184 | bytes 33554432 | tf_op jit(solution)/shard_map/line_beside_norm_grad/pallas_call | solution.py:617
  532.2 15.6 %fusion.3 = f32[1,1,2048,2048]{3,2,1,0:T(8,128)} fusion(f32[2,1,1,2048,2048]{4,3,2,1,0:T(8,128)} %param.35, f32[256,2048]{1,0:T(8,128)} %get-tuple-element.55), kind=kOutput, calls=%fused_computation.7 | convolution fusion | flops 2156396544 | bytes 35651584 | tf_op jit(solution)/shard_map/dot_general | solution.py:1220
  548.8 2.8 convert_reduce_fusion.1
  551.7 2.5 convert_reduce_fusion.2
  555.1 7.2 %exchange.1 = f32[8,8,128]{2,1,0:T(8,128)} custom-call(f32[8,8,128]{2,1,0:T(8,128)} %bitcast.181), custom_call_target="tpu_custom_call" | custom-call | tf_op jit(solution)/shard_map/exchange/pallas_call | solution.py:117
  565.2 1.7 convert.67
  566.9 1.1 slice_bitcast_fusion.5
  568.0 6.0 fusion.20
  574.2 1.3 pad_maximum_fusion
  575.4 9.0 %fusion.5 = f32[1,1,1536,1536]{3,2,1,0:T(8,128)} fusion(f32[2,1,1,1536,1536]{4,3,2,1,0:T(8,128)} %param.31, bf16[256,2048]{1,0:T(8,128)(2,1)S(1)} %convert.67), kind=kOutput, calls=%fused_computation.14 | convolution fusion | flops 1212678144 | bytes 19660800 | tf_op jit(solution)/shard_map/dot_general | solution.py:1220
  584.4 11.0 %fusion.23 = f32[256,2048]{1,0:T(8,128)} fusion(f32[256,2048]{1,0:T(8,128)} %param.26, f32[2,1,1,2048,2048]{4,3,2,1,0:T(8,128)} %param.35, f32[2,1,1,256,256]{4,3,2,1,0:T(8,128)} %param.34, f32[256,2048]{1,0:T(8,128)S(1)} %copy-done.1), kind=kOutput, calls=%fused_computation.31 | convolution fusion | flops 2417491968 | bytes 14811136 | tf_op jit(solution)/shard_map/dot_general | solution.py:1220
  595.5 3.5 fusion.40
  599.0 11.3 %fusion.1 = f32[1,1,2048,2048]{3,2,1,0:T(8,128)} fusion(f32[2,1,1,2048,2048]{4,3,2,1,0:T(8,128)} %param.36, f32[256,2048]{1,0:T(8,128)S(1)} %copy-done), kind=kOutput, calls=%fused_computation.4 | convolution fusion | flops 2156396544 | bytes 35651584 | tf_op jit(solution)/shard_map/dot_general | solution.py:1220
  610.3 1.3 fusion.30
  611.6 2.9 convolution_subtract_fusion.1
  614.4 1.9 fusion.34
  616.4 2.1 fusion.36
  618.4 10.5 %convolution_subtract_fusion = f32[2048,256]{1,0:T(8,128)} fusion(f32[2048,256]{1,0:T(8,128)} %param.28, f32[2,1,1,2048,2048]{4,3,2,1,0:T(8,128)} %param.36, f32[2,1,1,256,256]{4,3,2,1,0:T(8,128)} %param.37, f32[256,2048]{1,0:T(8,128)S(1)} %copy-done), kind=kOutput, calls=%fused_computation.29 | convolution fusion | flops 2417491968 | bytes 14811136 | tf_op jit(solution)/shard_map/dot_general | solution.py:1220
  629.0 2.3 fusion.38
  632.2 1.3 copy.112
  (115 shorter events, 19.4 us)
Async XLA Ops:
  0.7 112.6 %copy-start.12 = (s32[1,16]{1,0:T(1,128)S(1)}, s32[1,16]{1,0:T(1,128)}, u32[]{:S(2)}) copy-start(s32[1,16]{1,0:T(1,128)} %param.21) | copy-start | bytes 196
  114.6 5.7 copy-start.9
  120.7 5.5 copy-start.3
  120.7 5.6 copy-start.5
  215.7 6.8 %copy-start.2 = (f32[2048,256]{1,0:T(8,128)S(1)}, f32[2048,256]{1,0:T(8,128)}, u32[]{:S(2)}) copy-start(f32[2048,256]{1,0:T(8,128)} %param.28) | copy-start | bytes 6291460
  547.8 15.5 %copy-start.10 = (f32[2,2,64]{2,1,0:T(2,128)S(1)}, f32[2,2,64]{2,1,0:T(2,128)}, u32[]{:S(2)}) copy-start(f32[2,2,64]{2,1,0:T(2,128)} %param.25) | copy-start | bytes 3076
  547.8 15.6 %copy-start.11 = (f32[2,2,64]{2,1,0:T(2,128)S(1)}, f32[2,2,64]{2,1,0:T(2,128)}, u32[]{:S(2)}) copy-start(f32[2,2,64]{2,1,0:T(2,128)} %param.29) | copy-start | bytes 3076
  551.7 15.3 %copy-start.4 = (f32[256,3,512]{2,0,1:T(8,128)S(1)}, f32[256,3,512]{2,0,1:T(8,128)}, u32[]{:S(2)}) copy-start(f32[256,3,512]{2,0,1:T(8,128)} %param.22) | copy-start | bytes 4718596
  575.4 9.0 %copy-start.1 = (f32[256,2048]{1,0:T(8,128)S(1)}, f32[256,2048]{1,0:T(8,128)}, u32[]{:S(2)}) copy-start(f32[256,2048]{1,0:T(8,128)} %get-tuple-element.55) | copy-start | bytes 6291460
  595.4 3.6 copy-start
  599.0 11.3 %copy-start.6 = (f32[2,1,1,512,512]{4,3,2,1,0:T(8,128)S(1)}, f32[2,1,1,512,512]{4,3,2,1,0:T(8,128)}, u32[]{:S(2)}) copy-start(f32[2,1,1,512,512]{4,3,2,1,0:T(8,128)} %param.32) | copy-start | bytes 6291460
  618.4 12.8 %copy-start.8 = (bf16[1024,512]{1,0:T(8,128)(2,1)S(1)}, bf16[1024,512]{1,0:T(8,128)(2,1)}, u32[]{:S(2)}) copy-start(bf16[1024,512]{1,0:T(8,128)(2,1)} %get-tuple-element.118) | copy-start | bytes 3145732
  629.0 3.3 copy-start.7

commit v3 on v2

v3 whole, which is shorter than its diff:
```python
import functools
import math

import jax
import jax.numpy as jnp
from jax import lax
from jax.experimental import pallas as pl
from jax.experimental.pallas import tpu as pltpu
from jax.sharding import PartitionSpec as P

HEAD_DIM = 64
ROT_DIM = 32
LANES = 128
ROW_TILE = 256


norm_eps = 1e-05
matrix_rate = 1.0
vector_rate = 0.4
masked_score = -1e30


def segment_of(ends, positions, axis, slots):
    finished = ends <= positions
    segment = jnp.sum(jnp.where(finished, 1, 0), axis=axis, keepdims=True)
    starting = jnp.max(jnp.where(finished, ends, 0), axis=axis, keepdims=True)
    return (segment, starting, segment < slots)


def rope_tables(offsets):
    lane = lax.rem(lax.broadcasted_iota(jnp.int32, (1, LANES), 1), HEAD_DIM)
    half_rot = ROT_DIM // 2
    freq_index = lax.rem(lane, half_rot).astype(jnp.float32)
    inverse = jnp.exp(-(2.0 * freq_index / ROT_DIM) * math.log(10000.0))
    angles = offsets * inverse
    cosine, sine = (jnp.cos(angles), jnp.sin(angles))
    keep = jnp.where(lane < ROT_DIM, cosine, 1.0)
    ahead = jnp.where(lane < half_rot, -sine, 0.0)
    behind = jnp.where((lane >= half_rot) & (lane < ROT_DIM), sine, 0.0)
    return (keep, ahead, behind)


def gelu_pair(values):
    square = values * values
    inner = math.sqrt(2.0 / math.pi) * values * (1.0 + 0.044715 * square)
    bent = jnp.tanh(inner)
    half = 0.5 * (1.0 + bent)
    slope = half + 0.5 * values * (1.0 - bent * bent) * math.sqrt(2.0 / math.pi) * (
        1.0 + 3.0 * 0.044715 * square
    )
    return (values * half, slope)


def take(array, index, axis=0):
    return lax.dynamic_index_in_dim(array, index, axis, keepdims=False)


def summed(*terms):
    total = terms[0].astype(jnp.float32)
    for term in terms[1:]:
        total = total + term.astype(jnp.float32)
    return total


def contract(left, right, left_axis, right_axis):
    return lax.dot_general(
        left, right, (((left_axis,), (right_axis,)), ((), ())), preferred_element_type=jnp.float32
    )


MESH_ID = pl.DeviceIdType.MESH


def remote(source, target, send_sem, recv_sem, axis, peer):
    return pltpu.make_async_remote_copy(
        src_ref=source,
        dst_ref=target,
        send_sem=send_sem,
        recv_sem=recv_sem,
        device_id={axis: peer},
        device_id_type=MESH_ID,
    )


def greet_line():
    size = lax.axis_size("dp")
    place = lax.axis_index("dp")
    barrier = pltpu.get_barrier_semaphore()
    core = lax.rem(place, 2)
    peers = [place + 1 - 2 * core, lax.rem(place + 2, size), lax.rem(place + size - 2, size)]
    for peer in peers:
        pl.semaphore_signal(barrier, inc=1, device_id={"dp": peer}, device_id_type=MESH_ID)
    return (barrier, len(peers))


PIECES = 2
VMEM_LIMIT = 60 * 1024 * 1024


def piecewise(body, first=0, last=PIECES):
    def once(piece, carry):
        body(piece)
        return carry

    lax.fori_loop(first, last, once, 0)


class LineGather:
    def __init__(self, own, full, send, recv):
        self.count = lax.axis_size("dp") // 2
        self.place = lax.axis_index("dp")
        self.spot = self.place // 2
        self.core = lax.rem(self.place, 2)
        self.own, self.full, self.send, self.recv = own, full, send, recv
        self.rows = own.shape[0]
        self.part = self.rows // PIECES

    def copy(self, kind, step, piece, chip, peer, from_own=False):
        offset = piece * self.part
        start = pl.multiple_of((2 * chip + self.core) * self.rows + offset, self.part)
        block = self.full.at[pl.ds(start, self.part), :]
        source = block
        if from_own:
            source = self.own.at[pl.ds(pl.multiple_of(offset, self.part), self.part), :]
        sems = (self.send.at[kind, step, piece], self.recv.at[kind, step, piece])
        return remote(source, block, *sems, "dp", peer)

    def rise(self, step, piece):
        return self.copy(0, step, piece, self.spot - step + 1, self.place + 2, step == 1)

    def fall(self, step, piece):
        return self.copy(1, step, piece, self.spot + step - 1, self.place - 2, step == 1)

    def show(self, kind, step, piece):
        chip = self.spot - step if kind == 2 else self.spot + step
        return self.copy(kind, step, piece, chip, self.place + 1 - 2 * self.core, step == 0)

    def keep(self):
        start = pl.multiple_of(self.place * self.rows, self.rows)
        target = self.full.at[pl.ds(start, self.rows), :]
        return pltpu.make_async_copy(self.own, target, self.send.at[3, 0, 0])

    def start(self):
        def body(piece):
            pl.when(self.spot + 1 < self.count)(lambda: self.rise(1, piece).start())
            pl.when(self.spot > 0)(lambda: self.fall(1, piece).start())
            self.show(2, 0, piece).start()

        piecewise(body)
        self.keep().start()

    def advance(self, step, first=0, last=PIECES):
        def body(piece):
            @pl.when(self.spot >= step)
            def _():
                self.rise(step, piece).wait_recv()
                pl.when(self.spot + 1 < self.count)(lambda: self.rise(step + 1, piece).start())
                self.show(2, step, piece).start()

            @pl.when(self.spot + step < self.count)
            def _():
                self.fall(step, piece).wait_recv()
                pl.when(self.spot > 0)(lambda: self.fall(step + 1, piece).start())
                self.show(3, step, piece).start()

        piecewise(body, first, last)

    def finish(self):
        self.keep().wait()

        def body(piece):
            self.show(2, 0, piece).wait()
            for step in range(1, self.count):
                rises = (self.spot + 1 < self.count) & (self.spot >= step - 1)
                falls = (self.spot > 0) & (self.spot + step - 1 < self.count)
                above = self.spot + step < self.count
                pl.when(rises)(lambda step=step: self.rise(step, piece).wait_send())
                pl.when(falls)(lambda step=step: self.fall(step, piece).wait_send())
                pl.when(self.spot >= step)(lambda step=step: self.show(2, step, piece).wait())
                pl.when(above)(lambda step=step: self.show(3, step, piece).wait())

        piecewise(body)


def gather_sems():
    count = lax.axis_size("dp") // 2
    return [pltpu.SemaphoreType.DMA((4, count + 1, PIECES)) for _ in range(2)]


def by_rows(rows, step, body):
    def once(index, carry):
        body(pl.ds(pl.multiple_of(index * step, step), step))
        return carry

    lax.fori_loop(0, rows // step, once, 0)


class LineSum:
    def __init__(self, blocks, from_below, from_above, send, recv):
        self.count = lax.axis_size("dp") // 2
        self.place = lax.axis_index("dp")
        self.spot = self.place // 2
        self.blocks, self.below, self.above = blocks, from_below, from_above
        self.send, self.recv = send, recv
        self.part = blocks.shape[1] // PIECES

    def rows(self, piece):
        return pl.ds(pl.multiple_of(piece * self.part, self.part), self.part)

    def move(self, kind, slots, step, piece, peer, block=None):
        rows = self.rows(piece)
        source = self.blocks.at[block, rows, :] if block is not None else slots.at[step - 2, rows, :]
        sems = (self.send.at[kind, step, piece], self.recv.at[kind, step, piece])
        return remote(source, slots.at[step - 1, rows, :], *sems, "dp", peer)

    def rise(self, step, piece, block=None):
        return self.move(0, self.below, step, piece, self.place + 2, block)

    def fall(self, step, piece, block=None):
        return self.move(1, self.above, step, piece, self.place - 2, block)

    def add(self, slots, step, block, piece):
        def body(rows):
            here = pl.ds(pl.multiple_of(piece * self.part + rows.start, rows.size), rows.size)
            total = slots[step - 2, here, :].astype(jnp.float32)
            total = total + self.blocks[block, here, :].astype(jnp.float32)
            slots[step - 2, here, :] = total.astype(jnp.bfloat16)

        by_rows(self.part, 16, body)

    def advance(self, step, first=0, last=PIECES):
        end = self.count - 1
        mirrored = end - self.spot

        def body(piece):
            pl.when(self.spot == 0)(lambda: self.rise(step, piece, self.count - step).start())
            pl.when(mirrored == 0)(lambda: self.fall(step, piece, step - 1).start())
            if step == 1:
                return

            @pl.when((self.spot > 0) & (self.spot < end) & (self.spot < step))
            def _():
                self.rise(step - 1, piece, 0).wait_recv()
                self.add(self.below, step, self.count + self.spot - step, piece)
                self.rise(step, piece).start()

            @pl.when((mirrored > 0) & (mirrored < end) & (mirrored < step))
            def _():
                self.fall(step - 1, piece, 0).wait_recv()
                self.add(self.above, step, self.spot - self.count + step, piece)
                self.fall(step, piece).start()

        piecewise(body, first, last)

    def hand_out(self, up_out, down_out):
        end = self.count - 1
        mirrored = end - self.spot

        def body(piece):
            rows = self.rows(piece)

            def move(out, slots, block):
                def once(small):
                    here = pl.ds(pl.multiple_of(rows.start + small.start, small.size), small.size)
                    total = self.blocks[block, here, :].astype(jnp.float32)
                    if slots is not None:
                        total = total + slots[end - 2, here, :].astype(jnp.float32)
                    out[here, :] = total.astype(jnp.bfloat16)

                by_rows(self.part, 16, once)

            pl.when(self.spot == 0)(lambda: move(up_out, None, 1))
            pl.when(mirrored == 0)(lambda: move(down_out, None, end - 1))

            @pl.when((self.spot > 0) & (self.spot < end))
            def _():
                self.rise(end - 1, piece, 0).wait_recv()
                move(up_out, self.below, self.spot + 1)

            @pl.when((mirrored > 0) & (mirrored < end))
            def _():
                self.fall(end - 1, piece, 0).wait_recv()
                move(down_out, self.above, self.spot - 1)

            pl.when(self.spot == end)(lambda: move(up_out, None, 0))
            pl.when(mirrored == end)(lambda: move(down_out, None, 0))
            for step in range(1, end):
                rises = (self.spot < step) & (self.spot < end)
                falls = (mirrored < step) & (mirrored < end)
                pl.when(rises)(lambda step=step: self.rise(step, piece, 0).wait_send())
                pl.when(falls)(lambda step=step: self.fall(step, piece, 0).wait_send())

        piecewise(body)

    def finish(self, out, first=0, last=PIECES):
        end = self.count - 1
        mirrored = end - self.spot

        def body(piece):
            start = piece * self.part

            def small(rows):
                return pl.ds(pl.multiple_of(start + rows.start, rows.size), rows.size)

            def begin(rows):
                out[small(rows), :] = self.blocks[self.spot, small(rows), :].astype(jnp.float32)

            by_rows(self.part, 16, begin)

            def gain(slots):
                def once(rows):
                    here = small(rows)
                    out[here, :] = out[here, :] + slots[end - 1, here, :].astype(jnp.float32)

                by_rows(self.part, 16, once)

            @pl.when(self.spot > 0)
            def _():
                self.rise(end, piece, 0).wait_recv()
                gain(self.below)

            @pl.when(self.spot < end)
            def _():
                self.fall(end, piece, 0).wait_recv()
                gain(self.above)

            for step in range(1, self.count):
                rises = (self.spot < step) & (self.spot < end)
                falls = (mirrored < step) & (mirrored < end)
                pl.when(rises)(lambda step=step: self.rise(step, piece, 0).wait_send())
                pl.when(falls)(lambda step=step: self.fall(step, piece, 0).wait_send())

        piecewise(body, first, last)


def sum_scratch(rows, columns):
    count = lax.axis_size("dp") // 2
    return [
        pltpu.VMEM((count - 1, rows, columns), jnp.bfloat16),
        pltpu.VMEM((count - 1, rows, columns), jnp.bfloat16),
        pltpu.SemaphoreType.DMA((2, count, PIECES)),
        pltpu.SemaphoreType.DMA((2, count, PIECES)),
    ]


class PairProducts:
    def __init__(self, lefts, rights, parcel, sums, send, recv):
        self.count = lax.axis_size("dp") // 2
        self.place = lax.axis_index("dp")
        self.core = lax.rem(self.place, 2)
        self.lefts, self.rights = lefts, rights
        self.parcel, self.sums, self.send, self.recv = parcel, sums, send, recv

    def copy(self, chip):
        return remote(
            self.parcel.at[chip],
            self.sums.at[chip],
            self.send.at[chip],
            self.recv.at[chip],
            "dp",
            self.place + 1 - 2 * self.core,
        )

    def product(self, chip, core, quarter):
        rows = self.sums.shape[1]
        width = self.sums.shape[2] // 4
        start = pl.multiple_of((2 * chip + core) * rows, rows)
        left = self.lefts[quarter][:, pl.ds(start, rows)]
        ref, first = self.rights[quarter]
        return contract(left, ref[:, pl.ds(first, width)], 0, 0)

    def far(self):
        width = self.sums.shape[2] // 4

        def once(chip, carry):
            for quarter in range(4):
                piece = self.product(chip, 1 - self.core, quarter)
                self.parcel[chip, :, pl.ds(quarter * width, width)] = piece.astype(jnp.bfloat16)
            self.copy(chip).start()
            return carry

        lax.fori_loop(0, self.count, once, 0)

    def near(self):
        width = self.sums.shape[2] // 4

        def once(chip, carry):
            self.copy(chip).wait()
            for quarter in range(4):
                columns = pl.ds(quarter * width, width)
                piece = self.product(chip, self.core, quarter)
                total = piece + self.sums[chip, :, columns].astype(jnp.float32)
                self.sums[chip, :, columns] = total.astype(jnp.bfloat16)
            return carry

        lax.fori_loop(0, self.count, once, 0)


def pair_scratch(rows, columns):
    count = lax.axis_size("dp") // 2
    return [
        pltpu.VMEM((count, rows, columns), jnp.bfloat16),
        pltpu.SemaphoreType.DMA((count,)),
        pltpu.SemaphoreType.DMA((count,)),
    ]


class BlockGather:
    def __init__(self, own, full, send, recv):
        self.size = lax.axis_size("mp")
        self.place = lax.axis_index("mp")
        self.own, self.full, self.send, self.recv = own, full, send, recv
        self.rows, self.width = own.shape

    def spread(self, index, rows, owner, peer, first):
        start = pl.multiple_of(owner * self.width, self.width)
        target = self.full.at[rows, pl.ds(start, self.width)]
        source = self.own if first else target
        return remote(source, target, self.send.at[index], self.recv.at[index], "mp", peer)

    def copy(self, index):
        every = pl.ds(0, self.rows)
        if self.size != 4:
            return self.spread(index, every, self.place, lax.rem(self.place + 1 + index, self.size), True)
        beside = self.place + 1 - 2 * lax.rem(self.place, 2)
        above = lax.rem(self.place + 2, 4)
        half = self.rows // 2
        if index < 2:
            return self.spread(index, every, self.place, (beside, above)[index], True)
        if index == 2:
            return self.spread(2, pl.ds(0, half), above, beside, False)
        return self.spread(3, pl.ds(half, half), beside, above, False)

    def keep(self):
        start = pl.multiple_of(self.place * self.width, self.width)
        target = self.full.at[:, pl.ds(start, self.width)]
        return pltpu.make_async_copy(self.own, target, self.send.at[self.size])

    def start(self):
        for index in range(2 if self.size == 4 else self.size - 1):
            self.copy(index).start()
        self.keep().start()

    def forward(self):
        if self.size == 4:
            self.copy(1).wait_recv()
            self.copy(2).start()
            self.copy(0).wait_recv()
            self.copy(3).start()

    def finish(self):
        self.keep().wait()
        for index in range(4 if self.size == 4 else self.size - 1):
            self.copy(index).wait_send()
            if index > 1 or self.size != 4:
                self.copy(index).wait_recv()


def block_sems():
    size = lax.axis_size("mp") + 1
    return [pltpu.SemaphoreType.DMA((size,)), pltpu.SemaphoreType.DMA((size,))]


def field_rows(spread_ref, first_row, index, piece):
    dp_size = lax.axis_size("dp")
    first = lax.axis_index("mp") * dp_size
    devices = [first + owner for owner in range(dp_size)]
    row, lane = divmod(index * piece, LANES)
    return vector_rows(spread_ref, devices, first_row + row, piece, lane)


def vector_rows(spread_ref, devices, row, piece, turn_to=0):
    if piece >= LANES:
        return [
            spread_ref[device, row + part : row + part + 1, :]
            for device in devices
            for part in range(piece // LANES)
        ]
    lane = lax.broadcasted_iota(jnp.int32, (1, LANES), 1)
    fold = LANES // piece
    groups = []
    for first in range(0, len(devices), fold):
        group = jnp.zeros((1, LANES), jnp.float32)
        for part in range(fold):
            values = spread_ref[devices[first + part], row : row + 1, :]
            turn = (part * piece - turn_to) % LANES
            values = pltpu.roll(values, turn, 1) if turn else values
            mine = (lane >= part * piece) & (lane < (part + 1) * piece)
            group = jnp.where(mine, values, group)
        groups.append(group)
    return groups


def cast_rows(source, target, here):
    target[here, :] = source[here, :].astype(target.dtype)


def first_kernel(
    piece,
    up_piece,
    slots,
    w_up_ref,
    w_qkv_ref,
    w_out_ref,
    w_down_ref,
    x_ref,
    gy_ref,
    small_ref,
    ends_ref,
    turned_out,
    full_ref,
    next_full,
    xn_ref,
    gy_full,
    spread_ref,
    stats_ref,
    act_out,
    slope_out,
    sums_ref,
    gather_send,
    gather_recv,
    next_send,
    next_recv,
    x_send,
    x_recv,
    gy_send,
    gy_recv,
    small_send,
    small_recv,
    parcel,
    pair_send,
    pair_recv,
    x_full,
    up_ref,
    act_ref,
    slope_ref,
    local_sems,
    block_ref,
    next_ref,
    valid_ref,
):
    columns = lax.axis_size("dp")
    total = columns * lax.axis_size("mp")
    mp_place = lax.axis_index("mp")
    place = mp_place * columns + lax.axis_index("dp")
    barrier = pltpu.get_barrier_semaphore()

    def device(step):
        peer = lax.rem(place + step, total)
        return {"mp": peer // columns, "dp": lax.rem(peer, columns)}

    def greet(step, carry):
        pl.semaphore_signal(barrier, inc=1, device_id=device(step), device_id_type=MESH_ID)
        return carry

    lax.fori_loop(1, total, greet, 0)
    by_rows(block_ref.shape[0], 64, lambda here: cast_rows(w_up_ref, block_ref, here))
    pl.semaphore_wait(barrier, total - 1)

    def small_copy(step):
        return pltpu.make_async_remote_copy(
            src_ref=small_ref.at[0],
            dst_ref=spread_ref.at[place],
            send_sem=small_send.at[step],
            recv_sem=small_recv.at[step],
            device_id=device(step),
            device_id_type=MESH_ID,
        )

    def begin(step, carry):
        small_copy(step).start()
        return carry

    def end(step, carry):
        small_copy(step).wait()
        return carry

    weight = LineGather(block_ref, full_ref, gather_send, gather_recv)
    later = LineGather(next_ref, next_full, next_send, next_recv)
    rows_x = BlockGather(x_ref, x_full, x_send, x_recv)
    rows_gy = BlockGather(gy_ref, gy_full, gy_send, gy_recv)
    products = PairProducts(
        [gy_full] * 4, quarters(act_ref), parcel, sums_ref, pair_send, pair_recv
    )
    lax.fori_loop(1, total, begin, 0)
    weight.start()
    rows_x.start()
    rows_gy.start()
    spread_ref[place] = small_ref[0]
    rows, width = xn_ref.shape
    depth = block_ref.shape[0]
    head_cols = w_qkv_ref.shape[2]
    for kind in range(3):
        next_ref[:, pl.ds(kind * head_cols, head_cols)] = w_qkv_ref[kind].astype(jnp.bfloat16)
    turned = jnp.transpose(w_out_ref[...]).astype(jnp.bfloat16)
    next_ref[:, pl.ds(3 * head_cols, head_cols)] = turned

    def turn_down(here):
        turned_out[:, here] = jnp.transpose(w_down_ref[here, :]).astype(jnp.bfloat16)

    by_rows(w_down_ref.shape[0], depth, turn_down)

    def mark(here):
        ids = lax.broadcasted_iota(jnp.int32, (ROW_TILE, 1), 0) + here.start
        valid = segment_of(ends_ref[0:1, :], ids, 1, slots)[2]
        valid_ref[here, :] = jnp.where(valid, 1.0, 0.0)

    by_rows(rows, ROW_TILE, mark)
    lax.fori_loop(1, total, end, 0)
    weight.advance(1)
    weight.advance(2)
    rows_x.forward()
    rows_gy.forward()
    weight.advance(3, 0, 1)
    later.start()
    weight.advance(3, 1)
    for step in range(4, weight.count):
        weight.advance(step)
    rows_x.finish()

    gains = vector_rows(spread_ref, range(total), 0, piece)
    shifts = vector_rows(spread_ref, range(total), 0, piece, piece)

    def normalize(here):
        values = x_full[here, :].astype(jnp.float32)
        mean = jnp.sum(values, axis=1, keepdims=True) * (1.0 / width)
        square = jnp.sum(values * values, axis=1, keepdims=True) * (1.0 / width)
        inv_std = lax.rsqrt(square - mean * mean + norm_eps)
        lanes = lax.broadcasted_iota(jnp.int32, (ROW_TILE, LANES), 1)
        stats_ref[here, :] = jnp.where(
            lanes == 0, mean, jnp.where(lanes == 1, inv_std, valid_ref[here, :])
        )
        for group in range(width // LANES):
            part = (x_full[here, pl.ds(group * LANES, LANES)].astype(jnp.float32) - mean) * inv_std
            part = part * gains[group] + shifts[group]
            xn_ref[here, pl.ds(group * LANES, LANES)] = part.astype(jnp.bfloat16)

    by_rows(rows, ROW_TILE, normalize)
    weight.finish()
    load = pltpu.make_async_copy(full_ref, up_ref, local_sems.at[0])
    load.start()
    rows_gy.finish()

    def blank(here):
        kept = gy_full[here, :].astype(jnp.float32) * valid_ref[here, :]
        gy_full[here, :] = kept.astype(jnp.bfloat16)

    by_rows(rows, ROW_TILE, blank)
    bias = vector_rows(
        spread_ref, [mp_place * columns + owner for owner in range(columns)], 1, up_piece
    )
    quarter_width = up_ref.shape[1] // 4
    groups = quarter_width // LANES
    load.wait()

    def tile(here):
        for quarter in range(4):
            part = pl.ds(quarter * quarter_width, quarter_width)
            shift = jnp.concatenate(bias[quarter * groups : (quarter + 1) * groups], axis=1)
            hidden = contract(xn_ref[here, :], up_ref[:, part], 1, 0) + shift
            activated, slope = gelu_pair(hidden)
            act_ref[here, part] = activated.astype(jnp.bfloat16)
            slope_ref[here, part] = slope.astype(jnp.bfloat16)

    by_rows(rows // 2, ROW_TILE, tile)
    later.advance(1)
    by_rows(rows // 2, ROW_TILE, lambda here: tile(pl.ds(rows // 2 + here.start, here.size)))
    stores = [
        pltpu.make_async_copy(act_ref, act_out, local_sems.at[1]),
        pltpu.make_async_copy(slope_ref, slope_out, local_sems.at[2]),
    ]
    for store in stores:
        store.start()
    later.advance(2, 0, 1)
    products.far()
    later.advance(2, 1)
    products.near()
    for step in range(3, later.count):
        later.advance(step)
    later.finish()
    for store in stores:
        store.wait()


def first_step(weights, tokens, cotangent, small, ends, slots, piece, up_piece):
    mp_size, dp_size = (lax.axis_size("mp"), lax.axis_size("dp"))
    count = dp_size // 2
    rows = tokens.shape[0]
    wide = (rows, tokens.shape[1] * mp_size)
    part, columns = weights[0].shape
    total = mp_size * dp_size
    low = jnp.bfloat16
    return carrying(
        functools.partial(first_kernel, piece, up_piece, slots),
        1,
        weights + (tokens, cotangent, small, ends),
        "vvvvhhvv",
        [
            ((part, columns), low),
            ((part * dp_size, columns), low),
            ((part * dp_size, columns), low),
            (wide, low),
            (wide, low),
            ((total,) + small.shape[1:], jnp.float32),
            ((rows, LANES), jnp.float32),
            ((rows, columns), low),
            ((rows, columns), low),
            ((count, part, columns), low),
        ],
        "vhhvvvvhhv",
        gather_sems()
        + gather_sems()
        + block_sems()
        + block_sems()
        + [pltpu.SemaphoreType.DMA((total,)), pltpu.SemaphoreType.DMA((total,))]
        + pair_scratch(part, columns)
        + [
            pltpu.VMEM(wide, low),
            pltpu.VMEM((part * dp_size, columns), low),
            pltpu.VMEM((rows, columns), low),
            pltpu.VMEM((rows, columns), low),
            pltpu.SemaphoreType.DMA((3,)),
            pltpu.VMEM((part, columns), low),
            pltpu.VMEM((part, columns), low),
            pltpu.VMEM((rows, 1), jnp.float32),
        ],
        4 * rows * wide[1] * columns,
        "gathers_beside_hidden",
    )


def greet_and_wait():
    barrier, count = greet_line()
    pl.semaphore_wait(barrier, count)


def quarters(ref):
    width = ref.shape[1] // 4
    return [(ref, quarter * width) for quarter in range(4)]


def carrying(kernel, collective_id, operands, in_places, outs, out_places, scratch, flops, name):
    spaces = {"h": pl.BlockSpec(memory_space=pl.ANY), "v": pl.BlockSpec(memory_space=pltpu.VMEM)}
    return pl.pallas_call(
        kernel,
        in_specs=[spaces[place] for place in in_places],
        out_specs=[spaces[place] for place in out_places],
        out_shape=[jax.ShapeDtypeStruct(shape, dtype) for shape, dtype in outs],
        scratch_shapes=scratch,
        compiler_params=pltpu.CompilerParams(
            collective_id=collective_id, has_side_effects=True, vmem_limit_bytes=VMEM_LIMIT
        ),
        cost_estimate=pl.CostEstimate(flops=flops, bytes_accessed=1 << 25, transcendentals=0),
        name=name,
    )(*operands)


def third_kernel(
    head_cols,
    slots,
    piece,
    field_row,
    block_ref,
    ready_hbm,
    xn_hbm,
    gy_hbm,
    weight_hbm,
    spread_ref,
    ends_ref,
    ends_col_ref,
    full_ref,
    grad_out,
    or_out,
    sums_ref,
    owned_ref,
    vector_ref,
    gather_send,
    gather_recv,
    below,
    above,
    line_send,
    line_recv,
    parcel,
    pair_send,
    pair_recv,
    mask_ref,
    low_ref,
    go_ref,
    dq_acc,
    dk_acc,
    dv_acc,
    ready_ref,
    xn_ref,
    gy_ref,
    weight_ref,
    grad_ref,
    or_ref,
    local_sems,
    keep_ref,
    ahead_ref,
    behind_ref,
):
    loads = [
        pltpu.make_async_copy(source, target, local_sems.at[index])
        for index, (source, target) in enumerate(
            [(ready_hbm, ready_ref), (xn_hbm, xn_ref), (weight_hbm, weight_ref), (gy_hbm, gy_ref)]
        )
    ]
    for load in loads:
        load.start()
    weight = LineGather(block_ref, full_ref, gather_send, gather_recv)
    line = LineSum(ready_ref, below, above, line_send, line_recv)
    rights = [(grad_ref, kind * head_cols) for kind in range(3)] + [(or_ref, 0)]
    products = PairProducts(
        [xn_ref] * 3 + [gy_ref], rights, parcel, sums_ref, pair_send, pair_recv
    )
    greet_and_wait()
    weight.start()
    loads[0].wait()
    line.advance(1)

    rows = xn_ref.shape[0]
    tiles = rows // ROW_TILE
    scale = HEAD_DIM ** (-0.5)
    row_positions = lax.broadcasted_iota(jnp.int32, (1, rows), 1)
    seg_row, _, row_valid = segment_of(ends_col_ref[...], row_positions, 0, slots)
    seg_row = jnp.where(row_valid, seg_row, slots + row_positions)
    for tile in range(tiles):
        here = pl.ds(tile * ROW_TILE, ROW_TILE)
        reach = (tile + 1) * ROW_TILE
        shape = (ROW_TILE, reach)
        ids = lax.broadcasted_iota(jnp.int32, (ROW_TILE, 1), 0) + tile * ROW_TILE
        seg_col, starting, valid = segment_of(ends_ref[0:1, :], ids, 1, slots)
        seg_col = jnp.where(valid, seg_col, slots + ids)
        tables = rope_tables((ids - starting).astype(jnp.float32))
        for ref, table in zip((keep_ref, ahead_ref, behind_ref), tables):
            ref[here, :] = table
        key_ids = lax.broadcasted_iota(jnp.int32, shape, 1)
        allowed = (seg_col == seg_row[:, :reach]) & (key_ids <= ids)
        mask_ref[here, pl.ds(0, reach)] = jnp.where(allowed, 0.0, masked_score)
    biases = [
        jnp.concatenate(field_rows(spread_ref, field_row, kind, piece), axis=1) for kind in range(3)
    ]

    def turned(values, here, direction):
        ahead = pltpu.roll(values, LANES - ROT_DIM // 2, 1)
        behind = pltpu.roll(values, ROT_DIM // 2, 1)
        return values * keep_ref[here, :] + direction * (
            ahead * ahead_ref[here, :] + behind * behind_ref[here, :]
        )

    def project(here):
        for kind in range(3):
            columns = pl.ds(kind * head_cols, head_cols)
            values = contract(xn_ref[here, :], weight_ref[:, columns], 1, 0) + biases[kind]
            if kind == 2:
                low_ref[here, columns] = values.astype(jnp.bfloat16)
                continue
            for first in range(0, head_cols, LANES):
                part = turned(values[:, first : first + LANES], here, 1.0).astype(jnp.bfloat16)
                if kind == 0:
                    part = part * scale
                low_ref[here, pl.ds(kind * head_cols + first, LANES)] = part
        columns = pl.ds(3 * head_cols, head_cols)
        values = contract(gy_ref[here, :], weight_ref[:, columns], 1, 0)
        go_ref[here, :] = values.astype(jnp.bfloat16)

    for load in loads[1:]:
        load.wait()
    by_rows(rows, ROW_TILE, project)
    vector_ref[...] = jnp.zeros_like(vector_ref)

    lane = lax.broadcasted_iota(jnp.int32, (ROW_TILE, LANES), 1)
    first_head = lane < HEAD_DIM

    def one_pair(pair, carry):
        column = pl.multiple_of(pair * LANES, LANES)
        q_lanes = pl.ds(column, LANES)
        k_lanes = pl.ds(pl.multiple_of(head_cols + column, LANES), LANES)
        v_lanes = pl.ds(pl.multiple_of(2 * head_cols + column, LANES), LANES)
        dk_acc[...] = jnp.zeros_like(dk_acc)
        dv_acc[...] = jnp.zeros_like(dv_acc)
        for tile in range(tiles):
            here = pl.ds(tile * ROW_TILE, ROW_TILE)
            keys = pl.ds(0, (tile + 1) * ROW_TILE)
            outs = []
            query_grads = []
            for head in range(LANES // HEAD_DIM):
                mine = first_head if head == 0 else jnp.logical_not(first_head)
                none = jnp.zeros((ROW_TILE, LANES), jnp.bfloat16)
                query = jnp.where(mine, low_ref[here, q_lanes], none)
                grad_out = jnp.where(mine, go_ref[here, q_lanes], none)
                scores = contract(query, low_ref[keys, k_lanes], 1, 1) + mask_ref[here, keys]
                peak = jnp.max(scores, axis=1, keepdims=True)
                weights = jnp.exp(scores - peak)
                share = 1.0 / jnp.sum(weights, axis=1, keepdims=True)
                probs = weights * share
                probs_low = probs.astype(jnp.bfloat16)
                outs.append(contract(probs_low, low_ref[keys, v_lanes], 1, 0))
                grad_probs = contract(grad_out, low_ref[keys, v_lanes], 1, 1)
                delta = jnp.sum(probs * grad_probs, axis=1, keepdims=True)
                grad_scores = (probs * (grad_probs - delta)).astype(jnp.bfloat16)
                query_grads.append(contract(grad_scores, low_ref[keys, k_lanes], 1, 0))
                dk_acc[keys, :] += contract(grad_scores, query, 0, 0)
                dv_acc[keys, :] += contract(probs_low, grad_out, 0, 0)
            or_ref[here, q_lanes] = jnp.where(first_head, outs[0], outs[1]).astype(jnp.bfloat16)
            dq_acc[here, :] = jnp.where(first_head, query_grads[0], query_grads[1])
        for tile in range(tiles):
            here = pl.ds(tile * ROW_TILE, ROW_TILE)
            parts = [
                (q_lanes, turned(dq_acc[here, :], here, -1.0) * scale),
                (k_lanes, turned(dk_acc[here, :], here, -1.0)),
                (v_lanes, dv_acc[here, :]),
            ]
            for lanes, part in parts:
                part = part.astype(jnp.bfloat16)
                grad_ref[here, lanes] = part
                vector_ref[0:1, lanes] += jnp.sum(part.astype(jnp.float32), axis=0, keepdims=True)

        @pl.when(pair == 0)
        def _():
            weight.advance(1)
            line.advance(2)

        @pl.when(pair == 1)
        def _():
            weight.advance(2, 0, 1)
            line.advance(3, 0, 1)

        return carry

    lax.fori_loop(0, head_cols // LANES, one_pair, 0)
    stores = [
        pltpu.make_async_copy(grad_ref, grad_out, local_sems.at[4]),
        pltpu.make_async_copy(or_ref, or_out, local_sems.at[5]),
    ]
    for store in stores:
        store.start()
    weight.advance(2, 1)
    line.advance(3, 1)
    products.far()
    weight.advance(3, 0, 1)
    products.near()
    weight.advance(3, 1)
    for step in range(4, weight.count):
        weight.advance(step)
        line.advance(step)
    line.finish(owned_ref)
    weight.finish()
    for store in stores:
        store.wait()


def third_step(
    block, ready, normed, grad_rows, full_qkvo, spread, ends, ends_col, slots, piece, field_row
):
    rows, width = normed.shape
    count = lax.axis_size("dp") // 2
    columns = full_qkvo.shape[1]
    head_cols = columns // 4
    part = width // (2 * count)
    low = jnp.bfloat16
    return carrying(
        functools.partial(third_kernel, head_cols, slots, piece, field_row),
        5,
        (
            block,
            ready,
            normed,
            grad_rows,
            full_qkvo,
            spread,
            ends,
            ends_col,
        ),
        "hhhhhvvv",
        [
            ((width, block.shape[1]), low),
            ((rows, 3 * head_cols), low),
            ((rows, head_cols), low),
            ((count, part, columns), low),
            ((part, ready.shape[2]), jnp.float32),
            ((8, columns), jnp.float32),
        ],
        "hhhvvv",
        gather_sems()
        + sum_scratch(part, ready.shape[2])
        + pair_scratch(part, columns)
        + [
            pltpu.VMEM((rows, rows), jnp.float32),
            pltpu.VMEM((rows, 3 * head_cols), low),
            pltpu.VMEM((rows, head_cols), low),
            pltpu.VMEM((rows, LANES), jnp.float32),
            pltpu.VMEM((rows, LANES), jnp.float32),
            pltpu.VMEM((rows, LANES), jnp.float32),
            pltpu.VMEM(ready.shape, low),
            pltpu.VMEM((rows, width), low),
            pltpu.VMEM((rows, width), low),
            pltpu.VMEM((width, columns), low),
            pltpu.VMEM((rows, 3 * head_cols), low),
            pltpu.VMEM((rows, head_cols), low),
            pltpu.SemaphoreType.DMA((6,)),
            pltpu.VMEM((rows, LANES), jnp.float32),
            pltpu.VMEM((rows, LANES), jnp.float32),
            pltpu.VMEM((rows, LANES), jnp.float32),
        ],
        4 * rows * width * columns + 12 * rows * rows * head_cols,
        "lines_beside_attention",
    )


def fourth_kernel(
    head_cols,
    piece,
    field_row,
    ready_hbm,
    xn_hbm,
    gy_hbm,
    down_hbm,
    slope_hbm,
    act_hbm,
    or_hbm,
    qkvo_hbm,
    x_ref,
    spread_ref,
    gh_out,
    sums_ref,
    owned_ref,
    vector_ref,
    out_ref,
    below,
    above,
    line_send,
    line_recv,
    parcel,
    pair_send,
    pair_recv,
    t_parts,
    t_got,
    t_send,
    t_recv,
    ready_ref,
    xn_ref,
    gy_ref,
    down_ref,
    wide_ref,
    or_ref,
    weight_ref,
    gh_ref,
    local_sems,
):
    loads = [
        pltpu.make_async_copy(source, target, local_sems.at[index])
        for index, (source, target) in enumerate(
            [
                (ready_hbm, ready_ref),
                (gy_hbm, gy_ref),
                (down_hbm, down_ref),
                (slope_hbm, wide_ref),
                (xn_hbm, xn_ref),
                (or_hbm, or_ref),
                (qkvo_hbm.at[:, pl.ds(3 * head_cols, head_cols)], weight_ref),
            ]
        )
    ]
    for load in loads:
        load.start()
    line = LineSum(ready_ref, below, above, line_send, line_recv)
    branches = BlockScatter(t_parts, t_got, t_send, t_recv)
    products = PairProducts(
        [xn_ref] * 4, quarters(gh_ref), parcel, sums_ref, pair_send, pair_recv
    )
    barrier, count = greet_line()
    count += greet_block()
    pl.semaphore_wait(barrier, count)
    loads[0].wait()
    line.advance(1)
    for load in loads[1:4]:
        load.wait()
    rows, share_width = x_ref.shape
    width = down_ref.shape[1] // 4
    vector_ref[...] = jnp.zeros_like(vector_ref)

    def tile(here):
        for quarter in range(4):
            columns = pl.ds(quarter * width, width)
            grad_act = contract(gy_ref[here, :], down_ref[:, columns], 1, 0)
            grad_hidden = grad_act * wide_ref[here, columns].astype(jnp.float32)
            grad_hidden = grad_hidden.astype(jnp.bfloat16)
            gh_ref[here, columns] = grad_hidden
            vector_ref[0:1, columns] += jnp.sum(
                grad_hidden.astype(jnp.float32), axis=0, keepdims=True
            )

    by_rows(rows, ROW_TILE, tile)
    late = pltpu.make_async_copy(act_hbm, wide_ref, local_sems.at[7])
    late.start()
    store = pltpu.make_async_copy(gh_ref, gh_out, local_sems.at[8])
    store.start()
    for load in loads[4:]:
        load.wait()
    line.advance(2, 0, 1)
    late.wait()

    def branch(share):
        start = pl.multiple_of(branches.owner(share) * share_width, share_width)
        where = pl.ds(start, share_width)

        def once(here):
            part = contract(or_ref[here, :], weight_ref[where, :], 1, 1)
            part = part + contract(wide_ref[here, :], down_ref[where, :], 1, 1)
            t_parts[share, here, :] = part.astype(jnp.bfloat16)

        by_rows(rows, ROW_TILE, once)
        branches.after(share)

    shares = branches.size
    for share in range(shares - 1):
        branch(share)
    line.advance(2, 1)
    branches.second()
    products.far()
    line.advance(3, 0, 1)
    products.near()
    line.advance(3, 1)
    for step in range(4, line.count):
        line.advance(step)
    branch(shares - 1)
    branches.finish()
    biases = [
        jnp.concatenate(field_rows(spread_ref, field_row, kind, piece), axis=1) for kind in (3, 4)
    ]
    for tile_index in range(rows // ROW_TILE):
        here = pl.ds(tile_index * ROW_TILE, ROW_TILE)
        total = x_ref[here, :].astype(jnp.float32) + branches.total(tile_index, ROW_TILE)
        total = total + biases[0] + biases[1]
        out_ref[here, :] = total.astype(jnp.bfloat16)
    line.finish(owned_ref)
    store.wait()


def fourth_step(
    ready,
    normed,
    grad_rows,
    turned_down,
    slope,
    activated,
    attended,
    full_qkvo,
    tokens,
    spread,
    piece,
    field_row,
):
    rows, width = normed.shape
    head_cols = attended.shape[1]
    count, part, columns = ready.shape
    low = jnp.bfloat16
    return carrying(
        functools.partial(fourth_kernel, head_cols, piece, field_row),
        6,
        (
            ready,
            normed,
            grad_rows,
            turned_down,
            slope,
            activated,
            attended,
            full_qkvo,
            tokens,
            spread,
        ),
        "hhhhhhhhvv",
        [
            ((rows, columns), low),
            ((count, part, columns), low),
            ((part, columns), jnp.float32),
            ((8, columns), jnp.float32),
            (tokens.shape, low),
        ],
        "hvvvv",
        sum_scratch(part, columns)
        + pair_scratch(part, columns)
        + scatter_scratch(rows, tokens.shape[1])
        + [
            pltpu.VMEM(ready.shape, low),
            pltpu.VMEM((rows, width), low),
            pltpu.VMEM((rows, width), low),
            pltpu.VMEM((width, columns), low),
            pltpu.VMEM((rows, columns), low),
            pltpu.VMEM((rows, head_cols), low),
            pltpu.VMEM((width, head_cols), low),
            pltpu.VMEM((rows, columns), low),
            pltpu.SemaphoreType.DMA((9,)),
        ],
        6 * rows * width * columns,
        "line_beside_hidden_grad",
    )


def greet_block():
    size = lax.axis_size("mp")
    place = lax.axis_index("mp")
    barrier = pltpu.get_barrier_semaphore()
    for step in range(1, size):
        peer = lax.rem(place + step, size)
        pl.semaphore_signal(barrier, inc=1, device_id={"mp": peer}, device_id_type=MESH_ID)
    return size - 1


class BlockScatter:
    def __init__(self, parts, got, send, recv):
        self.size = lax.axis_size("mp")
        self.place = lax.axis_index("mp")
        self.parts, self.got, self.send, self.recv = parts, got, send, recv
        self.half = parts.shape[1] // 2
        self.beside = self.place + 1 - 2 * lax.rem(self.place, 2)
        self.above = lax.rem(self.place + 2, 4)

    def owner(self, index):
        if self.size == 4:
            return [lax.rem(self.beside + 2, 4), self.beside, self.above, self.place][index]
        return lax.rem(self.place + 1 + index, self.size)

    def copy(self, index):
        if self.size == 4:
            part, bottom, peer = [
                (0, 0, self.beside),
                (0, 1, self.above),
                (1, 0, self.beside),
                (2, 1, self.above),
                (2, 0, self.above),
                (1, 1, self.beside),
            ][index]
            source = self.parts.at[part, pl.ds(bottom * self.half, self.half), :]
        else:
            source = self.parts.at[index]
            peer = self.owner(index)
        sems = (self.send.at[index], self.recv.at[index])
        return remote(source, self.got.at[index], *sems, "mp", peer)

    def after(self, index):
        if self.size != 4:
            if index < self.size - 1:
                self.copy(index).start()
            return
        for number in ((0, 1), (2,), (3,), ())[index]:
            self.copy(number).start()

    def second(self):
        if self.size != 4:
            return
        for number, part, bottom in ((0, 2, 0), (1, 1, 1)):
            self.copy(number).wait_recv()

            def body(rows, number=number, part=part, bottom=bottom):
                here = pl.ds(bottom * self.half + rows.start, rows.size)
                total = summed(self.parts[part, here, :], self.got[number, rows, :])
                self.parts[part, here, :] = total.astype(jnp.bfloat16)

            by_rows(self.half, 64, body)
            self.copy(number + 4).start()

    def finish(self):
        if self.size != 4:
            for index in range(self.size - 1):
                self.copy(index).wait()
            return
        for index in range(6):
            if index > 1:
                self.copy(index).wait_recv()
            self.copy(index).wait_send()

    def total(self, tile, rows):
        here = pl.ds(tile * rows, rows)
        own = self.parts[self.size - 1, here, :]
        if self.size != 4:
            return summed(own, *[self.got[index, here, :] for index in range(self.size - 1)])
        bottom = (tile * rows) // self.half
        there = pl.ds(tile * rows - bottom * self.half, rows)
        return summed(own, self.got[2 + bottom, there, :], self.got[4 + bottom, there, :])


def scatter_scratch(rows, width):
    size = lax.axis_size("mp")
    slots = (6, rows // 2, width) if size == 4 else (size - 1, rows, width)
    return [
        pltpu.VMEM((size, rows, width), jnp.bfloat16),
        pltpu.VMEM(slots, jnp.bfloat16),
        pltpu.SemaphoreType.DMA((slots[0],)),
        pltpu.SemaphoreType.DMA((slots[0],)),
    ]


STREAM = 256
SLOTS = 3


def stream(tiles, loads, stores, compute, primed=False):
    ahead = SLOTS - 1
    if not primed:
        prime(tiles, loads)

    def once(tile, carry):
        slot = lax.rem(tile, SLOTS)

        @pl.when(tile + ahead < tiles)
        def _():
            for copy in loads(tile + ahead, lax.rem(tile + ahead, SLOTS)):
                copy.start()

        for copy in loads(tile, slot):
            copy.wait()

        @pl.when(tile >= SLOTS)
        def _():
            for copy in stores(tile - SLOTS, slot):
                copy.wait()

        compute(tile, slot)
        for copy in stores(tile, slot):
            copy.start()
        return carry

    lax.fori_loop(0, tiles, once, 0)
    for tile in range(max(tiles - SLOTS, 0), tiles):
        for copy in stores(tile, tile % SLOTS):
            copy.wait()


def prime(tiles, loads):
    for tile in range(min(SLOTS - 1, tiles)):
        for copy in loads(tile, tile):
            copy.start()


def fetch(pairs, sems):
    copies = [
        pltpu.make_async_copy(source, target, sems.at[index])
        for index, (source, target) in enumerate(pairs)
    ]
    for copy in copies:
        copy.start()
    return copies


def step_tall(grad, root_left, root_right, master, master_out):
    depth, size = grad.shape
    tile_rows = min(STREAM, size)

    def scope(root_in, side_in, side_new, sems):
        root = root_right[1, 0, 0].astype(jnp.bfloat16)

        def where(tile):
            return pl.ds(pl.multiple_of(tile * tile_rows, tile_rows), tile_rows)

        def loads(tile, slot):
            here = where(tile)
            source = root_left.at[1, 0, 0, here, :]
            return [
                pltpu.make_async_copy(source, root_in.at[slot], sems.at[0, slot]),
                pltpu.make_async_copy(master.at[here, :], side_in.at[slot], sems.at[1, slot]),
            ]

        def stores(tile, slot):
            target = master_out.at[where(tile), :]
            return [pltpu.make_async_copy(side_new.at[slot], target, sems.at[2, slot])]

        def compute(tile, slot):
            first = contract(root_in[slot].astype(jnp.bfloat16), grad[...], 1, 1)
            step = contract(first.astype(jnp.bfloat16), root, 1, 0)
            side_new[slot] = side_in[slot] - matrix_rate * step

        stream(size // tile_rows, loads, stores, compute)

    pl.run_scoped(
        scope,
        pltpu.VMEM((SLOTS, tile_rows, size), jnp.float32),
        pltpu.VMEM((SLOTS, tile_rows, depth), jnp.float32),
        pltpu.VMEM((SLOTS, tile_rows, depth), jnp.float32),
        pltpu.SemaphoreType.DMA((3, SLOTS)),
    )


def step_wide(grad, root_left, root_right, master, master_out):
    depth, size = grad.shape
    tile_rows = min(STREAM, size)
    plane = master.shape[2]

    def scope(root_in, low, sems):
        first = contract(root_left[1, 0, 0].astype(jnp.bfloat16), grad[...], 1, 0)
        low[...] = first.astype(jnp.bfloat16)

        def where(tile):
            return pl.ds(pl.multiple_of(tile * tile_rows, tile_rows), tile_rows)

        def loads(tile, slot):
            source = root_right.at[1, 0, 0, :, where(tile)]
            return [pltpu.make_async_copy(source, root_in.at[slot], sems.at[slot])]

        def compute(tile, slot):
            step = contract(low[...], root_in[slot].astype(jnp.bfloat16), 1, 0)
            start = tile * tile_rows
            here = pl.ds(pl.multiple_of(lax.rem(start, plane), tile_rows), tile_rows)
            kind = start // plane
            master_out[kind, :, here] = master[kind, :, here] - matrix_rate * step

        stream(size // tile_rows, loads, lambda tile, slot: [], compute)

    pl.run_scoped(
        scope,
        pltpu.VMEM((SLOTS, size, tile_rows), jnp.float32),
        pltpu.VMEM((depth, size), jnp.bfloat16),
        pltpu.SemaphoreType.DMA((SLOTS,)),
    )


def fifth_kernel(
    head_cols,
    piece,
    ready_hbm,
    gh_hbm,
    grad_hbm,
    qkvo_ref,
    up_ref,
    x_hbm,
    gy_hbm,
    stats_hbm,
    spread_ref,
    vector_three,
    vector_four,
    down_hbm,
    owned_hbm,
    down_left,
    down_right,
    w_down,
    qkv_left,
    qkv_right,
    w_qkv_hbm,
    out_left,
    out_right,
    w_out,
    dx_out,
    up_send,
    down_send,
    own_ref,
    sums_ref,
    w_down_new,
    w_qkv_out,
    w_out_new,
    below,
    above,
    line_send,
    line_recv,
    g_parts,
    g_got,
    g_send,
    g_recv,
    terms_ref,
    terms_got,
    terms_send,
    terms_recv,
    vector_ref,
    vector_got,
    vector_send,
    vector_recv,
    ready_ref,
    gh_ref,
    grad_ref,
    low_down,
    low_qkv,
    low_out,
    x_ref,
    gy_ref,
    stats_ref,
    owned_down,
    owned_qkvo,
    w_qkv,
    w_qkv_new,
    dx_ref,
    load_sems,
):
    loads = fetch(
        [
            (ready_hbm, ready_ref),
            (grad_hbm, grad_ref),
            (gh_hbm, gh_ref),
            (owned_hbm, owned_qkvo),
            (down_hbm, owned_down),
            (w_qkv_hbm, w_qkv),
            (x_hbm, x_ref),
            (gy_hbm, gy_ref),
            (stats_hbm, stats_ref),
        ],
        load_sems,
    )
    line = LineSum(ready_ref, below, above, line_send, line_recv)
    from_norm = BlockScatter(g_parts, g_got, g_send, g_recv)
    mp_size = from_norm.size
    mp_place = from_norm.place
    dp_size = lax.axis_size("dp")
    dp_place = lax.axis_index("dp")
    rows, width = x_ref.shape
    model_width = width * mp_size
    tiles = rows // ROW_TILE
    barrier = pltpu.get_barrier_semaphore()

    def greet(step, carry):
        peer = lax.rem(dp_place + step, dp_size)
        pl.semaphore_signal(barrier, inc=1, device_id={"dp": peer}, device_id_type=MESH_ID)
        return carry

    lax.fori_loop(1, dp_size, greet, 0)
    pl.semaphore_wait(barrier, dp_size - 1 + greet_block())
    loads[0].wait()
    line.advance(1)
    for load in loads[1:3]:
        load.wait()

    def parts(one_ref, two_ref, sems):
        def load(share):
            start = pl.multiple_of(from_norm.owner(share) * width, width)
            slot = share % 2
            where = pl.ds(start, width)
            narrow = pl.ds(0, 3 * head_cols)
            return [
                pltpu.make_async_copy(qkvo_ref.at[where, narrow], one_ref.at[slot], sems.at[0, slot]),
                pltpu.make_async_copy(up_ref.at[where, :], two_ref.at[slot], sems.at[1, slot]),
            ]

        for copy in load(0):
            copy.start()
        for share in range(mp_size):
            slot = share % 2
            for copy in load(share):
                copy.wait()
            if share + 1 < mp_size:
                for copy in load(share + 1):
                    copy.start()

            def tile(here, share=share, slot=slot):
                part = contract(grad_ref[here, :], one_ref[slot], 1, 1)
                part = part + contract(gh_ref[here, :], two_ref[slot], 1, 1)
                g_parts[share, here, :] = part.astype(jnp.bfloat16)

            by_rows(rows, ROW_TILE, tile)
            from_norm.after(share)

    columns = up_ref.shape[1]
    pl.run_scoped(
        parts,
        pltpu.VMEM((2, width, 3 * head_cols), jnp.bfloat16),
        pltpu.VMEM((2, width, columns), jnp.bfloat16),
        pltpu.SemaphoreType.DMA((2, 2)),
    )
    for step in range(2, line.count - 1):
        line.advance(step)
    from_norm.second()
    for load in loads[3:]:
        load.wait()
    low_down[...] = owned_down[...].astype(jnp.bfloat16)
    low_qkv[...] = owned_qkvo[:, pl.ds(0, 3 * head_cols)].astype(jnp.bfloat16)
    low_out[...] = owned_qkvo[:, pl.ds(3 * head_cols, head_cols)].astype(jnp.bfloat16)
    step_tall(low_out, out_left, out_right, w_out, w_out_new)
    from_norm.finish()

    def lane_pair(first, second):
        lane = lax.broadcasted_iota(jnp.int32, (ROW_TILE, LANES), 1)
        return jnp.where(lane == 0, first, jnp.where(lane == 1, second, 0.0))

    owners = [mp_place * dp_size + owner for owner in range(dp_size)]
    gain = jnp.concatenate(vector_rows(spread_ref, owners, 0, piece), axis=1)
    sums = [jnp.zeros((1, width), jnp.float32) for _ in range(3)]
    for tile in range(tiles):
        here = pl.ds(tile * ROW_TILE, ROW_TILE)
        normalized = (x_ref[here, :].astype(jnp.float32) - stats_ref[here, 0:1]) * stats_ref[here, 1:2]
        grad = from_norm.total(tile, ROW_TILE)
        gained = grad * gain
        terms = lane_pair(
            jnp.sum(gained, axis=1, keepdims=True),
            jnp.sum(gained * normalized, axis=1, keepdims=True),
        )
        terms_ref[:, here] = jnp.transpose(terms)[:8, :]
        upstream = gy_ref[here, :].astype(jnp.float32) * stats_ref[here, 2:3]
        sums[0] += jnp.sum(grad * normalized, axis=0, keepdims=True)
        sums[1] += jnp.sum(grad, axis=0, keepdims=True)
        sums[2] += jnp.sum(upstream, axis=0, keepdims=True)

    vector_ref[...] = jnp.zeros_like(vector_ref)
    vector_ref[0:1, :] = vector_three[0:1, :]
    vector_ref[1:2, :] = vector_four[0:1, :]
    for index in range(3):
        vector_ref[2 + index : 3 + index, pl.ds(0, width)] = sums[index]

    def terms_copy(step):
        peer = lax.rem(mp_place + step, mp_size)
        slot = step - 1
        sems = (terms_send.at[slot], terms_recv.at[slot])
        return remote(terms_ref, terms_got.at[slot], *sems, "mp", peer)

    def vector_copy(step):
        peer = lax.rem(dp_place + step, dp_size)
        slot = step - 1
        sems = (vector_send.at[slot], vector_recv.at[slot])
        return remote(vector_ref, vector_got.at[slot], *sems, "dp", peer)

    def vector_begin(step, carry):
        vector_copy(step).start()
        return carry

    for step in range(1, mp_size):
        terms_copy(step).start()
    lax.fori_loop(1, dp_size, vector_begin, 0)
    step_wide(low_qkv, qkv_left, qkv_right, w_qkv, w_qkv_new)
    stores = [pltpu.make_async_copy(w_qkv_new, w_qkv_out, load_sems.at[len(loads)])]
    stores[0].start()
    for step in range(1, mp_size):
        terms_copy(step).wait()
    for tile in range(tiles):
        here = pl.ds(tile * ROW_TILE, ROW_TILE)
        terms = terms_ref[:, here]
        for slot in range(mp_size - 1):
            terms = terms + terms_got[slot, :, here]
        wide = jnp.concatenate([terms, jnp.zeros((LANES - 8, ROW_TILE), jnp.float32)], axis=0)
        terms = jnp.transpose(wide) * (1.0 / model_width)
        inv_std = stats_ref[here, 1:2]
        normalized = (x_ref[here, :].astype(jnp.float32) - stats_ref[here, 0:1]) * inv_std
        gained = from_norm.total(tile, ROW_TILE) * gain
        upstream = gy_ref[here, :].astype(jnp.float32) * stats_ref[here, 2:3]
        dx_ref[here, :] = upstream + inv_std * (gained - terms[:, 0:1] - normalized * terms[:, 1:2])
    stores.append(pltpu.make_async_copy(dx_ref, dx_out, load_sems.at[len(loads) + 1]))
    stores[1].start()
    step_tall(low_down, down_left, down_right, w_down, w_down_new)

    def vector_end(step, carry):
        vector_copy(step).wait()
        return carry

    lax.fori_loop(1, dp_size, vector_end, 0)
    total = vector_ref[...]
    for slot in range(dp_size - 1):
        total = total + vector_got[slot]
    sums_ref[...] = total
    by_rows(own_ref.shape[0], 32, lambda here: keep_block(ready_ref, line.spot, own_ref, here))
    line.hand_out(up_send, down_send)
    for store in stores:
        store.wait()


def keep_block(blocks, index, out, here):
    out[here, :] = blocks[index, here, :]


def fifth_step(
    ready,
    grad_hidden,
    grad_projected,
    full_qkvo,
    full_up,
    tokens,
    cotangent,
    stats,
    spread,
    vector_three,
    vector_four,
    owned_down,
    owned_qkvo,
    down,
    qkv,
    out,
    piece,
):
    rows, width = tokens.shape
    head_cols = grad_projected.shape[1] // 3
    count, part, columns = ready.shape
    mp_size = lax.axis_size("mp")
    dp_size = lax.axis_size("dp")
    low = jnp.bfloat16
    exact = jnp.float32
    return carrying(
        functools.partial(fifth_kernel, head_cols, piece),
        7,
        (
            ready,
            grad_hidden,
            grad_projected,
            full_qkvo,
            full_up,
            tokens,
            cotangent,
            stats,
            spread,
            vector_three,
            vector_four,
            owned_down,
            owned_qkvo,
        )
        + down
        + qkv
        + out,
        "hhhhhhhhvvvhh" + "hvh" + "vhh" + "hvh",
        [
            ((rows, width), exact),
            ((part, columns), low),
            ((part, columns), low),
            ((part, columns), low),
            ((8, columns), exact),
            (down[2].shape, exact),
            (qkv[2].shape, exact),
            (out[2].shape, exact),
        ],
        "hvvvvhhh",
        sum_scratch(part, columns)
        + scatter_scratch(rows, width)
        + [
            pltpu.VMEM((8, rows), exact),
            pltpu.VMEM((mp_size - 1, 8, rows), exact),
            pltpu.SemaphoreType.DMA((mp_size - 1,)),
            pltpu.SemaphoreType.DMA((mp_size - 1,)),
            pltpu.VMEM((8, columns), exact),
            pltpu.VMEM((dp_size - 1, 8, columns), exact),
            pltpu.SemaphoreType.DMA((dp_size - 1,)),
            pltpu.SemaphoreType.DMA((dp_size - 1,)),
            pltpu.VMEM(ready.shape, low),
            pltpu.VMEM((rows, columns), low),
            pltpu.VMEM((rows, 3 * head_cols), low),
            pltpu.VMEM((part, columns), low),
            pltpu.VMEM((part, 3 * head_cols), low),
            pltpu.VMEM((part, head_cols), low),
            pltpu.VMEM((rows, width), low),
            pltpu.VMEM((rows, width), low),
            pltpu.VMEM(stats.shape, exact),
            pltpu.VMEM((part, columns), exact),
            pltpu.VMEM((part, columns), exact),
            pltpu.VMEM(qkv[2].shape, exact),
            pltpu.VMEM(qkv[2].shape, exact),
            pltpu.VMEM((rows, width), exact),
            pltpu.SemaphoreType.DMA((11,)),
        ],
        4 * rows * width * mp_size * columns,
        "line_beside_norm_grad",
    )


class Averager:
    def __init__(self, grad, stats, stats_out, buffers, sems):
        self.grad, self.stats, self.stats_out = grad, stats, stats_out
        self.stat_in, self.stat_new = buffers
        self.sems = sems
        self.tile_rows = self.stat_in.shape[1]
        self.tiles = grad.shape[1] // self.tile_rows

    def where(self, tile):
        return pl.ds(pl.multiple_of(tile * self.tile_rows, self.tile_rows), self.tile_rows)

    def loads(self, tile, slot):
        source = self.stats.at[0, 0, 0, self.where(tile), :]
        return [pltpu.make_async_copy(source, self.stat_in.at[slot], self.sems.at[0, slot])]

    def stores(self, tile, slot):
        target = self.stats_out.at[0, 0, self.where(tile), :]
        return [pltpu.make_async_copy(self.stat_new.at[slot], target, self.sems.at[1, slot])]

    def compute(self, tile, slot):
        product = contract(self.grad[:, self.where(tile)], self.grad[...], 0, 0)
        self.stat_new[slot] = 0.5 * self.stat_in[slot] + 0.5 * product

    def run(self):
        stream(self.tiles, self.loads, self.stores, self.compute, True)


class Updater(Averager):
    def __init__(self, grad, stats, stats_out, buffers, sems, first, master, master_out, more):
        super().__init__(grad, stats, stats_out, buffers, sems)
        self.first, self.master, self.master_out = first, master, master_out
        self.root_in, self.side_in, self.side_new = more

    def loads(self, tile, slot):
        here = self.where(tile)
        source = self.stats.at[1, 0, 0, :, here]
        return super().loads(tile, slot) + [
            pltpu.make_async_copy(source, self.root_in.at[slot], self.sems.at[2, slot]),
            pltpu.make_async_copy(
                self.master.at[:, here], self.side_in.at[slot], self.sems.at[3, slot]
            ),
        ]

    def stores(self, tile, slot):
        target = self.master_out.at[:, self.where(tile)]
        return super().stores(tile, slot) + [
            pltpu.make_async_copy(self.side_new.at[slot], target, self.sems.at[4, slot])
        ]

    def compute(self, tile, slot):
        super().compute(tile, slot)
        step = contract(self.first[...], self.root_in[slot].astype(jnp.bfloat16), 1, 0)
        self.side_new[slot] = self.side_in[slot] - matrix_rate * step


def average_small(small, small_new, grad):
    small_new[0, 0] = 0.5 * small[0, 0, 0] + 0.5 * contract(grad[...], grad[...], 1, 1)


def statistics_kernel(
    passed,
    owned_down,
    owned_qkvo,
    down_left,
    down_right,
    qkv_left,
    qkv_right,
    out_left,
    out_right,
    *refs,
):
    sources, refs = (refs[:passed], refs[passed:])
    targets, refs = (refs[:passed], refs[passed:])
    held, refs = (refs[:passed], refs[passed:])
    (
        down_left_new,
        down_right_new,
        qkv_left_new,
        qkv_right_new,
        out_left_new,
        out_right_new,
        low_down,
        low_qkv,
        low_out,
        down_in,
        down_new,
        qkv_in,
        qkv_new,
        out_in,
        out_new,
        sems,
        pass_sems,
    ) = refs
    units = [
        Averager(low_down, down_left, down_left_new, (down_in, down_new), sems.at[0]),
        Averager(low_qkv, qkv_right, qkv_right_new, (qkv_in, qkv_new), sems.at[1]),
        Averager(low_out, out_left, out_left_new, (out_in, out_new), sems.at[2]),
    ]
    for unit in units:
        prime(unit.tiles, unit.loads)
    into = fetch(zip(sources, held), pass_sems.at[0])
    edge = low_qkv.shape[1]
    low_down[...] = owned_down[...].astype(jnp.bfloat16)
    low_qkv[...] = owned_qkvo[:, pl.ds(0, edge)].astype(jnp.bfloat16)
    low_out[...] = owned_qkvo[:, pl.ds(edge, low_out.shape[1])].astype(jnp.bfloat16)
    average_small(down_right, down_right_new, low_down)
    average_small(qkv_left, qkv_left_new, low_qkv)
    average_small(out_right, out_right_new, low_out)
    for copy in into:
        copy.wait()
    onward = fetch(zip(held, targets), pass_sems.at[1])
    for unit in units:
        unit.run()
    for copy in onward:
        copy.wait()


def statistics_step(owned, stats, passed):
    exact = jnp.float32
    low = jnp.bfloat16
    spaces = {"h": pl.BlockSpec(memory_space=pl.ANY), "v": pl.BlockSpec(memory_space=pltpu.VMEM)}
    depth = owned[0].shape[0]
    sizes = [stats[0].shape[-1], stats[3].shape[-1], stats[4].shape[-1]]
    shapes = [jax.ShapeDtypeStruct(array.shape, array.dtype) for array in passed]
    scratch = [pltpu.VMEM(array.shape, array.dtype) for array in passed]
    shapes += [jax.ShapeDtypeStruct(array.shape[1:], exact) for array in stats]
    averages = [pltpu.VMEM((depth, size), low) for size in sizes]
    for size in sizes:
        averages += [pltpu.VMEM((SLOTS, min(STREAM, size), size), exact) for _ in range(2)]
    averages += [
        pltpu.SemaphoreType.DMA((3, 2, SLOTS)),
        pltpu.SemaphoreType.DMA((2, len(passed))),
    ]
    count = len(passed)

    def kernel(*refs):
        inputs, rest = (refs[: 8 + count], refs[8 + count :])
        targets, rest = (rest[:count], rest[count:])
        stats_new, rest = (rest[:6], rest[6:])
        statistics_kernel(count, *inputs, *targets, *rest[:count], *stats_new, *rest[count:])

    return pl.pallas_call(
        kernel,
        in_specs=[spaces[place] for place in "vv" + "hvvhhv" + "h" * count],
        out_specs=[spaces[place] for place in "h" * count + "hvvhhv"],
        out_shape=shapes,
        scratch_shapes=scratch + averages,
        compiler_params=pltpu.CompilerParams(vmem_limit_bytes=VMEM_LIMIT),
        cost_estimate=pl.CostEstimate(
            flops=1 << 33, bytes_accessed=sum(array.size * 4 for array in stats), transcendentals=0
        ),
        name="statistics",
    )(*owned, *stats, *passed)


def last_kernel(
    own_ref,
    rising_ref,
    falling_ref,
    up_left,
    up_right,
    w_up,
    up_left_new,
    up_right_new,
    w_up_new,
    low_up,
    first,
    up_in,
    up_new,
    root_in,
    side_in,
    side_new,
    sems,
):
    unit = Updater(
        low_up,
        up_right,
        up_right_new,
        (up_in, up_new),
        sems,
        first,
        w_up,
        w_up_new,
        (root_in, side_in, side_new),
    )
    prime(unit.tiles, unit.loads)
    low_up[...] = summed(own_ref[...], rising_ref[...], falling_ref[...]).astype(jnp.bfloat16)
    root = up_left[1, 0, 0].astype(jnp.bfloat16)
    first[...] = contract(root, low_up[...], 1, 0).astype(jnp.bfloat16)
    average_small(up_left, up_left_new, low_up)
    unit.run()


def last_step(blocks, up_left, up_right, w_up):
    exact = jnp.float32
    low = jnp.bfloat16
    spaces = {"h": pl.BlockSpec(memory_space=pl.ANY), "v": pl.BlockSpec(memory_space=pltpu.VMEM)}
    depth, columns = w_up.shape
    tile_rows = min(STREAM, columns)
    return pl.pallas_call(
        last_kernel,
        in_specs=[spaces[place] for place in "vvvvhh"],
        out_specs=[spaces[place] for place in "vhh"],
        out_shape=[
            jax.ShapeDtypeStruct(up_left.shape[1:], exact),
            jax.ShapeDtypeStruct(up_right.shape[1:], exact),
            jax.ShapeDtypeStruct(w_up.shape, exact),
        ],
        scratch_shapes=[
            pltpu.VMEM((depth, columns), low),
            pltpu.VMEM((depth, columns), low),
            pltpu.VMEM((SLOTS, tile_rows, columns), exact),
            pltpu.VMEM((SLOTS, tile_rows, columns), exact),
            pltpu.VMEM((SLOTS, columns, tile_rows), exact),
            pltpu.VMEM((SLOTS, depth, tile_rows), exact),
            pltpu.VMEM((SLOTS, depth, tile_rows), exact),
            pltpu.SemaphoreType.DMA((5, SLOTS)),
        ],
        compiler_params=pltpu.CompilerParams(vmem_limit_bytes=VMEM_LIMIT),
        cost_estimate=pl.CostEstimate(
            flops=1 << 33, bytes_accessed=12 * columns * columns, transcendentals=0
        ),
        name="last_weight",
    )(*blocks, up_left, up_right, w_up)


def vector_update(state, grad):
    stat_new = 0.5 * state[1] + 0.5 * grad * grad
    param_new = state[0] - vector_rate * grad * lax.rsqrt(stat_new)
    return (param_new, stat_new)


def local(
    tokens,
    cotangent,
    seq_lengths,
    w_qkv,
    qkv_bias_state,
    w_out,
    out_bias_state,
    w_up,
    up_bias_state,
    w_down,
    ln_state,
    qkv_left,
    qkv_right,
    out_left,
    out_right,
    up_left,
    up_right,
    down_left,
    down_right,
):
    row_count, share_width = tokens.shape
    mp_size = lax.axis_size("mp")
    dp_size = lax.axis_size("dp")
    model_width = share_width * mp_size
    own_width = w_qkv.shape[2]
    mp_place = lax.axis_index("mp")

    piece = ln_state.shape[2]
    up_piece = up_bias_state.shape[1]

    def lane_rows(*values):
        flat = jnp.concatenate([value.reshape(-1) for value in values])
        return jnp.pad(flat, (0, -flat.shape[0] % LANES)).reshape(-1, LANES)

    small = jnp.concatenate(
        [
            lane_rows(ln_state[0]),
            lane_rows(up_bias_state[0]),
            lane_rows(qkv_bias_state[0], out_bias_state[0]),
        ],
        axis=0,
    )
    up_rows = lane_rows(up_bias_state[0]).shape[0]
    small = jnp.pad(small, ((0, 8 - small.shape[0]), (0, 0))).astype(jnp.bfloat16)
    slots = seq_lengths.shape[1]
    ends = jnp.pad(
        jnp.cumsum(seq_lengths[0]), (0, LANES - slots), constant_values=2 * row_count
    ).astype(jnp.int32)
    planes = w_qkv.transpose(1, 0, 2)
    (
        turned_block,
        full_up,
        full_qkvo,
        normed,
        grad_rows,
        spread,
        stats,
        activated,
        slope,
        ready_down,
    ) = first_step(
        (w_up, planes, w_out, w_down),
        tokens,
        cotangent,
        small.astype(jnp.float32)[None],
        jnp.broadcast_to(ends[None, :], (8, LANES)),
        slots,
        piece,
        up_piece,
    )
    field_row = 1 + up_rows
    turned_down, grad_projected, attended, ready_qkvo, owned_down, vector_three = third_step(
        turned_block,
        ready_down,
        normed,
        grad_rows,
        full_qkvo,
        spread,
        jnp.broadcast_to(ends[None, :], (8, LANES)),
        ends[:, None],
        slots,
        piece,
        field_row,
    )
    grad_hidden, ready_up, owned_qkvo, vector_four, output = fourth_step(
        ready_qkvo,
        normed,
        grad_rows,
        turned_down,
        slope,
        activated,
        attended,
        full_qkvo,
        tokens,
        spread,
        piece,
        field_row,
    )
    input_grad, up_send, down_send, up_own, sums, new_w_down, new_planes, new_w_out = fifth_step(
        ready_up,
        grad_hidden,
        grad_projected,
        full_qkvo,
        full_up,
        tokens,
        cotangent,
        stats,
        spread,
        vector_three,
        vector_four,
        owned_down,
        owned_qkvo,
        (down_left, down_right, w_down),
        (qkv_left, qkv_right, planes),
        (out_left, out_right, w_out),
        piece,
    )
    steps = range(dp_size - 2)
    rising = lax.ppermute(up_send, "dp", [(place, place + 2) for place in steps])
    falling = lax.ppermute(down_send, "dp", [(place + 2, place) for place in steps])
    (
        output,
        input_grad,
        new_w_down,
        new_planes,
        new_w_out,
        down_left_new,
        down_right_new,
        qkv_left_new,
        qkv_right_new,
        out_left_new,
        out_right_new,
    ) = statistics_step(
        (owned_down, owned_qkvo),
        (down_left, down_right, qkv_left, qkv_right, out_left, out_right),
        (output, input_grad, new_w_down, new_planes, new_w_out),
    )
    up_left_new, up_right_new, new_w_up = last_step(
        (up_own, rising, falling), up_left, up_right, w_up
    )
    new_w_qkv = new_planes.transpose(1, 0, 2)

    dp_place = lax.axis_index("dp")

    def mine(values, count):
        return take(values.reshape(count, dp_size, -1), dp_place, 1)

    owned_bqkv = mine(sums[0, : 3 * own_width], 3)
    owned_bup = mine(sums[1], 1)[0]
    owned_norm = jnp.concatenate([mine(sums[2, :share_width], 1), mine(sums[3, :share_width], 1)])
    bias_total = mine(sums[4, :share_width], 1)
    owned_obias = jnp.concatenate([bias_total, bias_total])
    qkv_params, qkv_stats = vector_update(qkv_bias_state, owned_bqkv)
    obias_params, obias_stats = vector_update(out_bias_state, owned_obias)
    norm_new_params, norm_new_stats = vector_update(ln_state, owned_norm)
    new_up_bias, new_up_stat = vector_update(up_bias_state, owned_bup)
    new_vector_params = jnp.concatenate([qkv_params, obias_params, norm_new_params], axis=0)
    new_vector_stats = jnp.concatenate([qkv_stats, obias_stats, norm_new_stats], axis=0)
    return (
        output,
        input_grad,
        new_w_qkv,
        new_w_out,
        new_w_up,
        new_w_down,
        new_vector_params,
        new_vector_stats,
        new_up_bias,
        new_up_stat,
        qkv_left_new,
        qkv_right_new,
        out_left_new,
        out_right_new,
        up_left_new,
        up_right_new,
        down_left_new,
        down_right_new,
    )


def solution(mesh):
    return jax.shard_map(
        local,
        mesh=mesh,
        in_specs=(
            P("dp", "mp"),
            P("dp", "mp"),
            P("dp", None),
            P("dp", None, "mp"),
            P(None, None, ("mp", "dp")),
            P("mp", "dp"),
            P(None, None, ("mp", "dp")),
            P("dp", "mp"),
            P(None, ("mp", "dp")),
            P("mp", "dp"),
            P(None, None, ("mp", "dp")),
            P(None, "mp", "dp", None, None),
            P(None, "mp", "dp", None, None),
            P(None, "mp", "dp", None, None),
            P(None, "mp", "dp", None, None),
            P(None, "mp", "dp", None, None),
            P(None, "mp", "dp", None, None),
            P(None, "mp", "dp", None, None),
            P(None, "mp", "dp", None, None),
        ),
        out_specs=(
            P("dp", "mp"),
            P("dp", "mp"),
            P("dp", None, "mp"),
            P("mp", "dp"),
            P("dp", "mp"),
            P("mp", "dp"),
            P(None, ("mp", "dp")),
            P(None, ("mp", "dp")),
            P(("mp", "dp")),
            P(("mp", "dp")),
            P("mp", "dp", None, None),
            P("mp", "dp", None, None),
            P("mp", "dp", None, None),
            P("mp", "dp", None, None),
            P("mp", "dp", None, None),
            P("mp", "dp", None, None),
            P("mp", "dp", None, None),
            P("mp", "dp", None, None),
        ),
        check_vma=False,
    )
```

time: 642 us -> 488 us (0.76)
  matrix products: 77.4 us -> 0 us
  Pallas kernels: 506 us -> 461 us
  other arithmetic: 32.2 us -> 2.66 us
  local copies, waits for them, and re-layouts: 17.3 us -> 9.38 us
    dot_general x12 -> x0, matrix products: 77.4 us -> none  [dot_f32(): lax.dot_general(left.astype(jnp.bfloat16), right.astype(jnp.bfloat16), ((...]
    pallas_call x2, Pallas kernels: 113 us -> 51.6 us  [the longest x1 30.1 us: statistics_step(): pl.pallas_call(kernel, in_specs=[spaces[place] for place in 'vv' + 'hvvhh...]
    pallas_call x4, Pallas kernels: 392 us -> 409 us  [carrying(): pl.pallas_call(kernel, in_specs=[spaces[place] for place in in_places], o...]
    reduce_sum x4 -> x0, other arithmetic: 11.8 us -> none  [the longest x1 5.72 us: local(): jnp.mean(inputs * inputs, axis=1, keepdims=True) - row_mean * row_mean]
    convert_element_type x5 -> x0, other arithmetic: 8.13 us -> none  [the longest x1 4.75 us: local(): ((inputs - row_mean) * inv_std * norm_all[0] + norm_all[1]).astype(jnp.bf...]
  transfers between devices with their start and end apart: 0 -> 2, of which waited for: 0 -> 0; matrix products, arithmetic and copies ran while one was open for 0% -> 1% of each run, Pallas kernels for 0% -> 6%
where the time goes in v3:
time: 488 us; the launch traced here: 479 us
  Pallas kernels  461 us (94%)
  local copies, waits for them, and re-layouts  9.38 us (2%)
  starting transfers between devices  5.55 us (1%)
    pallas_call x4, Pallas kernels, carrying(): pl.pallas_call(kernel, in_specs=[spaces[place] for place in in_places], o...  409 us
    pallas_call x1, Pallas kernels, statistics_step(): pl.pallas_call(kernel, in_specs=[spaces[place] for place in 'vv' + 'hvvhh...  30.1 us
    pallas_call x1, Pallas kernels, last_step(): pl.pallas_call(last_kernel, in_specs=[spaces[place] for place in 'vvvvhh'...  21.5 us
  transfers between devices with their start and end apart: 2, of which 0 were waited for; matrix products, arithmetic and copies ran while one was open for 1% of the time, Pallas kernels for 6%

profile of v3, /device:TPU:0, one launch (start us, length us, event | category | flops | bytes accessed | tf_op | source)
XLA Modules:
  0.0 479.5 jit_solution(15975315762107739285)
XLA Ops:
  0.7 0.7 slice.73
  1.3 0.1 reshape_squeeze.25
  1.4 0.8 fusion.22
  2.2 0.1 reshape_squeeze.24
  2.3 0.7 convert_reduce_fusion
  3.0 0.7 slice.74
  3.7 0.1 reshape.87
  3.7 0.7 copy.42
  4.5 0.1 reduce.1
  4.6 0.7 copy.43.ends_col_ref
  5.4 0.1 fusion.17
  5.5 0.6 fusion.8.small_ref
  6.1 0.6 broadcast_in_dim.20.ends_ref
  6.7 157.6 %gathers_beside_hidden.1 = (bf16[256,2048]{1,0:T(8,128)(2,1)}, bf16[2048,2048]{1,0:T(8,128)(2,1)}, bf16[2048,2048]{1,0:T(8,128)(2,1)}, bf16[1024,2048]{1,0:T(8,1...) custom-call(f32[256,2048]{1,0:T(8,128)} %w_up.1, ...), custom_call_target="tpu_custom_call" | custom-call | flops 17179869184 | bytes 33554432 | tf_op jit(solution)/shard_map/gathers_beside_hidden/pallas_call | solution.py:744
  164.3 109.0 %lines_beside_attention.1 = (bf16[2048,2048]{1,0:T(8,128)(2,1)}, bf16[1024,1536]{1,0:T(8,128)(2,1)}, bf16[1024,512]{1,0:T(8,128)(2,1)}, bf16[4,256,2048]{2,1,0:T...) custom-call(bf16[256,2048]{1,0:T(8,128)(2,1)} %get-tuple-element.61.block_ref, ...), custom_call_target="tpu_custom_call" | custom-call | flops 23622320128 | bytes 33554432 | tf_op jit(solution)/shard_map/lines_beside_attention/pallas_call | solution.py:744
  273.3 75.0 %line_beside_hidden_grad.1 = (bf16[1024,2048]{1,0:T(8,128)(2,1)}, bf16[4,256,2048]{2,1,0:T(8,128)(2,1)}, f32[256,2048]{1,0:T(8,128)}, f32[8,2048]{1,0:T(8,128)}, bf16[1024,512]{1,0:T(8,128)(2,1)}) custom-call(bf16[4,256,2048]{2,1,0:T(8,128)(2,1)} %get-tuple-element.68.ready_hbm, bf16[1024,2048]{1,0:T(8,128)(2,1)} %get-tuple-element.63.xn_hbm, ...), custom_call_target="tpu_custom_call" | custom-call | flops 25769803776 | bytes 33554432 | tf_op jit(solution)/shard_map/line_beside_hidden_grad/pallas_call | solution.py:744
  348.3 67.5 %line_beside_norm_grad.1 = (f32[1024,512]{1,0:T(8,128)}, bf16[256,2048]{1,0:T(8,128)(2,1)}, bf16[256,2048]{1,0:T(8,128)(2,1)}, bf16[256,2048]{1,0:T(8,128)(2,1)}...) custom-call(bf16[4,256,2048]{2,1,0:T(8,128)(2,1)} %get-tuple-element.75.ready_hbm, ...), custom_call_target="tpu_custom_call" | custom-call | flops 17179869184 | bytes 33554432 | tf_op jit(solution)/shard_map/line_beside_norm_grad/pallas_call | solution.py:744
  415.9 4.0 collective-permute-start
  419.9 1.5 collective-permute-start.1
  421.4 0.9 slice_reduce_fusion.4
  422.3 0.8 slice_reduce_fusion.1
  423.1 0.9 slice_reduce_fusion
  424.0 0.1 reshape_squeeze.29
  424.1 0.1 reshape_squeeze.27
  424.2 0.1 reshape_squeeze.28
  424.4 0.6 pad_maximum_fusion
  425.0 0.6 pad_maximum_fusion.1
  425.6 0.6 multiply_subtract_fusion
  426.2 30.1 %statistics.1 = (bf16[1024,512]{1,0:T(8,128)(2,1)}, f32[1024,512]{1,0:T(8,128)}, f32[2048,256]{1,0:T(8,128)}, f32[3,256,512]{2,1,0:T(8,128)}, f32[512,256]{1,0:T...) custom-call(f32[256,2048]{1,0:T(8,128)} %get-tuple-element.67.down_h, ...), custom_call_target="tpu_custom_call" | custom-call | flops 8589934592 | bytes 56098816 | tf_op jit(solution)/shard_map/statistics/pallas_call | solution.py:1888
  456.4 1.0 copy-done
  457.3 0.4 copy-done.1
  457.7 21.5 %last_weight.1 = (f32[1,1,256,256]{3,2,1,0:T(8,128)}, f32[1,1,2048,2048]{3,2,1,0:T(8,128)}, f32[256,2048]{1,0:T(8,128)}) custom-call(bf16[256,2048]{1,0:T(8,128)(2,1)} %get-tuple-element.90.own_ref, bf16[256,2048]{1,0:T(8,128)(2,1)} %copy-done, bf16[256,2048]{1,0:T(8,128)(2,1)} %copy-done.1, f32[2,1,1,256,256]{4,3,2,1,0:T(8,128)} %up_left.1, ...), custom_call_target="tpu_custom_call" | custom-call | flops 8589934592 | bytes 50331648 | tf_op jit(solution)/shard_map/last_weight/pallas_call | solution.py:1946
  (23 shorter events, 0.2 us)
Async XLA Ops:
  348.3 74.8 %copy-start.2 = (f32[2,256]{1,0:T(2,128)S(1)}, f32[2,256]{1,0:T(2,128)}, u32[]{:S(2)}) copy-start(f32[2,256]{1,0:T(2,128)} %param.27) | copy-start | bytes 6148
  348.3 75.9 %copy-start.3 = (f32[2,2,64]{2,1,0:T(2,128)S(1)}, f32[2,2,64]{2,1,0:T(2,128)}, u32[]{:S(2)}) copy-start(f32[2,2,64]{2,1,0:T(2,128)} %param.25) | copy-start | bytes 3076
  348.3 76.1 %copy-start.4 = (f32[2,2,64]{2,1,0:T(2,128)S(1)}, f32[2,2,64]{2,1,0:T(2,128)}, u32[]{:S(2)}) copy-start(f32[2,2,64]{2,1,0:T(2,128)} %param.29) | copy-start | bytes 3076
  415.9 40.5 %collective-permute-start = (bf16[256,2048]{1,0:T(8,128)(2,1)}, bf16[256,2048]{1,0:T(8,128)(2,1)S(1)}, u32[]{:S(2)}, u32[]{:S(2)}) collective-permute-start(bf16[256,2048]{1,0:T(8,128)(2,1)} %get-tuple-element.91), channel_id=1, source_target_pairs={{0,2},{1,3},{2,4},{3,5},{4,6},{5,7},{8,10},{9,11},{10,12},{11,13},... | collective-permute-start | bytes 3145736 | tf_op jit(solution)/shard_map/ppermute | solution.py:2098
  419.9 36.4 %collective-permute-start.1 = (bf16[256,2048]{1,0:T(8,128)(2,1)}, bf16[256,2048]{1,0:T(8,128)(2,1)S(1)}, u32[]{:S(2)}, u32[]{:S(2)}) collective-permute-start(bf16[256,2048]{1,0:T(8,128)(2,1)} %get-tuple-element.92), channel_id=1, source_target_pairs={{2,0},{3,1},{4,2},{5,3},{6,4},{7,5},{10,8},{11,9},{12,10},{13,11},... | collective-permute-start | bytes 3145736 | tf_op jit(solution)/shard_map/ppermute | solution.py:2099
  456.4 1.0 copy-start
  456.4 1.3 copy-start.1

commit v4 on v3

--- a/solution.py
+++ b/solution.py
@@ -303,14 +303,15 @@
                 return pl.ds(pl.multiple_of(start + rows.start, rows.size), rows.size)
 
             def begin(rows):
-                out[small(rows), :] = self.blocks[self.spot, small(rows), :].astype(jnp.float32)
+                out[small(rows), :] = self.blocks[self.spot, small(rows), :].astype(out.dtype)
 
             by_rows(self.part, 16, begin)
 
             def gain(slots):
                 def once(rows):
                     here = small(rows)
-                    out[here, :] = out[here, :] + slots[end - 1, here, :].astype(jnp.float32)
+                    total = summed(out[here, :], slots[end - 1, here, :])
+                    out[here, :] = total.astype(out.dtype)
 
                 by_rows(self.part, 16, once)
 
@@ -500,9 +501,9 @@
     up_piece,
     slots,
     w_up_ref,
-    w_qkv_ref,
-    w_out_ref,
-    w_down_ref,
+    w_qkv_hbm,
+    w_out_hbm,
+    w_down_hbm,
     x_ref,
     gy_ref,
     small_ref,
@@ -510,13 +511,13 @@
     turned_out,
     full_ref,
     next_full,
-    xn_ref,
-    gy_full,
+    xn_out,
+    gy_out,
     spread_ref,
     stats_ref,
     act_out,
     slope_out,
-    sums_ref,
+    sums_out,
     gather_send,
     gather_recv,
     next_send,
@@ -538,7 +539,17 @@
     block_ref,
     next_ref,
     valid_ref,
+    xn_ref,
+    gy_full,
+    sums_ref,
+    w_qkv_ref,
+    w_out_ref,
+    w_down_ref,
 ):
+    loads = fetch(
+        [(w_qkv_hbm, w_qkv_ref), (w_out_hbm, w_out_ref), (w_down_hbm, w_down_ref)],
+        local_sems.at[pl.ds(6, 3)],
+    )
     columns = lax.axis_size("dp")
     total = columns * lax.axis_size("mp")
     mp_place = lax.axis_index("mp")
@@ -590,6 +601,8 @@
     rows, width = xn_ref.shape
     depth = block_ref.shape[0]
     head_cols = w_qkv_ref.shape[2]
+    for copy in loads:
+        copy.wait()
     for kind in range(3):
         next_ref[:, pl.ds(kind * head_cols, head_cols)] = w_qkv_ref[kind].astype(jnp.bfloat16)
     turned = jnp.transpose(w_out_ref[...]).astype(jnp.bfloat16)
@@ -636,6 +649,7 @@
             xn_ref[here, pl.ds(group * LANES, LANES)] = part.astype(jnp.bfloat16)
 
     by_rows(rows, ROW_TILE, normalize)
+    stores = fetch([(xn_ref, xn_out)], local_sems.at[pl.ds(3, 1)])
     weight.finish()
     load = pltpu.make_async_copy(full_ref, up_ref, local_sems.at[0])
     load.start()
@@ -646,6 +660,7 @@
         gy_full[here, :] = kept.astype(jnp.bfloat16)
 
     by_rows(rows, ROW_TILE, blank)
+    stores += fetch([(gy_full, gy_out)], local_sems.at[pl.ds(4, 1)])
     bias = vector_rows(
         spread_ref, [mp_place * columns + owner for owner in range(columns)], 1, up_piece
     )
@@ -665,16 +680,12 @@
     by_rows(rows // 2, ROW_TILE, tile)
     later.advance(1)
     by_rows(rows // 2, ROW_TILE, lambda here: tile(pl.ds(rows // 2 + here.start, here.size)))
-    stores = [
-        pltpu.make_async_copy(act_ref, act_out, local_sems.at[1]),
-        pltpu.make_async_copy(slope_ref, slope_out, local_sems.at[2]),
-    ]
-    for store in stores:
-        store.start()
+    stores += fetch([(act_ref, act_out), (slope_ref, slope_out)], local_sems.at[pl.ds(1, 2)])
     later.advance(2, 0, 1)
     products.far()
     later.advance(2, 1)
     products.near()
+    stores += fetch([(sums_ref, sums_out)], local_sems.at[pl.ds(5, 1)])
     for step in range(3, later.count):
         later.advance(step)
     later.finish()
@@ -694,7 +705,7 @@
         functools.partial(first_kernel, piece, up_piece, slots),
         1,
         weights + (tokens, cotangent, small, ends),
-        "vvvvhhvv",
+        "vhhhhhvv",
         [
             ((part, columns), low),
             ((part * dp_size, columns), low),
@@ -707,7 +718,7 @@
             ((rows, columns), low),
             ((count, part, columns), low),
         ],
-        "vhhvvvvhhv",
+        "vhhhhvvhhh",
         gather_sems()
         + gather_sems()
         + block_sems()
@@ -719,11 +730,15 @@
             pltpu.VMEM((part * dp_size, columns), low),
             pltpu.VMEM((rows, columns), low),
             pltpu.VMEM((rows, columns), low),
-            pltpu.SemaphoreType.DMA((3,)),
+            pltpu.SemaphoreType.DMA((9,)),
             pltpu.VMEM((part, columns), low),
             pltpu.VMEM((part, columns), low),
             pltpu.VMEM((rows, 1), jnp.float32),
-        ],
+            pltpu.VMEM(wide, low),
+            pltpu.VMEM(wide, low),
+            pltpu.VMEM((count, part, columns), low),
+        ]
+        + [pltpu.VMEM(weight.shape, weight.dtype) for weight in weights[1:]],
         4 * rows * wide[1] * columns,
         "gathers_beside_hidden",
     )
@@ -753,6 +768,15 @@
         cost_estimate=pl.CostEstimate(flops=flops, bytes_accessed=1 << 25, transcendentals=0),
         name=name,
     )(*operands)
+
+
+PLAN = {
+    "projected": (),
+    0: ((1, 0), (1, 1)),
+    1: ((2, 0),),
+    "attended": ((2, 1),),
+    "far": ((3, 0),),
+}
 
 
 def third_kernel(
@@ -771,7 +795,7 @@
     full_ref,
     grad_out,
     or_out,
-    sums_ref,
+    sums_out,
     owned_ref,
     vector_ref,
     gather_send,
@@ -799,6 +823,7 @@
     keep_ref,
     ahead_ref,
     behind_ref,
+    sums_ref,
 ):
     loads = [
         pltpu.make_async_copy(source, target, local_sems.at[index])
@@ -869,6 +894,17 @@
         load.wait()
     by_rows(rows, ROW_TILE, project)
     vector_ref[...] = jnp.zeros_like(vector_ref)
+
+    done = set()
+    pairs = head_cols // LANES
+
+    def events(wanted):
+        for step, piece in wanted:
+            if (step, piece) not in done and step < weight.count:
+                done.add((step, piece))
+                weight.advance(step, piece, piece + 1)
+                if step + 1 < weight.count:
+                    line.advance(step + 1, piece, piece + 1)
 
     lane = lax.broadcasted_iota(jnp.int32, (ROW_TILE, LANES), 1)
     first_head = lane < HEAD_DIM
@@ -917,34 +953,25 @@
                 grad_ref[here, lanes] = part
                 vector_ref[0:1, lanes] += jnp.sum(part.astype(jnp.float32), axis=0, keepdims=True)
 
-        @pl.when(pair == 0)
-        def _():
-            weight.advance(1)
-            line.advance(2)
-
-        @pl.when(pair == 1)
-        def _():
-            weight.advance(2, 0, 1)
-            line.advance(3, 0, 1)
-
+        for index in range(pairs):
+            if index in PLAN:
+                pl.when(pair == index)(functools.partial(events, PLAN[index]))
         return carry
 
-    lax.fori_loop(0, head_cols // LANES, one_pair, 0)
+    events(PLAN["projected"])
+    lax.fori_loop(0, pairs, one_pair, 0)
     stores = [
         pltpu.make_async_copy(grad_ref, grad_out, local_sems.at[4]),
         pltpu.make_async_copy(or_ref, or_out, local_sems.at[5]),
     ]
     for store in stores:
         store.start()
-    weight.advance(2, 1)
-    line.advance(3, 1)
+    events(PLAN["attended"])
     products.far()
-    weight.advance(3, 0, 1)
+    events(PLAN["far"])
     products.near()
-    weight.advance(3, 1)
-    for step in range(4, weight.count):
-        weight.advance(step)
-        line.advance(step)
+    stores += fetch([(sums_ref, sums_out)], local_sems.at[pl.ds(6, 1)])
+    events([(step, piece) for step in range(1, weight.count) for piece in range(PIECES)])
     line.finish(owned_ref)
     weight.finish()
     for store in stores:
@@ -979,10 +1006,10 @@
             ((rows, 3 * head_cols), low),
             ((rows, head_cols), low),
             ((count, part, columns), low),
-            ((part, ready.shape[2]), jnp.float32),
+            ((part, ready.shape[2]), low),
             ((8, columns), jnp.float32),
         ],
-        "hhhvvv",
+        "hhhhvv",
         gather_sems()
         + sum_scratch(part, ready.shape[2])
         + pair_scratch(part, columns)
@@ -999,10 +1026,11 @@
             pltpu.VMEM((width, columns), low),
             pltpu.VMEM((rows, 3 * head_cols), low),
             pltpu.VMEM((rows, head_cols), low),
-            pltpu.SemaphoreType.DMA((6,)),
+            pltpu.SemaphoreType.DMA((7,)),
             pltpu.VMEM((rows, LANES), jnp.float32),
             pltpu.VMEM((rows, LANES), jnp.float32),
             pltpu.VMEM((rows, LANES), jnp.float32),
+            pltpu.VMEM((count, part, columns), low),
         ],
         4 * rows * width * columns + 12 * rows * rows * head_cols,
         "lines_beside_attention",
@@ -1024,8 +1052,10 @@
     x_ref,
     spread_ref,
     gh_out,
-    sums_ref,
-    owned_ref,
+    sums_out,
+    up_send,
+    down_send,
+    own_ref,
     vector_ref,
     out_ref,
     below,
@@ -1048,18 +1078,19 @@
     weight_ref,
     gh_ref,
     local_sems,
+    sums_ref,
 ):
     loads = [
         pltpu.make_async_copy(source, target, local_sems.at[index])
         for index, (source, target) in enumerate(
             [
                 (ready_hbm, ready_ref),
-                (gy_hbm, gy_ref),
                 (down_hbm, down_ref),
-                (slope_hbm, wide_ref),
-                (xn_hbm, xn_ref),
+                (act_hbm, wide_ref),
                 (or_hbm, or_ref),
                 (qkvo_hbm.at[:, pl.ds(3 * head_cols, head_cols)], weight_ref),
+                (gy_hbm, gy_ref),
+                (xn_hbm, xn_ref),
             ]
         )
     ]
@@ -1075,7 +1106,7 @@
     pl.semaphore_wait(barrier, count)
     loads[0].wait()
     line.advance(1)
-    for load in loads[1:4]:
+    for load in loads[1:5]:
         load.wait()
     rows, share_width = x_ref.shape
     width = down_ref.shape[1] // 4
@@ -1092,16 +1123,6 @@
                 grad_hidden.astype(jnp.float32), axis=0, keepdims=True
             )
 
-    by_rows(rows, ROW_TILE, tile)
-    late = pltpu.make_async_copy(act_hbm, wide_ref, local_sems.at[7])
-    late.start()
-    store = pltpu.make_async_copy(gh_ref, gh_out, local_sems.at[8])
-    store.start()
-    for load in loads[4:]:
-        load.wait()
-    line.advance(2, 0, 1)
-    late.wait()
-
     def branch(share):
         start = pl.multiple_of(branches.owner(share) * share_width, share_width)
         where = pl.ds(start, share_width)
@@ -1111,21 +1132,26 @@
             part = part + contract(wide_ref[here, :], down_ref[where, :], 1, 1)
             t_parts[share, here, :] = part.astype(jnp.bfloat16)
 
-        by_rows(rows, ROW_TILE, once)
+        by_rows(rows, 2 * ROW_TILE, once)
         branches.after(share)
 
     shares = branches.size
-    for share in range(shares - 1):
+    for share in range(shares):
         branch(share)
+        if share == 2:
+            line.advance(2, 0, 1)
+    late = pltpu.make_async_copy(slope_hbm, wide_ref, local_sems.at[7])
+    late.start()
     line.advance(2, 1)
     branches.second()
+    for load in loads[5:]:
+        load.wait()
+    late.wait()
+    by_rows(rows, ROW_TILE, tile)
+    stores = fetch([(gh_ref, gh_out)], local_sems.at[pl.ds(8, 1)])
     products.far()
-    line.advance(3, 0, 1)
-    products.near()
-    line.advance(3, 1)
-    for step in range(4, line.count):
+    for step in range(3, line.count - 1):
         line.advance(step)
-    branch(shares - 1)
     branches.finish()
     biases = [
         jnp.concatenate(field_rows(spread_ref, field_row, kind, piece), axis=1) for kind in (3, 4)
@@ -1135,8 +1161,12 @@
         total = x_ref[here, :].astype(jnp.float32) + branches.total(tile_index, ROW_TILE)
         total = total + biases[0] + biases[1]
         out_ref[here, :] = total.astype(jnp.bfloat16)
-    line.finish(owned_ref)
-    store.wait()
+    products.near()
+    stores += fetch([(sums_ref, sums_out)], local_sems.at[pl.ds(9, 1)])
+    by_rows(own_ref.shape[0], 32, lambda here: keep_block(ready_ref, line.spot, own_ref, here))
+    line.hand_out(up_send, down_send)
+    for store in stores:
+        store.wait()
 
 
 def fourth_step(
@@ -1176,11 +1206,13 @@
         [
             ((rows, columns), low),
             ((count, part, columns), low),
-            ((part, columns), jnp.float32),
+            ((part, columns), low),
+            ((part, columns), low),
+            ((part, columns), low),
             ((8, columns), jnp.float32),
             (tokens.shape, low),
         ],
-        "hvvvv",
+        "hhvvvvv",
         sum_scratch(part, columns)
         + pair_scratch(part, columns)
         + scatter_scratch(rows, tokens.shape[1])
@@ -1193,7 +1225,8 @@
             pltpu.VMEM((rows, head_cols), low),
             pltpu.VMEM((width, head_cols), low),
             pltpu.VMEM((rows, columns), low),
-            pltpu.SemaphoreType.DMA((9,)),
+            pltpu.SemaphoreType.DMA((10,)),
+            pltpu.VMEM((count, part, columns), low),
         ],
         6 * rows * width * columns,
         "line_beside_hidden_grad",
@@ -1346,77 +1379,6 @@
     return copies
 
 
-def step_tall(grad, root_left, root_right, master, master_out):
-    depth, size = grad.shape
-    tile_rows = min(STREAM, size)
-
-    def scope(root_in, side_in, side_new, sems):
-        root = root_right[1, 0, 0].astype(jnp.bfloat16)
-
-        def where(tile):
-            return pl.ds(pl.multiple_of(tile * tile_rows, tile_rows), tile_rows)
-
-        def loads(tile, slot):
-            here = where(tile)
-            source = root_left.at[1, 0, 0, here, :]
-            return [
-                pltpu.make_async_copy(source, root_in.at[slot], sems.at[0, slot]),
-                pltpu.make_async_copy(master.at[here, :], side_in.at[slot], sems.at[1, slot]),
-            ]
-
-        def stores(tile, slot):
-            target = master_out.at[where(tile), :]
-            return [pltpu.make_async_copy(side_new.at[slot], target, sems.at[2, slot])]
-
-        def compute(tile, slot):
-            first = contract(root_in[slot].astype(jnp.bfloat16), grad[...], 1, 1)
-            step = contract(first.astype(jnp.bfloat16), root, 1, 0)
-            side_new[slot] = side_in[slot] - matrix_rate * step
-
-        stream(size // tile_rows, loads, stores, compute)
-
-    pl.run_scoped(
-        scope,
-        pltpu.VMEM((SLOTS, tile_rows, size), jnp.float32),
-        pltpu.VMEM((SLOTS, tile_rows, depth), jnp.float32),
-        pltpu.VMEM((SLOTS, tile_rows, depth), jnp.float32),
-        pltpu.SemaphoreType.DMA((3, SLOTS)),
-    )
-
-
-def step_wide(grad, root_left, root_right, master, master_out):
-    depth, size = grad.shape
-    tile_rows = min(STREAM, size)
-    plane = master.shape[2]
-
-    def scope(root_in, low, sems):
-        first = contract(root_left[1, 0, 0].astype(jnp.bfloat16), grad[...], 1, 0)
-        low[...] = first.astype(jnp.bfloat16)
-
-        def where(tile):
-            return pl.ds(pl.multiple_of(tile * tile_rows, tile_rows), tile_rows)
-
-        def loads(tile, slot):
-            source = root_right.at[1, 0, 0, :, where(tile)]
-            return [pltpu.make_async_copy(source, root_in.at[slot], sems.at[slot])]
-
-        def compute(tile, slot):
-            step = contract(low[...], root_in[slot].astype(jnp.bfloat16), 1, 0)
-            start = tile * tile_rows
-            here = pl.ds(pl.multiple_of(lax.rem(start, plane), tile_rows), tile_rows)
-            kind = start // plane
-            master_out[kind, :, here] = master[kind, :, here] - matrix_rate * step
-
-        stream(size // tile_rows, loads, lambda tile, slot: [], compute)
-
-    pl.run_scoped(
-        scope,
-        pltpu.VMEM((SLOTS, size, tile_rows), jnp.float32),
-        pltpu.VMEM((depth, size), jnp.bfloat16),
-        pltpu.SemaphoreType.DMA((SLOTS,)),
-    )
-
-
 def fifth_kernel(
     head_cols,
     piece,
@@ -1431,25 +1393,15 @@
     spread_ref,
     vector_three,
     vector_four,
-    down_hbm,
-    owned_hbm,
-    down_left,
-    down_right,
-    w_down,
-    qkv_left,
-    qkv_right,
-    w_qkv_hbm,
-    out_left,
-    out_right,
-    w_out,
-    dx_out,
+    earlier,
+    earlier_rising,
+    earlier_falling,
+    gained_out,
+    terms_out,
     up_send,
     down_send,
     own_ref,
     sums_ref,
-    w_down_new,
-    w_qkv_out,
-    w_out_new,
     below,
     above,
     line_send,
@@ -1469,17 +1421,10 @@
     ready_ref,
     gh_ref,
     grad_ref,
-    low_down,
-    low_qkv,
-    low_out,
     x_ref,
     gy_ref,
     stats_ref,
-    owned_down,
-    owned_qkvo,
-    w_qkv,
-    w_qkv_new,
-    dx_ref,
+    gained_ref,
     load_sems,
 ):
     loads = fetch(
@@ -1487,9 +1432,6 @@
             (ready_hbm, ready_ref),
             (grad_hbm, grad_ref),
             (gh_hbm, gh_ref),
-            (owned_hbm, owned_qkvo),
-            (down_hbm, owned_down),
-            (w_qkv_hbm, w_qkv),
             (x_hbm, x_ref),
             (gy_hbm, gy_ref),
             (stats_hbm, stats_ref),
@@ -1503,7 +1445,6 @@
     dp_size = lax.axis_size("dp")
     dp_place = lax.axis_index("dp")
     rows, width = x_ref.shape
-    model_width = width * mp_size
     tiles = rows // ROW_TILE
     barrier = pltpu.get_barrier_semaphore()
 
@@ -1545,7 +1486,7 @@
                 part = part + contract(gh_ref[here, :], two_ref[slot], 1, 1)
                 g_parts[share, here, :] = part.astype(jnp.bfloat16)
 
-            by_rows(rows, ROW_TILE, tile)
+            by_rows(rows, 2 * ROW_TILE, tile)
             from_norm.after(share)
 
     columns = up_ref.shape[1]
@@ -1560,10 +1501,6 @@
     from_norm.second()
     for load in loads[3:]:
         load.wait()
-    low_down[...] = owned_down[...].astype(jnp.bfloat16)
-    low_qkv[...] = owned_qkvo[:, pl.ds(0, 3 * head_cols)].astype(jnp.bfloat16)
-    low_out[...] = owned_qkvo[:, pl.ds(3 * head_cols, head_cols)].astype(jnp.bfloat16)
-    step_tall(low_out, out_left, out_right, w_out, w_out_new)
     from_norm.finish()
 
     def lane_pair(first, second):
@@ -1578,6 +1515,7 @@
         normalized = (x_ref[here, :].astype(jnp.float32) - stats_ref[here, 0:1]) * stats_ref[here, 1:2]
         grad = from_norm.total(tile, ROW_TILE)
         gained = grad * gain
+        gained_ref[here, :] = gained
         terms = lane_pair(
             jnp.sum(gained, axis=1, keepdims=True),
             jnp.sum(gained * normalized, axis=1, keepdims=True),
@@ -1588,12 +1526,16 @@
         sums[1] += jnp.sum(grad, axis=0, keepdims=True)
         sums[2] += jnp.sum(upstream, axis=0, keepdims=True)
 
-    vector_ref[...] = jnp.zeros_like(vector_ref)
-    vector_ref[0:1, :] = vector_three[0:1, :]
-    vector_ref[1:2, :] = vector_four[0:1, :]
-    for index in range(3):
-        vector_ref[2 + index : 3 + index, pl.ds(0, width)] = sums[index]
-
+    store = pltpu.make_async_copy(gained_ref, gained_out, load_sems.at[len(loads)])
+    store.start()
+    three_width = vector_three.shape[1]
+    fields = [vector_three[0:1, pl.ds(0, three_width - head_cols)], vector_four[0:1, :]] + sums
+    flat = jnp.concatenate(fields, axis=1)
+    per_row = vector_ref.shape[1]
+    for row in range(8):
+        part = flat[:, row * per_row : (row + 1) * per_row]
+        if part.shape[1]:
+            vector_ref[row : row + 1, pl.ds(0, part.shape[1])] = part
     def terms_copy(step):
         peer = lax.rem(mp_place + step, mp_size)
         slot = step - 1
@@ -1613,40 +1555,27 @@
     for step in range(1, mp_size):
         terms_copy(step).start()
     lax.fori_loop(1, dp_size, vector_begin, 0)
-    step_wide(low_qkv, qkv_left, qkv_right, w_qkv, w_qkv_new)
-    stores = [pltpu.make_async_copy(w_qkv_new, w_qkv_out, load_sems.at[len(loads)])]
-    stores[0].start()
-    for step in range(1, mp_size):
-        terms_copy(step).wait()
-    for tile in range(tiles):
-        here = pl.ds(tile * ROW_TILE, ROW_TILE)
-        terms = terms_ref[:, here]
-        for slot in range(mp_size - 1):
-            terms = terms + terms_got[slot, :, here]
-        wide = jnp.concatenate([terms, jnp.zeros((LANES - 8, ROW_TILE), jnp.float32)], axis=0)
-        terms = jnp.transpose(wide) * (1.0 / model_width)
-        inv_std = stats_ref[here, 1:2]
-        normalized = (x_ref[here, :].astype(jnp.float32) - stats_ref[here, 0:1]) * inv_std
-        gained = from_norm.total(tile, ROW_TILE) * gain
-        upstream = gy_ref[here, :].astype(jnp.float32) * stats_ref[here, 2:3]
-        dx_ref[here, :] = upstream + inv_std * (gained - terms[:, 0:1] - normalized * terms[:, 1:2])
-    stores.append(pltpu.make_async_copy(dx_ref, dx_out, load_sems.at[len(loads) + 1]))
-    stores[1].start()
-    step_tall(low_down, down_left, down_right, w_down, w_down_new)
-
     def vector_end(step, carry):
         vector_copy(step).wait()
         return carry
 
+    by_rows(own_ref.shape[0], 32, lambda here: keep_block(ready_ref, line.spot, own_ref, here))
+    line.hand_out(up_send, down_send)
+    terms = terms_ref[...]
+    for step in range(1, mp_size):
+        terms_copy(step).wait()
+        terms = terms + terms_got[step - 1]
+    terms_out[...] = terms
     lax.fori_loop(1, dp_size, vector_end, 0)
     total = vector_ref[...]
     for slot in range(dp_size - 1):
         total = total + vector_got[slot]
-    sums_ref[...] = total
-    by_rows(own_ref.shape[0], 32, lambda here: keep_block(ready_ref, line.spot, own_ref, here))
-    line.hand_out(up_send, down_send)
-    for store in stores:
-        store.wait()
+    flat = jnp.concatenate([total[row : row + 1, :] for row in range(8)], axis=1)
+    start = 0
+    for row, field in enumerate(fields):
+        sums_ref[row : row + 1, pl.ds(0, field.shape[1])] = flat[:, start : start + field.shape[1]]
+        start += field.shape[1]
+    store.wait()
 
 
 def keep_block(blocks, index, out, here):
@@ -1665,11 +1594,7 @@
     spread,
     vector_three,
     vector_four,
-    owned_down,
-    owned_qkvo,
-    down,
-    qkv,
-    out,
+    earlier,
     piece,
 ):
     rows, width = tokens.shape
@@ -1679,6 +1604,8 @@
     dp_size = lax.axis_size("dp")
     low = jnp.bfloat16
     exact = jnp.float32
+    packed = 3 * head_cols + columns + 3 * width
+    packed = -(-packed // (8 * LANES)) * LANES
     return carrying(
         functools.partial(fifth_kernel, head_cols, piece),
         7,
@@ -1694,24 +1621,18 @@
             spread,
             vector_three,
             vector_four,
-            owned_down,
-            owned_qkvo,
         )
-        + down
-        + qkv
-        + out,
-        "hhhhhhhhvvvhh" + "hvh" + "vhh" + "hvh",
+        + earlier,
+        "hhhhhhhhvvvhhh",
         [
             ((rows, width), exact),
+            ((8, rows), exact),
             ((part, columns), low),
             ((part, columns), low),
             ((part, columns), low),
             ((8, columns), exact),
-            (down[2].shape, exact),
-            (qkv[2].shape, exact),
-            (out[2].shape, exact),
         ],
-        "hvvvvhhh",
+        "hvvvvv",
         sum_scratch(part, columns)
         + scatter_scratch(rows, width)
         + [
@@ -1719,25 +1640,18 @@
             pltpu.VMEM((mp_size - 1, 8, rows), exact),
             pltpu.SemaphoreType.DMA((mp_size - 1,)),
             pltpu.SemaphoreType.DMA((mp_size - 1,)),
-            pltpu.VMEM((8, columns), exact),
-            pltpu.VMEM((dp_size - 1, 8, columns), exact),
+            pltpu.VMEM((8, packed), exact),
+            pltpu.VMEM((dp_size - 1, 8, packed), exact),
             pltpu.SemaphoreType.DMA((dp_size - 1,)),
             pltpu.SemaphoreType.DMA((dp_size - 1,)),
             pltpu.VMEM(ready.shape, low),
             pltpu.VMEM((rows, columns), low),
             pltpu.VMEM((rows, 3 * head_cols), low),
-            pltpu.VMEM((part, columns), low),
-            pltpu.VMEM((part, 3 * head_cols), low),
-            pltpu.VMEM((part, head_cols), low),
             pltpu.VMEM((rows, width), low),
             pltpu.VMEM((rows, width), low),
             pltpu.VMEM(stats.shape, exact),
-            pltpu.VMEM((part, columns), exact),
-            pltpu.VMEM((part, columns), exact),
-            pltpu.VMEM(qkv[2].shape, exact),
-            pltpu.VMEM(qkv[2].shape, exact),
             pltpu.VMEM((rows, width), exact),
-            pltpu.SemaphoreType.DMA((11,)),
+            pltpu.SemaphoreType.DMA((7,)),
         ],
         4 * rows * width * mp_size * columns,
         "line_beside_norm_grad",
@@ -1747,7 +1661,7 @@
 class Averager:
     def __init__(self, grad, stats, stats_out, buffers, sems):
         self.grad, self.stats, self.stats_out = grad, stats, stats_out
-        self.stat_in, self.stat_new = buffers
+        self.stat_in, self.stat_new, self.root_in, self.side_in, self.side_new = buffers
         self.sems = sems
         self.tile_rows = self.stat_in.shape[1]
         self.tiles = grad.shape[1] // self.tile_rows
@@ -1756,224 +1670,345 @@
         return pl.ds(pl.multiple_of(tile * self.tile_rows, self.tile_rows), self.tile_rows)
 
     def loads(self, tile, slot):
-        source = self.stats.at[0, 0, 0, self.where(tile), :]
-        return [pltpu.make_async_copy(source, self.stat_in.at[slot], self.sems.at[0, slot])]
+        pairs = [
+            (self.stats.at[0, 0, 0, self.where(tile), :], self.stat_in),
+            (self.root_tile(tile), self.root_in),
+            (self.side(self.master, tile), self.side_in),
+        ]
+        return [
+            pltpu.make_async_copy(source, target.at[slot], self.sems.at[index, slot])
+            for index, (source, target) in enumerate(pairs)
+        ]
 
     def stores(self, tile, slot):
-        target = self.stats_out.at[0, 0, self.where(tile), :]
-        return [pltpu.make_async_copy(self.stat_new.at[slot], target, self.sems.at[1, slot])]
+        pairs = [
+            (self.stat_new, self.stats_out.at[0, 0, self.where(tile), :]),
+            (self.side_new, self.side(self.master_out, tile)),
+        ]
+        return [
+            pltpu.make_async_copy(source.at[slot], target, self.sems.at[3 + index, slot])
+            for index, (source, target) in enumerate(pairs)
+        ]
 
     def compute(self, tile, slot):
         product = contract(self.grad[:, self.where(tile)], self.grad[...], 0, 0)
         self.stat_new[slot] = 0.5 * self.stat_in[slot] + 0.5 * product
+        step = self.step(self.root_in[slot].astype(jnp.bfloat16))
+        self.side_new[slot] = self.side_in[slot] - matrix_rate * step
+
+    def start(self):
+        prime(self.tiles, self.loads)
 
     def run(self):
         stream(self.tiles, self.loads, self.stores, self.compute, True)
 
 
-class Updater(Averager):
-    def __init__(self, grad, stats, stats_out, buffers, sems, first, master, master_out, more):
+class WideUnit(Averager):
+    def __init__(self, grad, stats, stats_out, buffers, sems, first, small, small_out, master, out):
         super().__init__(grad, stats, stats_out, buffers, sems)
-        self.first, self.master, self.master_out = first, master, master_out
-        self.root_in, self.side_in, self.side_new = more
-
-    def loads(self, tile, slot):
-        here = self.where(tile)
-        source = self.stats.at[1, 0, 0, :, here]
-        return super().loads(tile, slot) + [
-            pltpu.make_async_copy(source, self.root_in.at[slot], self.sems.at[2, slot]),
-            pltpu.make_async_copy(
-                self.master.at[:, here], self.side_in.at[slot], self.sems.at[3, slot]
-            ),
-        ]
-
-    def stores(self, tile, slot):
-        target = self.master_out.at[:, self.where(tile)]
-        return super().stores(tile, slot) + [
-            pltpu.make_async_copy(self.side_new.at[slot], target, self.sems.at[4, slot])
-        ]
-
-    def compute(self, tile, slot):
-        super().compute(tile, slot)
-        step = contract(self.first[...], self.root_in[slot].astype(jnp.bfloat16), 1, 0)
-        self.side_new[slot] = self.side_in[slot] - matrix_rate * step
-
-
-def average_small(small, small_new, grad):
-    small_new[0, 0] = 0.5 * small[0, 0, 0] + 0.5 * contract(grad[...], grad[...], 1, 1)
-
-
-def statistics_kernel(
+        self.first, self.small, self.small_out = first, small, small_out
+        self.master, self.master_out = master, out
+
+    def root_tile(self, tile):
+        return self.stats.at[1, 0, 0, :, self.where(tile)]
+
+    def side(self, ref, tile):
+        if len(ref.shape) == 2:
+            return ref.at[:, self.where(tile)]
+        per_plane = ref.shape[2] // self.tile_rows
+        return ref.at[tile // per_plane, :, self.where(lax.rem(tile, per_plane))]
+
+    def prepare(self):
+        root = self.small[1, 0, 0].astype(jnp.bfloat16)
+        self.first[...] = contract(root, self.grad[...], 1, 0).astype(jnp.bfloat16)
+        average_small(self.small, self.small_out, self.grad)
+
+    def step(self, root):
+        return contract(self.first[...], root, 1, 0)
+
+
+class TallUnit(Averager):
+    def __init__(self, grad, stats, stats_out, buffers, sems, small, small_out, master, out):
+        super().__init__(grad, stats, stats_out, buffers, sems)
+        self.small, self.small_out = small, small_out
+        self.master, self.master_out = master, out
+
+    def root_tile(self, tile):
+        return self.stats.at[1, 0, 0, self.where(tile), :]
+
+    def side(self, ref, tile):
+        return ref.at[self.where(tile), :]
+
+    def prepare(self):
+        average_small(self.small, self.small_out, self.grad)
+
+    def step(self, root):
+        first = contract(root, self.grad[...], 1, 1).astype(jnp.bfloat16)
+        return contract(first, self.small[1, 0, 0].astype(jnp.bfloat16), 1, 0)
+
+
+def average_small(small, small_out, grad):
+    small_out[0, 0] = 0.5 * small[0, 0, 0] + 0.5 * contract(grad[...], grad[...], 1, 1)
+
+
+def unit_scratch(depth, size, wide):
+    tile_rows = min(STREAM, size)
+    exact = jnp.float32
+    root = (size, tile_rows) if wide else (tile_rows, size)
+    side = (depth, tile_rows) if wide else (tile_rows, depth)
+    shapes = [(tile_rows, size), (tile_rows, size), root, side, side]
+    return [pltpu.VMEM((SLOTS,) + shape, exact) for shape in shapes] + [
+        pltpu.SemaphoreType.DMA((5, SLOTS))
+    ]
+
+
+def local_call(kernel, operands, in_places, outs, out_places, scratch, name):
+    spaces = {"h": pl.BlockSpec(memory_space=pl.ANY), "v": pl.BlockSpec(memory_space=pltpu.VMEM)}
+    return pl.pallas_call(
+        kernel,
+        in_specs=[spaces[place] for place in in_places],
+        out_specs=[spaces[place] for place in out_places],
+        out_shape=[jax.ShapeDtypeStruct(shape, dtype) for shape, dtype in outs],
+        scratch_shapes=scratch,
+        compiler_params=pltpu.CompilerParams(vmem_limit_bytes=VMEM_LIMIT),
+        cost_estimate=pl.CostEstimate(flops=1 << 33, bytes_accessed=1 << 26, transcendentals=0),
+        name=name,
+    )(*operands)
+
+
+def down_kernel(
+    grad, stats, small, master, earlier, stats_out, small_out, master_out, *scratch
+):
+    *buffers, sems = scratch
+    unit = TallUnit(
+        grad, stats, stats_out, buffers, sems, small, small_out, master, master_out
+    )
+    unit.start()
+    unit.prepare()
+    unit.run()
+
+
+def down_step(grad, left, right, master, earlier):
+    exact = jnp.float32
+    return local_call(
+        down_kernel,
+        (grad, left, right, master, earlier),
+        "vhvhh",
+        [(left.shape[1:], exact), (right.shape[1:], exact), (master.shape, exact)],
+        "hvh",
+        unit_scratch(grad.shape[0], grad.shape[1], False),
+        "down_weight",
+    )
+
+
+def update_vectors(sums, states, up_state, params_out, stats_out, up_out, up_stat_out):
+    columns = sums.shape[1]
+    place = lax.axis_index("dp")
+    qkv_state, out_state, norm_state = states
+    piece = qkv_state.shape[2]
+    stride = lax.axis_size("dp") * piece
+    own = pltpu.roll(sums[...], lax.rem(columns - place * piece, columns), 1)
+    picks = [(qkv_state, kind, own[0:1, kind * stride : kind * stride + piece]) for kind in range(3)]
+    picks += [(out_state, kind, own[4:5, :piece]) for kind in range(2)]
+    picks += [(norm_state, kind, own[2 + kind : 3 + kind, :piece]) for kind in range(2)]
+
+    def update(param, stat, grad):
+        stat_new = 0.5 * stat + 0.5 * grad * grad
+        return (param - vector_rate * grad * lax.rsqrt(stat_new), stat_new)
+
+    for row, (state, kind, grad) in enumerate(picks):
+        param, stat = update(state[0, kind : kind + 1, :], state[1, kind : kind + 1, :], grad)
+        params_out[row : row + 1, :] = param
+        stats_out[row : row + 1, :] = stat
+    piece = up_state.shape[1]
+    own = pltpu.roll(sums[...], lax.rem(columns - place * piece, columns), 1)
+    param, stat = update(up_state[0:1, :], up_state[1:2, :], own[1:2, :piece])
+    up_out[...] = param
+    up_stat_out[...] = stat
+
+
+def attention_weights_kernel(
     passed,
-    owned_down,
-    owned_qkvo,
-    down_left,
-    down_right,
+    own_ref,
+    rising_ref,
+    falling_ref,
     qkv_left,
     qkv_right,
+    w_qkv,
     out_left,
     out_right,
+    w_out,
+    sums,
+    qkv_state,
+    out_state,
+    norm_state,
+    up_state,
+    x_ref,
+    gy_ref,
+    stats_ref,
+    gained_ref,
+    terms_ref,
     *refs,
 ):
     sources, refs = (refs[:passed], refs[passed:])
     targets, refs = (refs[:passed], refs[passed:])
-    held, refs = (refs[:passed], refs[passed:])
     (
-        down_left_new,
-        down_right_new,
         qkv_left_new,
         qkv_right_new,
+        w_qkv_new,
         out_left_new,
         out_right_new,
-        low_down,
+        w_out_new,
+        params_out,
+        stats_out,
+        up_out,
+        up_stat_out,
+        dx_out,
         low_qkv,
         low_out,
-        down_in,
-        down_new,
-        qkv_in,
-        qkv_new,
-        out_in,
-        out_new,
-        sems,
-        pass_sems,
-    ) = refs
-    units = [
-        Averager(low_down, down_left, down_left_new, (down_in, down_new), sems.at[0]),
-        Averager(low_qkv, qkv_right, qkv_right_new, (qkv_in, qkv_new), sems.at[1]),
-        Averager(low_out, out_left, out_left_new, (out_in, out_new), sems.at[2]),
-    ]
-    for unit in units:
-        prime(unit.tiles, unit.loads)
+        first,
+        dx_ref,
+        dx_sem,
+    ), refs = (refs[:16], refs[16:])
+    held, refs = (refs[:passed], refs[passed:])
+    pass_sems, *buffers = refs
+    qkv = WideUnit(
+        low_qkv,
+        qkv_right,
+        qkv_right_new,
+        buffers[:5],
+        buffers[5],
+        first,
+        qkv_left,
+        qkv_left_new,
+        w_qkv,
+        w_qkv_new,
+    )
+    out = TallUnit(
+        low_out,
+        out_left,
+        out_left_new,
+        buffers[6:11],
+        buffers[11],
+        out_right,
+        out_right_new,
+        w_out,
+        w_out_new,
+    )
+    qkv.start()
+    out.start()
     into = fetch(zip(sources, held), pass_sems.at[0])
     edge = low_qkv.shape[1]
-    low_down[...] = owned_down[...].astype(jnp.bfloat16)
-    low_qkv[...] = owned_qkvo[:, pl.ds(0, edge)].astype(jnp.bfloat16)
-    low_out[...] = owned_qkvo[:, pl.ds(edge, low_out.shape[1])].astype(jnp.bfloat16)
-    average_small(down_right, down_right_new, low_down)
-    average_small(qkv_left, qkv_left_new, low_qkv)
-    average_small(out_right, out_right_new, low_out)
+    owned = summed(own_ref[...], rising_ref[...], falling_ref[...]).astype(jnp.bfloat16)
+    low_qkv[...] = owned[:, :edge]
+    low_out[...] = owned[:, edge:]
+    qkv.prepare()
+    out.prepare()
     for copy in into:
         copy.wait()
     onward = fetch(zip(held, targets), pass_sems.at[1])
-    for unit in units:
-        unit.run()
+    rows, width = x_ref.shape
+    model_width = width * lax.axis_size("mp")
+    for tile in range(rows // ROW_TILE):
+        here = pl.ds(tile * ROW_TILE, ROW_TILE)
+        zeros = jnp.zeros((LANES - 8, ROW_TILE), jnp.float32)
+        terms = jnp.transpose(jnp.concatenate([terms_ref[:, here], zeros], axis=0))
+        terms = terms * (1.0 / model_width)
+        inv_std = stats_ref[here, 1:2]
+        normalized = (x_ref[here, :].astype(jnp.float32) - stats_ref[here, 0:1]) * inv_std
+        upstream = gy_ref[here, :].astype(jnp.float32) * stats_ref[here, 2:3]
+        change = gained_ref[here, :] - terms[:, 0:1] - normalized * terms[:, 1:2]
+        dx_ref[here, :] = upstream + inv_std * change
+    onward += fetch([(dx_ref, dx_out)], dx_sem)
+    qkv.run()
+    out.run()
+    update_vectors(
+        sums, (qkv_state, out_state, norm_state), up_state, params_out, stats_out, up_out, up_stat_out
+    )
     for copy in onward:
         copy.wait()
 
 
-def statistics_step(owned, stats, passed):
+def attention_weights_step(blocks, qkv, out, sums, states, norm, passed):
     exact = jnp.float32
     low = jnp.bfloat16
-    spaces = {"h": pl.BlockSpec(memory_space=pl.ANY), "v": pl.BlockSpec(memory_space=pltpu.VMEM)}
-    depth = owned[0].shape[0]
-    sizes = [stats[0].shape[-1], stats[3].shape[-1], stats[4].shape[-1]]
-    shapes = [jax.ShapeDtypeStruct(array.shape, array.dtype) for array in passed]
-    scratch = [pltpu.VMEM(array.shape, array.dtype) for array in passed]
-    shapes += [jax.ShapeDtypeStruct(array.shape[1:], exact) for array in stats]
-    averages = [pltpu.VMEM((depth, size), low) for size in sizes]
-    for size in sizes:
-        averages += [pltpu.VMEM((SLOTS, min(STREAM, size), size), exact) for _ in range(2)]
-    averages += [
-        pltpu.SemaphoreType.DMA((3, 2, SLOTS)),
-        pltpu.SemaphoreType.DMA((2, len(passed))),
-    ]
+    depth = blocks[0].shape[0]
+    sizes = (qkv[1].shape[-1], out[0].shape[-1])
     count = len(passed)
-
-    def kernel(*refs):
-        inputs, rest = (refs[: 8 + count], refs[8 + count :])
-        targets, rest = (rest[:count], rest[count:])
-        stats_new, rest = (rest[:6], rest[6:])
-        statistics_kernel(count, *inputs, *targets, *rest[:count], *stats_new, *rest[count:])
-
-    return pl.pallas_call(
-        kernel,
-        in_specs=[spaces[place] for place in "vv" + "hvvhhv" + "h" * count],
-        out_specs=[spaces[place] for place in "h" * count + "hvvhhv"],
-        out_shape=shapes,
-        scratch_shapes=scratch + averages,
-        compiler_params=pltpu.CompilerParams(vmem_limit_bytes=VMEM_LIMIT),
-        cost_estimate=pl.CostEstimate(
-            flops=1 << 33, bytes_accessed=sum(array.size * 4 for array in stats), transcendentals=0
-        ),
-        name="statistics",
-    )(*owned, *stats, *passed)
-
-
-def last_kernel(
+    piece = states[0].shape[2]
+    up_piece = states[3].shape[1]
+    return local_call(
+        functools.partial(attention_weights_kernel, count),
+        blocks + qkv + out + (sums,) + states + norm + passed,
+        "vvv" + "vhh" + "hvh" + "v" + "vvvv" + "vvvvv" + "h" * count,
+        [(array.shape, array.dtype) for array in passed]
+        + [
+            (qkv[0].shape[1:], exact),
+            (qkv[1].shape[1:], exact),
+            (qkv[2].shape, exact),
+            (out[0].shape[1:], exact),
+            (out[1].shape[1:], exact),
+            (out[2].shape, exact),
+            ((7, piece), exact),
+            ((7, piece), exact),
+            ((1, up_piece), exact),
+            ((1, up_piece), exact),
+            (norm[0].shape, exact),
+        ],
+        "h" * count + "vhh" + "hvh" + "vvvv" + "h",
+        [
+            pltpu.VMEM((depth, sizes[0]), low),
+            pltpu.VMEM((depth, sizes[1]), low),
+            pltpu.VMEM((depth, sizes[0]), low),
+            pltpu.VMEM(norm[0].shape, exact),
+            pltpu.SemaphoreType.DMA((1,)),
+        ]
+        + [pltpu.VMEM(array.shape, array.dtype) for array in passed]
+        + [pltpu.SemaphoreType.DMA((2, count))]
+        + unit_scratch(depth, sizes[0], True)
+        + unit_scratch(depth, sizes[1], False),
+        "attention_weights",
+    )
+
+
+def up_kernel(
     own_ref,
     rising_ref,
     falling_ref,
-    up_left,
-    up_right,
-    w_up,
-    up_left_new,
-    up_right_new,
-    w_up_new,
-    low_up,
+    small,
+    stats,
+    master,
+    earlier,
+    small_out,
+    stats_out,
+    master_out,
+    grad,
     first,
-    up_in,
-    up_new,
-    root_in,
-    side_in,
-    side_new,
-    sems,
+    *scratch,
 ):
-    unit = Updater(
-        low_up,
-        up_right,
-        up_right_new,
-        (up_in, up_new),
-        sems,
-        first,
-        w_up,
-        w_up_new,
-        (root_in, side_in, side_new),
-    )
-    prime(unit.tiles, unit.loads)
-    low_up[...] = summed(own_ref[...], rising_ref[...], falling_ref[...]).astype(jnp.bfloat16)
-    root = up_left[1, 0, 0].astype(jnp.bfloat16)
-    first[...] = contract(root, low_up[...], 1, 0).astype(jnp.bfloat16)
-    average_small(up_left, up_left_new, low_up)
+    *buffers, sems = scratch
+    unit = WideUnit(
+        grad, stats, stats_out, buffers, sems, first, small, small_out, master, master_out
+    )
+    unit.start()
+    grad[...] = summed(own_ref[...], rising_ref[...], falling_ref[...]).astype(jnp.bfloat16)
+    unit.prepare()
     unit.run()
 
 
-def last_step(blocks, up_left, up_right, w_up):
+def up_step(blocks, left, right, master, earlier):
     exact = jnp.float32
-    low = jnp.bfloat16
-    spaces = {"h": pl.BlockSpec(memory_space=pl.ANY), "v": pl.BlockSpec(memory_space=pltpu.VMEM)}
-    depth, columns = w_up.shape
-    tile_rows = min(STREAM, columns)
-    return pl.pallas_call(
-        last_kernel,
-        in_specs=[spaces[place] for place in "vvvvhh"],
-        out_specs=[spaces[place] for place in "vhh"],
-        out_shape=[
-            jax.ShapeDtypeStruct(up_left.shape[1:], exact),
-            jax.ShapeDtypeStruct(up_right.shape[1:], exact),
-            jax.ShapeDtypeStruct(w_up.shape, exact),
-        ],
-        scratch_shapes=[
-            pltpu.VMEM((depth, columns), low),
-            pltpu.VMEM((depth, columns), low),
-            pltpu.VMEM((SLOTS, tile_rows, columns), exact),
-            pltpu.VMEM((SLOTS, tile_rows, columns), exact),
-            pltpu.VMEM((SLOTS, columns, tile_rows), exact),
-            pltpu.VMEM((SLOTS, depth, tile_rows), exact),
-            pltpu.VMEM((SLOTS, depth, tile_rows), exact),
-            pltpu.SemaphoreType.DMA((5, SLOTS)),
-        ],
-        compiler_params=pltpu.CompilerParams(vmem_limit_bytes=VMEM_LIMIT),
-        cost_estimate=pl.CostEstimate(
-            flops=1 << 33, bytes_accessed=12 * columns * columns, transcendentals=0
-        ),
-        name="last_weight",
-    )(*blocks, up_left, up_right, w_up)
-
-
-def vector_update(state, grad):
-    stat_new = 0.5 * state[1] + 0.5 * grad * grad
-    param_new = state[0] - vector_rate * grad * lax.rsqrt(stat_new)
-    return (param_new, stat_new)
+    depth, columns = master.shape
+    return local_call(
+        up_kernel,
+        blocks + (left, right, master, earlier),
+        "vvvvhhh",
+        [(left.shape[1:], exact), (right.shape[1:], exact), (master.shape, exact)],
+        "vhh",
+        [pltpu.VMEM((depth, columns), jnp.bfloat16) for _ in range(2)]
+        + unit_scratch(depth, columns, True),
+        "up_weight",
+    )
 
 
 def local(
@@ -2061,7 +2096,7 @@
         piece,
         field_row,
     )
-    grad_hidden, ready_up, owned_qkvo, vector_four, output = fourth_step(
+    grad_hidden, ready_up, *sends, vector_four, output = fourth_step(
         ready_qkvo,
         normed,
         grad_rows,
@@ -2075,7 +2110,18 @@
         piece,
         field_row,
     )
-    input_grad, up_send, down_send, up_own, sums, new_w_down, new_planes, new_w_out = fifth_step(
+    steps = range(dp_size - 2)
+
+    def last_hop(up_send, down_send, own):
+        rising = lax.ppermute(up_send, "dp", [(place, place + 2) for place in steps])
+        falling = lax.ppermute(down_send, "dp", [(place + 2, place) for place in steps])
+        return (own, rising, falling)
+
+    blocks_qkvo = last_hop(*sends)
+    down_left_new, down_right_new, new_w_down = down_step(
+        owned_down, down_left, down_right, w_down, ready_up
+    )
+    gained, terms, *sends, sums = fifth_step(
         ready_up,
         grad_hidden,
         grad_projected,
@@ -2087,54 +2133,38 @@
         spread,
         vector_three,
         vector_four,
-        owned_down,
-        owned_qkvo,
-        (down_left, down_right, w_down),
+        (down_right_new,) + blocks_qkvo[1:],
+        piece,
+    )
+    blocks_up = last_hop(*sends)
+    (
+        output,
+        qkv_left_new,
+        qkv_right_new,
+        new_planes,
+        out_left_new,
+        out_right_new,
+        new_w_out,
+        new_vector_params,
+        new_vector_stats,
+        new_up_bias,
+        new_up_stat,
+        input_grad,
+    ) = attention_weights_step(
+        blocks_qkvo,
         (qkv_left, qkv_right, planes),
         (out_left, out_right, w_out),
-        piece,
-    )
-    steps = range(dp_size - 2)
-    rising = lax.ppermute(up_send, "dp", [(place, place + 2) for place in steps])
-    falling = lax.ppermute(down_send, "dp", [(place + 2, place) for place in steps])
-    (
-        output,
-        input_grad,
-        new_w_down,
-        new_planes,
-        new_w_out,
-        down_left_new,
-        down_right_new,
-        qkv_left_new,
-        qkv_right_new,
-        out_left_new,
-        out_right_new,
-    ) = statistics_step(
-        (owned_down, owned_qkvo),
-        (down_left, down_right, qkv_left, qkv_right, out_left, out_right),
-        (output, input_grad, new_w_down, new_planes, new_w_out),
-    )
-    up_left_new, up_right_new, new_w_up = last_step(
-        (up_own, rising, falling), up_left, up_right, w_up
+        sums,
+        (qkv_bias_state, out_bias_state, ln_state, up_bias_state),
+        (tokens, cotangent, stats, gained, terms),
+        (output,),
     )
     new_w_qkv = new_planes.transpose(1, 0, 2)
-
-    dp_place = lax.axis_index("dp")
-
-    def mine(values, count):
-        return take(values.reshape(count, dp_size, -1), dp_place, 1)
-
-    owned_bqkv = mine(sums[0, : 3 * own_width], 3)
-    owned_bup = mine(sums[1], 1)[0]
-    owned_norm = jnp.concatenate([mine(sums[2, :share_width], 1), mine(sums[3, :share_width], 1)])
-    bias_total = mine(sums[4, :share_width], 1)
-    owned_obias = jnp.concatenate([bias_total, bias_total])
-    qkv_params, qkv_stats = vector_update(qkv_bias_state, owned_bqkv)
-    obias_params, obias_stats = vector_update(out_bias_state, owned_obias)
-    norm_new_params, norm_new_stats = vector_update(ln_state, owned_norm)
-    new_up_bias, new_up_stat = vector_update(up_bias_state, owned_bup)
-    new_vector_params = jnp.concatenate([qkv_params, obias_params, norm_new_params], axis=0)
-    new_vector_stats = jnp.concatenate([qkv_stats, obias_stats, norm_new_stats], axis=0)
+    up_left_new, up_right_new, new_w_up = up_step(
+        blocks_up, up_left, up_right, w_up, new_vector_params
+    )
+    new_up_bias = new_up_bias.reshape(-1)
+    new_up_stat = new_up_stat.reshape(-1)
     return (
         output,
         input_grad,

time: 488 us -> 466 us (0.955)
  Pallas kernels: 461 us -> 434 us
  waiting for transfers between devices: 0.01 us -> 5.69 us
    pallas_call x4, Pallas kernels: 409 us -> 370 us  [carrying(): pl.pallas_call(kernel, in_specs=[spaces[place] for place in in_places], o...]
    pallas_call x2 -> x3, Pallas kernels: 51.6 us -> 64.5 us  [local_call(): pl.pallas_call(kernel, in_specs=[spaces[place] for place in in_places], o...]
    ppermute x2 -> x4, waiting for transfers between devices: 0.01 us -> 5.69 us  [the longest x2 5.68 us: last_hop(): lax.ppermute(down_send, 'dp', [(place + 2, place) for place in steps])]
  transfers between devices with their start and end apart: 2 -> 4, of which waited for: 0 -> 2; matrix products, arithmetic and copies ran while one was open for 1% -> 0% of each run, Pallas kernels for 6% -> 9%
where the time goes in v4:
time: 466 us; the launch traced here: 458 us
  Pallas kernels  434 us (93%)
  starting transfers between devices  8.53 us (2%)
  local copies, waits for them, and re-layouts  7.69 us (2%)
  waiting for transfers between devices  5.69 us (1%)
    pallas_call x4, Pallas kernels, carrying(): pl.pallas_call(kernel, in_specs=[spaces[place] for place in in_places], o...  370 us
    pallas_call x3, Pallas kernels, local_call(): pl.pallas_call(kernel, in_specs=[spaces[place] for place in in_places], o...  64.5 us
  transfers between devices with their start and end apart: 4, of which 2 were waited for; matrix products, arithmetic and copies ran while one was open for 0% of the time, Pallas kernels for 9%

profile of v4, /device:TPU:0, one launch (start us, length us, event | category | flops | bytes accessed | tf_op | source)
XLA Modules:
  0.0 458.1 jit_solution(10792364369909549900)
XLA Ops:
  0.7 0.7 copy.40
  1.4 0.1 reduce.2
  1.6 0.7 fusion.9
  2.3 0.1 reshape_squeeze.9
  2.3 0.7 slice.32
  3.0 0.1 reshape_squeeze.10
  3.1 0.7 slice.33
  3.8 0.1 reshape.84
  3.9 0.7 fusion.12
  4.6 0.7 copy.41.ends_col_ref
  5.3 0.1 fusion.11
  5.4 0.6 fusion.6.small_ref
  6.0 0.6 broadcast_in_dim.20.ends_ref
  6.6 152.6 %gathers_beside_hidden.1 = (bf16[256,2048]{1,0:T(8,128)(2,1)}, bf16[2048,2048]{1,0:T(8,128)(2,1)}, bf16[2048,2048]{1,0:T(8,128)(2,1)}, bf16[1024,2048]{1,0:T(8,1...) custom-call(f32[256,2048]{1,0:T(8,128)} %master.3, ...), custom_call_target="tpu_custom_call" | custom-call | flops 17179869184 | bytes 33554432 | tf_op jit(solution)/shard_map/gathers_beside_hidden/pallas_call | solution.py:759
  159.2 107.3 %lines_beside_attention.1 = (bf16[2048,2048]{1,0:T(8,128)(2,1)}, bf16[1024,1536]{1,0:T(8,128)(2,1)}, bf16[1024,512]{1,0:T(8,128)(2,1)}, bf16[4,256,2048]{2,1,0:T...) custom-call(bf16[256,2048]{1,0:T(8,128)(2,1)} %get-tuple-element.65.block_ref, ...), custom_call_target="tpu_custom_call" | custom-call | flops 23622320128 | bytes 33554432 | tf_op jit(solution)/shard_map/lines_beside_attention/pallas_call | solution.py:759
  266.5 55.7 %line_beside_hidden_grad.1 = (bf16[1024,2048]{1,0:T(8,128)(2,1)}, bf16[4,256,2048]{2,1,0:T(8,128)(2,1)}, bf16[256,2048]{1,0:T(8,128)(2,1)}, bf16[256,2048]{1,0:T...) custom-call(bf16[4,256,2048]{2,1,0:T(8,128)(2,1)} %get-tuple-element.71.ready_hbm, ...), custom_call_target="tpu_custom_call" | custom-call | flops 25769803776 | bytes 33554432 | tf_op jit(solution)/shard_map/line_beside_hidden_grad/pallas_call | solution.py:759
  322.2 2.5 collective-permute-start
  324.8 1.3 collective-permute-start.1
  326.1 20.7 %down_weight.1 = (f32[1,1,2048,2048]{3,2,1,0:T(8,128)}, f32[1,1,256,256]{3,2,1,0:T(8,128)}, f32[2048,256]{1,0:T(8,128)}) custom-call(bf16[256,2048]{1,0:T(8,128)(2,1)} %get-tuple-element.86.grad, f32[2,1,1,2048,2048]{4,3,2,1,0:T(8,128)} %stats.2, f32[2,1,1,256,256]{4,3,2,1,0:T(8,128)} %small.2, f32[2048,256]{1,0:T(8,128)} %master.2, ...), custom_call_target="tpu_custom_call" | custom-call | flops 8589934592 | bytes 67108864 | tf_op jit(solution)/shard_map/down_weight/pallas_call | solution.py:1767
  346.8 0.0 collective-permute-done.earlier_rising.rising_ref
  346.8 0.0 copy-start
  346.8 2.9 collective-permute-done.1.earlier_falling.falling_ref
  349.7 1.0 copy-done.1
  350.7 54.1 %line_beside_norm_grad.1 = (f32[1024,512]{1,0:T(8,128)}, f32[8,1024]{1,0:T(8,128)}, bf16[256,2048]{1,0:T(8,128)(2,1)}, bf16[256,2048]{1,0:T(8,128)(2,1)}, bf16[256,2048]{1,0:T(8,128)(2,1)}, /*index=5*/f32[8,2048]{1,0:T(8,128)}) custom-call(bf16[4,256,2048]{2,1,0:T(8,128)(2,1)} %get-tuple-element.79.earlier.ready_hbm, ...), custom_call_target="tpu_custom_call" | custom-call | flops 17179869184 | bytes 33554432 | tf_op jit(solution)/shard_map/line_beside_norm_grad/pallas_call | solution.py:759
  404.8 3.4 collective-permute-start.2
  408.2 1.3 collective-permute-start.3
  409.6 0.6 copy.42.qkv_state
  410.1 22.3 %attention_weights.1 = (bf16[1024,512]{1,0:T(8,128)(2,1)}, f32[1,1,256,256]{3,2,1,0:T(8,128)}, f32[1,1,1536,1536]{3,2,1,0:T(8,128)}, f32[3,256,512]{2,1,0:T(8,12...) custom-call(bf16[256,2048]{1,0:T(8,128)(2,1)} %get-tuple-element.76., ...), custom_call_target="tpu_custom_call" | custom-call | flops 8589934592 | bytes 67108864 | tf_op jit(solution)/shard_map/attention_weights/pallas_call | solution.py:1767
  432.5 0.0 collective-permute-done.2.rising_ref
  432.5 2.8 collective-permute-done.3.falling_ref
  435.2 1.0 copy-done.3
  436.3 21.5 %up_weight.1 = (f32[1,1,256,256]{3,2,1,0:T(8,128)}, f32[1,1,2048,2048]{3,2,1,0:T(8,128)}, f32[256,2048]{1,0:T(8,128)}) custom-call(bf16[256,2048]{1,0:T(8,128)(2,1)} %get-tuple-element.96.own_ref, bf16[256,2048]{1,0:T(8,128)(2,1)} %copy-done.2, bf16[256,2048]{1,0:T(8,128)(2,1)} %copy-done.3, f32[2,1,1,256,256]{4,3,2,1,0:T(8,128)} %small.3, ...), custom_call_target="tpu_custom_call" | custom-call | flops 8589934592 | bytes 67108864 | tf_op jit(solution)/shard_map/up_weight/pallas_call | solution.py:1767
  (9 shorter events, 0.1 us)
Async XLA Ops:
  322.2 24.5 %collective-permute-start = (bf16[256,2048]{1,0:T(8,128)(2,1)}, bf16[256,2048]{1,0:T(8,128)(2,1)S(1)}, u32[]{:S(2)}, u32[]{:S(2)}) collective-permute-start(bf16[256,2048]{1,0:T(8,128)(2,1)} %get-tuple-element.77), channel_id=1, source_target_pairs={{0,2},{1,3},{2,4},{3,5},{4,6},{5,7},{8,10},{9,11},{10,12},{11,13},... | collective-permute-start | bytes 3145736 | tf_op jit(solution)/shard_map/ppermute | solution.py:2116
  324.8 24.9 %collective-permute-start.1 = (bf16[256,2048]{1,0:T(8,128)(2,1)}, bf16[256,2048]{1,0:T(8,128)(2,1)S(1)}, u32[]{:S(2)}, u32[]{:S(2)}) collective-permute-start(bf16[256,2048]{1,0:T(8,128)(2,1)} %get-tuple-element.78), channel_id=1, source_target_pairs={{2,0},{3,1},{4,2},{5,3},{6,4},{7,5},{10,8},{11,9},{12,10},{13,11},... | collective-permute-start | bytes 3145736 | tf_op jit(solution)/shard_map/ppermute | solution.py:2117
  346.8 2.9 copy-start
  349.7 1.0 copy-start.1
  350.7 58.9 %copy-start.4 = (f32[2,3,64]{2,0,1:T(2,128)S(1)}, f32[2,3,64]{2,0,1:T(2,128)}, u32[]{:S(2)}) copy-start(f32[2,3,64]{2,0,1:T(2,128)} %param.23) | copy-start | bytes 4612
  404.8 27.6 %collective-permute-start.2 = (bf16[256,2048]{1,0:T(8,128)(2,1)}, bf16[256,2048]{1,0:T(8,128)(2,1)S(1)}, u32[]{:S(2)}, u32[]{:S(2)}) collective-permute-start(bf16[256,2048]{1,0:T(8,128)(2,1)} %get-tuple-element.97), channel_id=1, source_target_pairs={{0,2},{1,3},{2,4},{3,5},{4,6},{5,7},{8,10},{9,11},{10,12},{11,13},... | collective-permute-start | bytes 3145736 | tf_op jit(solution)/shard_map/ppermute | solution.py:2116
  408.2 27.0 %collective-permute-start.3 = (bf16[256,2048]{1,0:T(8,128)(2,1)}, bf16[256,2048]{1,0:T(8,128)(2,1)S(1)}, u32[]{:S(2)}, u32[]{:S(2)}) collective-permute-start(bf16[256,2048]{1,0:T(8,128)(2,1)} %get-tuple-element.98), channel_id=1, source_target_pairs={{2,0},{3,1},{4,2},{5,3},{6,4},{7,5},{10,8},{11,9},{12,10},{13,11},... | collective-permute-start | bytes 3145736 | tf_op jit(solution)/shard_map/ppermute | solution.py:2117
  432.5 2.8 copy-start.2
  435.2 1.0 copy-start.3

commit v5 on v4

--- a/solution.py
+++ b/solution.py
@@ -25,6 +25,18 @@
     segment = jnp.sum(jnp.where(finished, 1, 0), axis=axis, keepdims=True)
     starting = jnp.max(jnp.where(finished, ends, 0), axis=axis, keepdims=True)
     return (segment, starting, segment < slots)
+
+
+def ends_of(lengths, padded):
+    slots = lengths.shape[1]
+    padded[...] = jnp.zeros_like(padded)
+    padded[0:1, pl.ds(0, slots)] = lengths[...].astype(jnp.float32)
+    shape = (LANES, LANES)
+    slot = lax.broadcasted_iota(jnp.int32, shape, 0)
+    before = lax.broadcasted_iota(jnp.int32, shape, 1) <= slot
+    ends = jnp.sum(jnp.where(before, padded[0:1, :], 0.0), axis=1, keepdims=True)
+    ends = jnp.where(slot < slots, ends, 1e9)
+    return (jnp.transpose(ends)[0:1, :].astype(jnp.int32), ends[:, 0:1].astype(jnp.int32))
 
 
 def rope_tables(offsets):
@@ -492,22 +504,55 @@
     return groups
 
 
+def round_matrix(source, target):
+    size = source.shape[0]
+    tile_rows = min(STREAM, size)
+
+    def scope(before, after, sems):
+        def where(tile):
+            return pl.ds(pl.multiple_of(tile * tile_rows, tile_rows), tile_rows)
+
+        def loads(tile, slot):
+            return [
+                pltpu.make_async_copy(source.at[where(tile), :], before.at[slot], sems.at[0, slot])
+            ]
+
+        def stores(tile, slot):
+            return [
+                pltpu.make_async_copy(after.at[slot], target.at[where(tile), :], sems.at[1, slot])
+            ]
+
+        def compute(tile, slot):
+            after[slot] = before[slot].astype(after.dtype)
+
+        stream(size // tile_rows, loads, stores, compute)
+
+    shape = (SLOTS, tile_rows, size)
+    pl.run_scoped(
+        scope,
+        pltpu.VMEM(shape, source.dtype),
+        pltpu.VMEM(shape, target.dtype),
+        pltpu.SemaphoreType.DMA((2, SLOTS)),
+    )
+
+
 def cast_rows(source, target, here):
     target[here, :] = source[here, :].astype(target.dtype)
 
 
 def first_kernel(
-    piece,
-    up_piece,
-    slots,
     w_up_ref,
     w_qkv_hbm,
     w_out_hbm,
     w_down_hbm,
     x_ref,
     gy_ref,
-    small_ref,
-    ends_ref,
+    norm_state,
+    qkv_state,
+    out_state,
+    up_state,
+    lengths_ref,
+    right_ref,
     turned_out,
     full_ref,
     next_full,
@@ -518,6 +563,7 @@
     act_out,
     slope_out,
     sums_out,
+    right_low,
     gather_send,
     gather_recv,
     next_send,
@@ -545,11 +591,16 @@
     w_qkv_ref,
     w_out_ref,
     w_down_ref,
+    small_ref,
+    padded_ref,
 ):
     loads = fetch(
         [(w_qkv_hbm, w_qkv_ref), (w_out_hbm, w_out_ref), (w_down_hbm, w_down_ref)],
         local_sems.at[pl.ds(6, 3)],
     )
+    piece = norm_state.shape[2]
+    up_piece = up_state.shape[1]
+    slots = lengths_ref.shape[1]
     columns = lax.axis_size("dp")
     total = columns * lax.axis_size("mp")
     mp_place = lax.axis_index("mp")
@@ -566,6 +617,21 @@
 
     lax.fori_loop(1, total, greet, 0)
     by_rows(block_ref.shape[0], 64, lambda here: cast_rows(w_up_ref, block_ref, here))
+    small_ref[...] = jnp.zeros_like(small_ref)
+    up_rows = -(-up_piece // LANES)
+
+    def note(first_row, offset, values):
+        values = values.astype(jnp.bfloat16).astype(jnp.float32)
+        row, lane = divmod(offset, LANES)
+        small_ref[0, first_row + row : first_row + row + 1, pl.ds(lane, values.shape[1])] = values
+
+    for kind in range(2):
+        note(0, kind * piece, norm_state[0, kind : kind + 1, :])
+        note(1 + up_rows, (3 + kind) * piece, out_state[0, kind : kind + 1, :])
+    for kind in range(3):
+        note(1 + up_rows, kind * piece, qkv_state[kind, 0:1, :])
+    for first in range(0, up_piece, LANES):
+        note(1, first, up_state[0:1, first : min(first + LANES, up_piece)])
     pl.semaphore_wait(barrier, total - 1)
 
     def small_copy(step):
@@ -613,15 +679,19 @@
 
     by_rows(w_down_ref.shape[0], depth, turn_down)
 
+    ends_row, _ = ends_of(lengths_ref, padded_ref)
+
     def mark(here):
         ids = lax.broadcasted_iota(jnp.int32, (ROW_TILE, 1), 0) + here.start
-        valid = segment_of(ends_ref[0:1, :], ids, 1, slots)[2]
+        valid = segment_of(ends_row, ids, 1, slots)[2]
         valid_ref[here, :] = jnp.where(valid, 1.0, 0.0)
 
     by_rows(rows, ROW_TILE, mark)
     lax.fori_loop(1, total, end, 0)
     weight.advance(1)
+    round_matrix(right_ref.at[0, 0, 0], right_low.at[0, 0, 0])
     weight.advance(2)
+    round_matrix(right_ref.at[1, 0, 0], right_low.at[1, 0, 0])
     rows_x.forward()
     rows_gy.forward()
     weight.advance(3, 0, 1)
@@ -693,7 +763,7 @@
         store.wait()
 
 
-def first_step(weights, tokens, cotangent, small, ends, slots, piece, up_piece):
+def first_step(weights, tokens, cotangent, states, lengths, right):
     mp_size, dp_size = (lax.axis_size("mp"), lax.axis_size("dp"))
     count = dp_size // 2
     rows = tokens.shape[0]
@@ -702,23 +772,24 @@
     total = mp_size * dp_size
     low = jnp.bfloat16
     return carrying(
-        functools.partial(first_kernel, piece, up_piece, slots),
+        first_kernel,
         1,
-        weights + (tokens, cotangent, small, ends),
-        "vhhhhhvv",
+        weights + (tokens, cotangent) + states + (lengths, right),
+        "vhhhhhvvvvvh",
         [
             ((part, columns), low),
             ((part * dp_size, columns), low),
             ((part * dp_size, columns), low),
             (wide, low),
             (wide, low),
-            ((total,) + small.shape[1:], jnp.float32),
+            ((total, 8, LANES), jnp.float32),
             ((rows, LANES), jnp.float32),
             ((rows, columns), low),
             ((rows, columns), low),
             ((count, part, columns), low),
+            (right.shape, low),
         ],
-        "vhhhhvvhhh",
+        "vhhhhvvhhhh",
         gather_sems()
         + gather_sems()
         + block_sems()
@@ -738,7 +809,8 @@
             pltpu.VMEM(wide, low),
             pltpu.VMEM((count, part, columns), low),
         ]
-        + [pltpu.VMEM(weight.shape, weight.dtype) for weight in weights[1:]],
+        + [pltpu.VMEM(weight.shape, weight.dtype) for weight in weights[1:]]
+        + [pltpu.VMEM((1, 8, LANES), jnp.float32), pltpu.VMEM((8, LANES), jnp.float32)],
         4 * rows * wide[1] * columns,
         "gathers_beside_hidden",
     )
@@ -781,7 +853,6 @@
 
 def third_kernel(
     head_cols,
-    slots,
     piece,
     field_row,
     block_ref,
@@ -790,8 +861,7 @@
     gy_hbm,
     weight_hbm,
     spread_ref,
-    ends_ref,
-    ends_col_ref,
+    lengths_ref,
     full_ref,
     grad_out,
     or_out,
@@ -824,6 +894,7 @@
     ahead_ref,
     behind_ref,
     sums_ref,
+    padded_ref,
 ):
     loads = [
         pltpu.make_async_copy(source, target, local_sems.at[index])
@@ -847,15 +918,17 @@
     rows = xn_ref.shape[0]
     tiles = rows // ROW_TILE
     scale = HEAD_DIM ** (-0.5)
+    slots = lengths_ref.shape[1]
+    ends_row, ends_col = ends_of(lengths_ref, padded_ref)
     row_positions = lax.broadcasted_iota(jnp.int32, (1, rows), 1)
-    seg_row, _, row_valid = segment_of(ends_col_ref[...], row_positions, 0, slots)
+    seg_row, _, row_valid = segment_of(ends_col, row_positions, 0, slots)
     seg_row = jnp.where(row_valid, seg_row, slots + row_positions)
     for tile in range(tiles):
         here = pl.ds(tile * ROW_TILE, ROW_TILE)
         reach = (tile + 1) * ROW_TILE
         shape = (ROW_TILE, reach)
         ids = lax.broadcasted_iota(jnp.int32, (ROW_TILE, 1), 0) + tile * ROW_TILE
-        seg_col, starting, valid = segment_of(ends_ref[0:1, :], ids, 1, slots)
+        seg_col, starting, valid = segment_of(ends_row, ids, 1, slots)
         seg_col = jnp.where(valid, seg_col, slots + ids)
         tables = rope_tables((ids - starting).astype(jnp.float32))
         for ref, table in zip((keep_ref, ahead_ref, behind_ref), tables):
@@ -979,7 +1052,7 @@
 
 
 def third_step(
-    block, ready, normed, grad_rows, full_qkvo, spread, ends, ends_col, slots, piece, field_row
+    block, ready, normed, grad_rows, full_qkvo, spread, lengths, piece, field_row
 ):
     rows, width = normed.shape
     count = lax.axis_size("dp") // 2
@@ -988,7 +1061,7 @@
     part = width // (2 * count)
     low = jnp.bfloat16
     return carrying(
-        functools.partial(third_kernel, head_cols, slots, piece, field_row),
+        functools.partial(third_kernel, head_cols, piece, field_row),
         5,
         (
             block,
@@ -997,10 +1070,9 @@
             grad_rows,
             full_qkvo,
             spread,
-            ends,
-            ends_col,
+            lengths,
         ),
-        "hhhhhvvv",
+        "hhhhhvv",
         [
             ((width, block.shape[1]), low),
             ((rows, 3 * head_cols), low),
@@ -1031,6 +1103,7 @@
             pltpu.VMEM((rows, LANES), jnp.float32),
             pltpu.VMEM((rows, LANES), jnp.float32),
             pltpu.VMEM((count, part, columns), low),
+            pltpu.VMEM((8, LANES), jnp.float32),
         ],
         4 * rows * width * columns + 12 * rows * rows * head_cols,
         "lines_beside_attention",
@@ -1692,7 +1765,7 @@
 
     def compute(self, tile, slot):
         product = contract(self.grad[:, self.where(tile)], self.grad[...], 0, 0)
-        self.stat_new[slot] = 0.5 * self.stat_in[slot] + 0.5 * product
+        self.stat_new[slot] = 0.5 * self.stat_in[slot].astype(jnp.float32) + 0.5 * product
         step = self.step(self.root_in[slot].astype(jnp.bfloat16))
         self.side_new[slot] = self.side_in[slot] - matrix_rate * step
 
@@ -1751,13 +1824,14 @@
     small_out[0, 0] = 0.5 * small[0, 0, 0] + 0.5 * contract(grad[...], grad[...], 1, 1)
 
 
-def unit_scratch(depth, size, wide):
+def unit_scratch(depth, size, wide, source=jnp.float32):
     tile_rows = min(STREAM, size)
     exact = jnp.float32
     root = (size, tile_rows) if wide else (tile_rows, size)
     side = (depth, tile_rows) if wide else (tile_rows, depth)
     shapes = [(tile_rows, size), (tile_rows, size), root, side, side]
-    return [pltpu.VMEM((SLOTS,) + shape, exact) for shape in shapes] + [
+    types = [source, exact, source, exact, exact]
+    return [pltpu.VMEM((SLOTS,) + shape, kind) for shape, kind in zip(shapes, types)] + [
         pltpu.SemaphoreType.DMA((5, SLOTS))
     ]
 
@@ -1805,19 +1879,24 @@
     columns = sums.shape[1]
     place = lax.axis_index("dp")
     qkv_state, out_state, norm_state = states
-    piece = qkv_state.shape[2]
+    piece = norm_state.shape[2]
     stride = lax.axis_size("dp") * piece
     own = pltpu.roll(sums[...], lax.rem(columns - place * piece, columns), 1)
-    picks = [(qkv_state, kind, own[0:1, kind * stride : kind * stride + piece]) for kind in range(3)]
-    picks += [(out_state, kind, own[4:5, :piece]) for kind in range(2)]
-    picks += [(norm_state, kind, own[2 + kind : 3 + kind, :piece]) for kind in range(2)]
+    picks = [
+        (qkv_state[kind, 0:1, :], qkv_state[kind, 1:2, :], own[0:1, kind * stride : kind * stride + piece])
+        for kind in range(3)
+    ]
+    for state, rows in ((out_state, (4, 4)), (norm_state, (2, 3))):
+        for kind, row in enumerate(rows):
+            param, stat = (state[0, kind : kind + 1, :], state[1, kind : kind + 1, :])
+            picks.append((param, stat, own[row : row + 1, :piece]))
 
     def update(param, stat, grad):
         stat_new = 0.5 * stat + 0.5 * grad * grad
         return (param - vector_rate * grad * lax.rsqrt(stat_new), stat_new)
 
-    for row, (state, kind, grad) in enumerate(picks):
-        param, stat = update(state[0, kind : kind + 1, :], state[1, kind : kind + 1, :], grad)
+    for row, (param, stat, grad) in enumerate(picks):
+        param, stat = update(param, stat, grad)
         params_out[row : row + 1, :] = param
         stats_out[row : row + 1, :] = stat
     piece = up_state.shape[1]
@@ -1935,7 +2014,7 @@
     depth = blocks[0].shape[0]
     sizes = (qkv[1].shape[-1], out[0].shape[-1])
     count = len(passed)
-    piece = states[0].shape[2]
+    piece = states[2].shape[2]
     up_piece = states[3].shape[1]
     return local_call(
         functools.partial(attention_weights_kernel, count),
@@ -2006,7 +2085,7 @@
         [(left.shape[1:], exact), (right.shape[1:], exact), (master.shape, exact)],
         "vhh",
         [pltpu.VMEM((depth, columns), jnp.bfloat16) for _ in range(2)]
-        + unit_scratch(depth, columns, True),
+        + unit_scratch(depth, columns, True, right.dtype),
         "up_weight",
     )
 
@@ -2042,25 +2121,8 @@
     piece = ln_state.shape[2]
     up_piece = up_bias_state.shape[1]
 
-    def lane_rows(*values):
-        flat = jnp.concatenate([value.reshape(-1) for value in values])
-        return jnp.pad(flat, (0, -flat.shape[0] % LANES)).reshape(-1, LANES)
-
-    small = jnp.concatenate(
-        [
-            lane_rows(ln_state[0]),
-            lane_rows(up_bias_state[0]),
-            lane_rows(qkv_bias_state[0], out_bias_state[0]),
-        ],
-        axis=0,
-    )
-    up_rows = lane_rows(up_bias_state[0]).shape[0]
-    small = jnp.pad(small, ((0, 8 - small.shape[0]), (0, 0))).astype(jnp.bfloat16)
-    slots = seq_lengths.shape[1]
-    ends = jnp.pad(
-        jnp.cumsum(seq_lengths[0]), (0, LANES - slots), constant_values=2 * row_count
-    ).astype(jnp.int32)
     planes = w_qkv.transpose(1, 0, 2)
+    qkv_states = qkv_bias_state.transpose(1, 0, 2)
     (
         turned_block,
         full_up,
@@ -2072,17 +2134,16 @@
         activated,
         slope,
         ready_down,
+        up_right_low,
     ) = first_step(
         (w_up, planes, w_out, w_down),
         tokens,
         cotangent,
-        small.astype(jnp.float32)[None],
-        jnp.broadcast_to(ends[None, :], (8, LANES)),
-        slots,
-        piece,
-        up_piece,
-    )
-    field_row = 1 + up_rows
+        (ln_state, qkv_states, out_bias_state, up_bias_state),
+        seq_lengths,
+        up_right,
+    )
+    field_row = 1 - (-up_piece // LANES)
     turned_down, grad_projected, attended, ready_qkvo, owned_down, vector_three = third_step(
         turned_block,
         ready_down,
@@ -2090,9 +2151,7 @@
         grad_rows,
         full_qkvo,
         spread,
-        jnp.broadcast_to(ends[None, :], (8, LANES)),
-        ends[:, None],
-        slots,
+        seq_lengths,
         piece,
         field_row,
     )
@@ -2155,13 +2214,13 @@
         (qkv_left, qkv_right, planes),
         (out_left, out_right, w_out),
         sums,
-        (qkv_bias_state, out_bias_state, ln_state, up_bias_state),
+        (qkv_states, out_bias_state, ln_state, up_bias_state),
         (tokens, cotangent, stats, gained, terms),
         (output,),
     )
     new_w_qkv = new_planes.transpose(1, 0, 2)
     up_left_new, up_right_new, new_w_up = up_step(
-        blocks_up, up_left, up_right, w_up, new_vector_params
+        blocks_up, up_left, up_right_low, w_up, new_vector_params
     )
     new_up_bias = new_up_bias.reshape(-1)
     new_up_stat = new_up_stat.reshape(-1)

time: 466 us -> 456 us (0.979)
  local copies, waits for them, and re-layouts: 7.69 us -> 1.98 us
  transfers between devices with their start and end apart: 4 -> 4, of which waited for: 2 -> 2; matrix products, arithmetic and copies ran while one was open for 0% -> 0% of each run, Pallas kernels for 9% -> 10%
where the time goes in v5:
time: 456 us; the launch traced here: 448 us
  Pallas kernels  430 us (94%)
  starting transfers between devices  8.37 us (2%)
  waiting for transfers between devices  6.19 us (1%)
    pallas_call x4, Pallas kernels, carrying(): pl.pallas_call(kernel, in_specs=[spaces[place] for place in in_places], o...  370 us
    pallas_call x3, Pallas kernels, local_call(): pl.pallas_call(kernel, in_specs=[spaces[place] for place in in_places], o...  59.9 us
  transfers between devices with their start and end apart: 4, of which 2 were waited for; matrix products, arithmetic and copies ran while one was open for 0% of the time, Pallas kernels for 10%

profile of v5, /device:TPU:0, one launch (start us, length us, event | category | flops | bytes accessed | tf_op | source)
XLA Modules:
  0.0 447.6 jit_solution(4654194994996408328)
XLA Ops:
  0.7 152.7 %gathers_beside_hidden.1 = (bf16[256,2048]{1,0:T(8,128)(2,1)}, bf16[2048,2048]{1,0:T(8,128)(2,1)}, bf16[2048,2048]{1,0:T(8,128)(2,1)}, bf16[1024,2048]{1,0:T(8,1...) custom-call(f32[256,2048]{1,0:T(8,128)} %master.3, ...), custom_call_target="tpu_custom_call" | custom-call | flops 17179869184 | bytes 33554432 | tf_op jit(solution)/shard_map/gathers_beside_hidden/pallas_call | solution.py:831
  153.4 107.3 %lines_beside_attention.1 = (bf16[2048,2048]{1,0:T(8,128)(2,1)}, bf16[1024,1536]{1,0:T(8,128)(2,1)}, bf16[1024,512]{1,0:T(8,128)(2,1)}, bf16[4,256,2048]{2,1,0:T...) custom-call(bf16[256,2048]{1,0:T(8,128)(2,1)} %get-tuple-element.66.block_ref, ...), custom_call_target="tpu_custom_call" | custom-call | flops 23622320128 | bytes 33554432 | tf_op jit(solution)/shard_map/lines_beside_attention/pallas_call | solution.py:831
  260.6 55.8 %line_beside_hidden_grad.1 = (bf16[1024,2048]{1,0:T(8,128)(2,1)}, bf16[4,256,2048]{2,1,0:T(8,128)(2,1)}, bf16[256,2048]{1,0:T(8,128)(2,1)}, bf16[256,2048]{1,0:T...) custom-call(bf16[4,256,2048]{2,1,0:T(8,128)(2,1)} %get-tuple-element.72.ready_hbm, ...), custom_call_target="tpu_custom_call" | custom-call | flops 25769803776 | bytes 33554432 | tf_op jit(solution)/shard_map/line_beside_hidden_grad/pallas_call | solution.py:831
  316.5 2.5 collective-permute-start
  319.0 1.3 collective-permute-start.1
  320.3 20.7 %down_weight.1 = (f32[1,1,2048,2048]{3,2,1,0:T(8,128)}, f32[1,1,256,256]{3,2,1,0:T(8,128)}, f32[2048,256]{1,0:T(8,128)}) custom-call(bf16[256,2048]{1,0:T(8,128)(2,1)} %get-tuple-element.87.grad, f32[2,1,1,2048,2048]{4,3,2,1,0:T(8,128)} %stats.1, f32[2,1,1,256,256]{4,3,2,1,0:T(8,128)} %small.2, f32[2048,256]{1,0:T(8,128)} %master.2, ...), custom_call_target="tpu_custom_call" | custom-call | flops 8589934592 | bytes 67108864 | tf_op jit(solution)/shard_map/down_weight/pallas_call | solution.py:1841
  341.0 0.0 collective-permute-done.earlier_rising.rising_ref
  341.0 0.0 copy-start
  341.0 2.9 collective-permute-done.1.earlier_falling.falling_ref
  343.9 0.0 copy-start.1
  343.9 0.0 copy-done
  343.9 1.0 copy-done.1
  344.9 54.3 %line_beside_norm_grad.1 = (f32[1024,512]{1,0:T(8,128)}, f32[8,1024]{1,0:T(8,128)}, bf16[256,2048]{1,0:T(8,128)(2,1)}, bf16[256,2048]{1,0:T(8,128)(2,1)}, bf16[256,2048]{1,0:T(8,128)(2,1)}, /*index=5*/f32[8,2048]{1,0:T(8,128)}) custom-call(bf16[4,256,2048]{2,1,0:T(8,128)(2,1)} %get-tuple-element.80.earlier.ready_hbm, ...), custom_call_target="tpu_custom_call" | custom-call | flops 17179869184 | bytes 33554432 | tf_op jit(solution)/shard_map/line_beside_norm_grad/pallas_call | solution.py:831
  399.2 3.3 collective-permute-start.2
  402.5 1.3 collective-permute-start.3
  403.8 22.4 %attention_weights.1 = (bf16[1024,512]{1,0:T(8,128)(2,1)}, f32[1,1,256,256]{3,2,1,0:T(8,128)}, f32[1,1,1536,1536]{3,2,1,0:T(8,128)}, f32[3,256,512]{2,1,0:T(8,12...) custom-call(bf16[256,2048]{1,0:T(8,128)(2,1)} %get-tuple-element.77., ...), custom_call_target="tpu_custom_call" | custom-call | flops 8589934592 | bytes 67108864 | tf_op jit(solution)/shard_map/attention_weights/pallas_call | solution.py:1841
  426.2 0.0 collective-permute-done.2.rising_ref
  426.2 0.0 copy-start.2
  426.2 3.3 collective-permute-done.3.falling_ref
  429.5 0.0 copy-start.3
  429.5 0.0 copy-done.2
  429.5 1.0 copy-done.3
  430.5 16.8 %up_weight.1 = (f32[1,1,256,256]{3,2,1,0:T(8,128)}, f32[1,1,2048,2048]{3,2,1,0:T(8,128)}, f32[256,2048]{1,0:T(8,128)}) custom-call(bf16[256,2048]{1,0:T(8,128)(2,1)} %get-tuple-element.97.own_ref, bf16[256,2048]{1,0:T(8,128)(2,1)} %copy-done.2, bf16[256,2048]{1,0:T(8,128)(2,1)} %copy-done.3, f32[2,1,1,256,256]{4,3,2,1,0:T(8,128)} %small.3, ...), custom_call_target="tpu_custom_call" | custom-call | flops 8589934592 | bytes 67108864 | tf_op jit(solution)/shard_map/up_weight/pallas_call | solution.py:1841
Async XLA Ops:
  316.5 24.5 %collective-permute-start = (bf16[256,2048]{1,0:T(8,128)(2,1)}, bf16[256,2048]{1,0:T(8,128)(2,1)S(1)}, u32[]{:S(2)}, u32[]{:S(2)}) collective-permute-start(bf16[256,2048]{1,0:T(8,128)(2,1)} %get-tuple-element.78), channel_id=1, source_target_pairs={{0,2},{1,3},{2,4},{3,5},{4,6},{5,7},{8,10},{9,11},{10,12},{11,13},... | collective-permute-start | bytes 3145736 | tf_op jit(solution)/shard_map/ppermute | solution.py:2175
  319.0 24.9 %collective-permute-start.1 = (bf16[256,2048]{1,0:T(8,128)(2,1)}, bf16[256,2048]{1,0:T(8,128)(2,1)S(1)}, u32[]{:S(2)}, u32[]{:S(2)}) collective-permute-start(bf16[256,2048]{1,0:T(8,128)(2,1)} %get-tuple-element.79), channel_id=1, source_target_pairs={{2,0},{3,1},{4,2},{5,3},{6,4},{7,5},{10,8},{11,9},{12,10},{13,11},... | collective-permute-start | bytes 3145736 | tf_op jit(solution)/shard_map/ppermute | solution.py:2176
  341.0 2.9 copy-start
  343.9 1.0 copy-start.1
  399.2 27.0 %collective-permute-start.2 = (bf16[256,2048]{1,0:T(8,128)(2,1)}, bf16[256,2048]{1,0:T(8,128)(2,1)S(1)}, u32[]{:S(2)}, u32[]{:S(2)}) collective-permute-start(bf16[256,2048]{1,0:T(8,128)(2,1)} %get-tuple-element.98), channel_id=1, source_target_pairs={{0,2},{1,3},{2,4},{3,5},{4,6},{5,7},{8,10},{9,11},{10,12},{11,13},... | collective-permute-start | bytes 3145736 | tf_op jit(solution)/shard_map/ppermute | solution.py:2175
  402.5 27.0 %collective-permute-start.3 = (bf16[256,2048]{1,0:T(8,128)(2,1)}, bf16[256,2048]{1,0:T(8,128)(2,1)S(1)}, u32[]{:S(2)}, u32[]{:S(2)}) collective-permute-start(bf16[256,2048]{1,0:T(8,128)(2,1)} %get-tuple-element.99), channel_id=1, source_target_pairs={{2,0},{3,1},{4,2},{5,3},{6,4},{7,5},{10,8},{11,9},{12,10},{13,11},... | collective-permute-start | bytes 3145736 | tf_op jit(solution)/shard_map/ppermute | solution.py:2176
  426.2 3.3 copy-start.2
  429.5 1.0 copy-start.3

commit v6 on v5

--- a/solution.py
+++ b/solution.py
@@ -208,13 +208,14 @@
 
 
 class LineSum:
-    def __init__(self, blocks, from_below, from_above, send, recv):
+    def __init__(self, blocks, from_below, from_above, send, recv, begun=False):
         self.count = lax.axis_size("dp") // 2
         self.place = lax.axis_index("dp")
         self.spot = self.place // 2
         self.blocks, self.below, self.above = blocks, from_below, from_above
         self.send, self.recv = send, recv
         self.part = blocks.shape[1] // PIECES
+        self.begun = begun
 
     def rows(self, piece):
         return pl.ds(pl.multiple_of(piece * self.part, self.part), self.part)
@@ -252,13 +253,15 @@
 
             @pl.when((self.spot > 0) & (self.spot < end) & (self.spot < step))
             def _():
-                self.rise(step - 1, piece, 0).wait_recv()
+                if step > 2 or not self.begun:
+                    self.rise(step - 1, piece, 0).wait_recv()
                 self.add(self.below, step, self.count + self.spot - step, piece)
                 self.rise(step, piece).start()
 
             @pl.when((mirrored > 0) & (mirrored < end) & (mirrored < step))
             def _():
-                self.fall(step - 1, piece, 0).wait_recv()
+                if step > 2 or not self.begun:
+                    self.fall(step - 1, piece, 0).wait_recv()
                 self.add(self.above, step, self.spot - self.count + step, piece)
                 self.fall(step, piece).start()
 
@@ -304,6 +307,17 @@
 
         piecewise(body)
 
+    def end_first(self):
+        end = self.count - 1
+
+        def body(piece):
+            pl.when(self.spot == 0)(lambda: self.rise(1, piece, end).wait_send())
+            pl.when(self.spot == end)(lambda: self.fall(1, piece, 0).wait_send())
+            pl.when(self.spot == 1)(lambda: self.rise(1, piece, 0).wait_recv())
+            pl.when(self.spot == end - 1)(lambda: self.fall(1, piece, 0).wait_recv())
+
+        piecewise(body)
+
     def finish(self, out, first=0, last=PIECES):
         end = self.count - 1
         mirrored = end - self.spot
@@ -337,7 +351,7 @@
                 self.fall(end, piece, 0).wait_recv()
                 gain(self.above)
 
-            for step in range(1, self.count):
+            for step in range(2 if self.begun else 1, self.count):
                 rises = (self.spot < step) & (self.spot < end)
                 falls = (mirrored < step) & (mirrored < end)
                 pl.when(rises)(lambda step=step: self.rise(step, piece, 0).wait_send())
@@ -553,6 +567,8 @@
     up_state,
     lengths_ref,
     right_ref,
+    left_ref,
+    wide_ref,
     turned_out,
     full_ref,
     next_full,
@@ -564,6 +580,8 @@
     slope_out,
     sums_out,
     right_low,
+    left_low,
+    wide_low,
     gather_send,
     gather_recv,
     next_send,
@@ -688,6 +706,8 @@
 
     by_rows(rows, ROW_TILE, mark)
     lax.fori_loop(1, total, end, 0)
+    round_matrix(left_ref.at[0, 0, 0], left_low.at[0, 0, 0])
+    round_matrix(wide_ref.at[0, 0, 0], wide_low.at[0, 0, 0])
     weight.advance(1)
     round_matrix(right_ref.at[0, 0, 0], right_low.at[0, 0, 0])
     weight.advance(2)
@@ -756,6 +776,8 @@
     later.advance(2, 1)
     products.near()
     stores += fetch([(sums_ref, sums_out)], local_sems.at[pl.ds(5, 1)])
+    round_matrix(left_ref.at[1, 0, 0], left_low.at[1, 0, 0])
+    round_matrix(wide_ref.at[1, 0, 0], wide_low.at[1, 0, 0])
     for step in range(3, later.count):
         later.advance(step)
     later.finish()
@@ -763,7 +785,7 @@
         store.wait()
 
 
-def first_step(weights, tokens, cotangent, states, lengths, right):
+def first_step(weights, tokens, cotangent, states, lengths, right, left, wide_right):
     mp_size, dp_size = (lax.axis_size("mp"), lax.axis_size("dp"))
     count = dp_size // 2
     rows = tokens.shape[0]
@@ -774,8 +796,8 @@
     return carrying(
         first_kernel,
         1,
-        weights + (tokens, cotangent) + states + (lengths, right),
-        "vhhhhhvvvvvh",
+        weights + (tokens, cotangent) + states + (lengths, right, left, wide_right),
+        "vhhhhhvvvvvhhh",
         [
             ((part, columns), low),
             ((part * dp_size, columns), low),
@@ -788,8 +810,10 @@
             ((rows, columns), low),
             ((count, part, columns), low),
             (right.shape, low),
+            (left.shape, low),
+            (wide_right.shape, low),
         ],
-        "vhhhhvvhhhh",
+        "vhhhhvvhhhhhh",
         gather_sems()
         + gather_sems()
         + block_sems()
@@ -868,6 +892,8 @@
     sums_out,
     owned_ref,
     vector_ref,
+    up_first,
+    down_first,
     gather_send,
     gather_recv,
     below,
@@ -895,6 +921,10 @@
     behind_ref,
     sums_ref,
     padded_ref,
+    next_below,
+    next_above,
+    next_send,
+    next_recv,
 ):
     loads = [
         pltpu.make_async_copy(source, target, local_sems.at[index])
@@ -1044,9 +1074,15 @@
     events(PLAN["far"])
     products.near()
     stores += fetch([(sums_ref, sums_out)], local_sems.at[pl.ds(6, 1)])
+    following = LineSum(sums_ref, next_below, next_above, next_send, next_recv)
+    following.advance(1)
     events([(step, piece) for step in range(1, weight.count) for piece in range(PIECES)])
     line.finish(owned_ref)
     weight.finish()
+    following.end_first()
+    stores += fetch(
+        [(next_below.at[0], up_first), (next_above.at[0], down_first)], local_sems.at[pl.ds(7, 2)]
+    )
     for store in stores:
         store.wait()
 
@@ -1080,8 +1116,10 @@
             ((count, part, columns), low),
             ((part, ready.shape[2]), low),
             ((8, columns), jnp.float32),
+            ((part, columns), low),
+            ((part, columns), low),
         ],
-        "hhhhvv",
+        "hhhhvvhh",
         gather_sems()
         + sum_scratch(part, ready.shape[2])
         + pair_scratch(part, columns)
@@ -1098,12 +1136,16 @@
             pltpu.VMEM((width, columns), low),
             pltpu.VMEM((rows, 3 * head_cols), low),
             pltpu.VMEM((rows, head_cols), low),
-            pltpu.SemaphoreType.DMA((7,)),
+            pltpu.SemaphoreType.DMA((9,)),
             pltpu.VMEM((rows, LANES), jnp.float32),
             pltpu.VMEM((rows, LANES), jnp.float32),
             pltpu.VMEM((rows, LANES), jnp.float32),
             pltpu.VMEM((count, part, columns), low),
             pltpu.VMEM((8, LANES), jnp.float32),
+            pltpu.VMEM((1, part, columns), low),
+            pltpu.VMEM((1, part, columns), low),
+            pltpu.SemaphoreType.DMA((2, count, PIECES)),
+            pltpu.SemaphoreType.DMA((2, count, PIECES)),
         ],
         4 * rows * width * columns + 12 * rows * rows * head_cols,
         "lines_beside_attention",
@@ -1115,6 +1157,8 @@
     piece,
     field_row,
     ready_hbm,
+    up_first,
+    down_first,
     xn_hbm,
     gy_hbm,
     down_hbm,
@@ -1126,11 +1170,9 @@
     spread_ref,
     gh_out,
     sums_out,
-    up_send,
-    down_send,
-    own_ref,
+    own_out,
     vector_ref,
-    out_ref,
+    out_hbm,
     below,
     above,
     line_send,
@@ -1152,36 +1194,42 @@
     gh_ref,
     local_sems,
     sums_ref,
+    own_ref,
+    out_ref,
 ):
-    loads = [
-        pltpu.make_async_copy(source, target, local_sems.at[index])
-        for index, (source, target) in enumerate(
-            [
-                (ready_hbm, ready_ref),
-                (down_hbm, down_ref),
-                (act_hbm, wide_ref),
-                (or_hbm, or_ref),
-                (qkvo_hbm.at[:, pl.ds(3 * head_cols, head_cols)], weight_ref),
-                (gy_hbm, gy_ref),
-                (xn_hbm, xn_ref),
-            ]
-        )
+    branches = BlockScatter(t_parts, t_got, t_send, t_recv)
+    share_width = x_ref.shape[1]
+
+    def share_rows(share):
+        start = pl.multiple_of(branches.owner(share) * share_width, share_width)
+        return pl.ds(start, share_width)
+
+    pairs = [
+        (ready_hbm, ready_ref),
+        (up_first, below.at[0]),
+        (down_first, above.at[0]),
+        (act_hbm, wide_ref),
+        (or_hbm, or_ref),
+        (qkvo_hbm.at[:, pl.ds(3 * head_cols, head_cols)], weight_ref),
     ]
-    for load in loads:
-        load.start()
-    line = LineSum(ready_ref, below, above, line_send, line_recv)
-    branches = BlockScatter(t_parts, t_got, t_send, t_recv)
+    for share in range(branches.size):
+        pairs.append((down_hbm.at[share_rows(share), :], down_ref.at[share_rows(share), :]))
+    pairs += [(gy_hbm, gy_ref), (xn_hbm, xn_ref)]
+    loads = fetch(pairs, local_sems)
+    more_sems = local_sems.at[pl.ds(len(pairs), 5)]
+    line = LineSum(ready_ref, below, above, line_send, line_recv, True)
     products = PairProducts(
         [xn_ref] * 4, quarters(gh_ref), parcel, sums_ref, pair_send, pair_recv
     )
     barrier, count = greet_line()
     count += greet_block()
     pl.semaphore_wait(barrier, count)
-    loads[0].wait()
-    line.advance(1)
-    for load in loads[1:5]:
+    for load in loads[:3]:
         load.wait()
-    rows, share_width = x_ref.shape
+    line.advance(2)
+    for load in loads[3:6]:
+        load.wait()
+    rows = x_ref.shape[0]
     width = down_ref.shape[1] // 4
     vector_ref[...] = jnp.zeros_like(vector_ref)
 
@@ -1197,33 +1245,34 @@
             )
 
     def branch(share):
-        start = pl.multiple_of(branches.owner(share) * share_width, share_width)
-        where = pl.ds(start, share_width)
+        where = share_rows(share)
+        loads[6 + share].wait()
 
         def once(here):
             part = contract(or_ref[here, :], weight_ref[where, :], 1, 1)
             part = part + contract(wide_ref[here, :], down_ref[where, :], 1, 1)
             t_parts[share, here, :] = part.astype(jnp.bfloat16)
 
-        by_rows(rows, 2 * ROW_TILE, once)
-        branches.after(share)
+        for bottom in branches.halves(share):
+            once(pl.ds(bottom * (rows // 2), rows // 2))
+            branches.after_half(share, bottom)
 
     shares = branches.size
     for share in range(shares):
         branch(share)
-        if share == 2:
-            line.advance(2, 0, 1)
-    late = pltpu.make_async_copy(slope_hbm, wide_ref, local_sems.at[7])
+        if share == 1:
+            line.advance(3, 0, 1)
+    late = pltpu.make_async_copy(slope_hbm, wide_ref, more_sems.at[0])
     late.start()
-    line.advance(2, 1)
+    line.advance(3, 1)
     branches.second()
-    for load in loads[5:]:
+    for load in loads[6 + shares :]:
         load.wait()
     late.wait()
     by_rows(rows, ROW_TILE, tile)
-    stores = fetch([(gh_ref, gh_out)], local_sems.at[pl.ds(8, 1)])
+    stores = fetch([(gh_ref, gh_out)], more_sems.at[pl.ds(1, 1)])
     products.far()
-    for step in range(3, line.count - 1):
+    for step in range(4, line.count):
         line.advance(step)
     branches.finish()
     biases = [
@@ -1234,16 +1283,18 @@
         total = x_ref[here, :].astype(jnp.float32) + branches.total(tile_index, ROW_TILE)
         total = total + biases[0] + biases[1]
         out_ref[here, :] = total.astype(jnp.bfloat16)
+    stores += fetch([(out_ref, out_hbm)], more_sems.at[pl.ds(3, 1)])
     products.near()
-    stores += fetch([(sums_ref, sums_out)], local_sems.at[pl.ds(9, 1)])
-    by_rows(own_ref.shape[0], 32, lambda here: keep_block(ready_ref, line.spot, own_ref, here))
-    line.hand_out(up_send, down_send)
+    stores += fetch([(sums_ref, sums_out)], more_sems.at[pl.ds(2, 1)])
+    line.finish(own_ref)
+    stores += fetch([(own_ref, own_out)], more_sems.at[pl.ds(4, 1)])
     for store in stores:
         store.wait()
 
 
 def fourth_step(
     ready,
+    firsts,
     normed,
     grad_rows,
     turned_down,
@@ -1265,6 +1316,7 @@
         6,
         (
             ready,
+            *firsts,
             normed,
             grad_rows,
             turned_down,
@@ -1275,17 +1327,15 @@
             tokens,
             spread,
         ),
-        "hhhhhhhhvv",
+        "hhhhhhhhhhvv",
         [
             ((rows, columns), low),
             ((count, part, columns), low),
             ((part, columns), low),
-            ((part, columns), low),
-            ((part, columns), low),
             ((8, columns), jnp.float32),
             (tokens.shape, low),
         ],
-        "hhvvvvv",
+        "hhhvh",
         sum_scratch(part, columns)
         + pair_scratch(part, columns)
         + scatter_scratch(rows, tokens.shape[1])
@@ -1298,8 +1348,10 @@
             pltpu.VMEM((rows, head_cols), low),
             pltpu.VMEM((width, head_cols), low),
             pltpu.VMEM((rows, columns), low),
-            pltpu.SemaphoreType.DMA((10,)),
+            pltpu.SemaphoreType.DMA((13 + lax.axis_size("mp"),)),
             pltpu.VMEM((count, part, columns), low),
+            pltpu.VMEM((part, columns), low),
+            pltpu.VMEM(tokens.shape, low),
         ],
         6 * rows * width * columns,
         "line_beside_hidden_grad",
@@ -1355,6 +1407,18 @@
         for number in ((0, 1), (2,), (3,), ())[index]:
             self.copy(number).start()
 
+    def halves(self, index):
+        return (1, 0) if index == 2 and self.size == 4 else (0, 1)
+
+    def after_half(self, index, bottom):
+        if self.size != 4:
+            if bottom:
+                self.after(index)
+            return
+        number = {(0, 0): 0, (0, 1): 1, (1, 0): 2, (2, 1): 3}.get((index, bottom))
+        if number is not None:
+            self.copy(number).start()
+
     def second(self):
         if self.size != 4:
             return
@@ -1466,9 +1530,6 @@
     spread_ref,
     vector_three,
     vector_four,
-    earlier,
-    earlier_rising,
-    earlier_falling,
     gained_out,
     terms_out,
     up_send,
@@ -1559,8 +1620,9 @@
                 part = part + contract(gh_ref[here, :], two_ref[slot], 1, 1)
                 g_parts[share, here, :] = part.astype(jnp.bfloat16)
 
-            by_rows(rows, 2 * ROW_TILE, tile)
-            from_norm.after(share)
+            for bottom in from_norm.halves(share):
+                tile(pl.ds(bottom * (rows // 2), rows // 2))
+                from_norm.after_half(share, bottom)
 
     columns = up_ref.shape[1]
     pl.run_scoped(
@@ -1667,7 +1729,6 @@
     spread,
     vector_three,
     vector_four,
-    earlier,
     piece,
 ):
     rows, width = tokens.shape
@@ -1694,9 +1755,8 @@
             spread,
             vector_three,
             vector_four,
-        )
-        + earlier,
-        "hhhhhhhhvvvhhh",
+        ),
+        "hhhhhhhhvvv",
         [
             ((rows, width), exact),
             ((8, rows), exact),
@@ -1836,7 +1896,7 @@
     ]
 
 
-def local_call(kernel, operands, in_places, outs, out_places, scratch, name):
+def local_call(kernel, operands, in_places, outs, out_places, scratch, name, limit=VMEM_LIMIT):
     spaces = {"h": pl.BlockSpec(memory_space=pl.ANY), "v": pl.BlockSpec(memory_space=pltpu.VMEM)}
     return pl.pallas_call(
         kernel,
@@ -1844,7 +1904,7 @@
         out_specs=[spaces[place] for place in out_places],
         out_shape=[jax.ShapeDtypeStruct(shape, dtype) for shape, dtype in outs],
         scratch_shapes=scratch,
-        compiler_params=pltpu.CompilerParams(vmem_limit_bytes=VMEM_LIMIT),
+        compiler_params=pltpu.CompilerParams(vmem_limit_bytes=limit),
         cost_estimate=pl.CostEstimate(flops=1 << 33, bytes_accessed=1 << 26, transcendentals=0),
         name=name,
     )(*operands)
@@ -1870,7 +1930,7 @@
         "vhvhh",
         [(left.shape[1:], exact), (right.shape[1:], exact), (master.shape, exact)],
         "hvh",
-        unit_scratch(grad.shape[0], grad.shape[1], False),
+        unit_scratch(grad.shape[0], grad.shape[1], False, left.dtype),
         "down_weight",
     )
 
@@ -1908,9 +1968,7 @@
 
 def attention_weights_kernel(
     passed,
-    own_ref,
-    rising_ref,
-    falling_ref,
+    owned_ref,
     qkv_left,
     qkv_right,
     w_qkv,
@@ -1978,9 +2036,8 @@
     out.start()
     into = fetch(zip(sources, held), pass_sems.at[0])
     edge = low_qkv.shape[1]
-    owned = summed(own_ref[...], rising_ref[...], falling_ref[...]).astype(jnp.bfloat16)
-    low_qkv[...] = owned[:, :edge]
-    low_out[...] = owned[:, edge:]
+    low_qkv[...] = owned_ref[:, :edge]
+    low_out[...] = owned_ref[:, edge:]
     qkv.prepare()
     out.prepare()
     for copy in into:
@@ -2019,7 +2076,7 @@
     return local_call(
         functools.partial(attention_weights_kernel, count),
         blocks + qkv + out + (sums,) + states + norm + passed,
-        "vvv" + "vhh" + "hvh" + "v" + "vvvv" + "vvvvv" + "h" * count,
+        "v" + "vhh" + "hvh" + "v" + "vvvv" + "vvvvv" + "h" * count,
         [(array.shape, array.dtype) for array in passed]
         + [
             (qkv[0].shape[1:], exact),
@@ -2044,9 +2101,10 @@
         ]
         + [pltpu.VMEM(array.shape, array.dtype) for array in passed]
         + [pltpu.SemaphoreType.DMA((2, count))]
-        + unit_scratch(depth, sizes[0], True)
+        + unit_scratch(depth, sizes[0], True, qkv[1].dtype)
         + unit_scratch(depth, sizes[1], False),
         "attention_weights",
+        VMEM_LIMIT,
     )
 
 
@@ -2057,7 +2115,8 @@
     small,
     stats,
     master,
-    earlier,
+    earlier_one,
+    earlier_two,
     small_out,
     stats_out,
     master_out,
@@ -2075,18 +2134,19 @@
     unit.run()
 
 
-def up_step(blocks, left, right, master, earlier):
+def up_step(blocks, left, right, master, *earlier):
     exact = jnp.float32
     depth, columns = master.shape
     return local_call(
         up_kernel,
-        blocks + (left, right, master, earlier),
-        "vvvvhhh",
+        blocks + (left, right, master) + earlier,
+        "vvvvhhhh",
         [(left.shape[1:], exact), (right.shape[1:], exact), (master.shape, exact)],
         "vhh",
         [pltpu.VMEM((depth, columns), jnp.bfloat16) for _ in range(2)]
         + unit_scratch(depth, columns, True, right.dtype),
         "up_weight",
+        VMEM_LIMIT,
     )
 
 
@@ -2135,6 +2195,8 @@
         slope,
         ready_down,
         up_right_low,
+        down_left_low,
+        qkv_right_low,
     ) = first_step(
         (w_up, planes, w_out, w_down),
         tokens,
@@ -2142,9 +2204,11 @@
         (ln_state, qkv_states, out_bias_state, up_bias_state),
         seq_lengths,
         up_right,
+        down_left,
+        qkv_right,
     )
     field_row = 1 - (-up_piece // LANES)
-    turned_down, grad_projected, attended, ready_qkvo, owned_down, vector_three = third_step(
+    turned_down, grad_projected, attended, ready_qkvo, owned_down, vector_three, *firsts = third_step(
         turned_block,
         ready_down,
         normed,
@@ -2155,8 +2219,9 @@
         piece,
         field_row,
     )
-    grad_hidden, ready_up, *sends, vector_four, output = fourth_step(
+    grad_hidden, ready_up, owned_qkvo, vector_four, output = fourth_step(
         ready_qkvo,
+        firsts,
         normed,
         grad_rows,
         turned_down,
@@ -2176,10 +2241,6 @@
         falling = lax.ppermute(down_send, "dp", [(place + 2, place) for place in steps])
         return (own, rising, falling)
 
-    blocks_qkvo = last_hop(*sends)
-    down_left_new, down_right_new, new_w_down = down_step(
-        owned_down, down_left, down_right, w_down, ready_up
-    )
     gained, terms, *sends, sums = fifth_step(
         ready_up,
         grad_hidden,
@@ -2192,10 +2253,12 @@
         spread,
         vector_three,
         vector_four,
-        (down_right_new,) + blocks_qkvo[1:],
         piece,
     )
     blocks_up = last_hop(*sends)
+    down_left_new, down_right_new, new_w_down = down_step(
+        owned_down, down_left_low, down_right, w_down, sends[0]
+    )
     (
         output,
         qkv_left_new,
@@ -2210,8 +2273,8 @@
         new_up_stat,
         input_grad,
     ) = attention_weights_step(
-        blocks_qkvo,
-        (qkv_left, qkv_right, planes),
+        (owned_qkvo,),
+        (qkv_left, qkv_right_low, planes),
         (out_left, out_right, w_out),
         sums,
         (qkv_states, out_bias_state, ln_state, up_bias_state),
@@ -2220,7 +2283,7 @@
     )
     new_w_qkv = new_planes.transpose(1, 0, 2)
     up_left_new, up_right_new, new_w_up = up_step(
-        blocks_up, up_left, up_right_low, w_up, new_vector_params
+        blocks_up, up_left, up_right_low, w_up, new_vector_params, down_right_new
     )
     new_up_bias = new_up_bias.reshape(-1)
     new_up_stat = new_up_stat.reshape(-1)

time: 456 us -> 452 us (level)
  waiting for transfers between devices: 6.19 us -> 0.01 us
  Pallas kernels: 430 us -> 435 us
    pallas_call x4, Pallas kernels: 370 us -> 384 us  [carrying(): pl.pallas_call(kernel, in_specs=[spaces[place] for place in in_places], o...]
    pallas_call x3, Pallas kernels: 59.9 us -> 51.8 us  [local_call(): pl.pallas_call(kernel, in_specs=[spaces[place] for place in in_places], o...]
    ppermute x2 -> x1, waiting for transfers between devices: 6.18 us -> 0.01 us  [last_hop(): lax.ppermute(down_send, 'dp', [(place + 2, place) for place in steps])]
  transfers between devices with their start and end apart: 4 -> 2, of which waited for: 2 -> 0; matrix products, arithmetic and copies ran while one was open for 0% -> 0% of each run, Pallas kernels for 10% -> 8%
where the time goes in v6:
time: 452 us; the launch traced here: 444 us
  Pallas kernels  435 us (96%)
  starting transfers between devices  5.9 us (1%)
    pallas_call x4, Pallas kernels, carrying(): pl.pallas_call(kernel, in_specs=[spaces[place] for place in in_places], o...  384 us
    pallas_call x3, Pallas kernels, local_call(): pl.pallas_call(kernel, in_specs=[spaces[place] for place in in_places], o...  51.8 us
  transfers between devices with their start and end apart: 2, of which 0 were waited for; matrix products, arithmetic and copies ran while one was open for 0% of the time, Pallas kernels for 8%

profile of v6, /device:TPU:0, one launch (start us, length us, event | category | flops | bytes accessed | tf_op | source)
XLA Modules:
  0.0 443.6 jit_solution(5707845387761372040)
XLA Ops:
  0.7 153.0 %gathers_beside_hidden.1 = (bf16[256,2048]{1,0:T(8,128)(2,1)}, bf16[2048,2048]{1,0:T(8,128)(2,1)}, bf16[2048,2048]{1,0:T(8,128)(2,1)}, bf16[1024,2048]{1,0:T(8,1...) custom-call(f32[256,2048]{1,0:T(8,128)} %master.3, ...), custom_call_target="tpu_custom_call" | custom-call | flops 17179869184 | bytes 33554432 | tf_op jit(solution)/shard_map/gathers_beside_hidden/pallas_call | solution.py:855
  153.7 119.4 %lines_beside_attention.1 = (bf16[2048,2048]{1,0:T(8,128)(2,1)}, bf16[1024,1536]{1,0:T(8,128)(2,1)}, bf16[1024,512]{1,0:T(8,128)(2,1)}, bf16[4,256,2048]{2,1,0:T...) custom-call(bf16[256,2048]{1,0:T(8,128)(2,1)} %get-tuple-element.68., ...), custom_call_target="tpu_custom_call" | custom-call | flops 23622320128 | bytes 33554432 | tf_op jit(solution)/shard_map/lines_beside_attention/pallas_call | solution.py:855
  273.1 55.1 %line_beside_hidden_grad.1 = (bf16[1024,2048]{1,0:T(8,128)(2,1)}, bf16[4,256,2048]{2,1,0:T(8,128)(2,1)}, bf16[256,2048]{1,0:T(8,128)(2,1)}, f32[8,2048]{1,0:T(8,128)}, bf16[1024,512]{1,0:T(8,128)(2,1)}) custom-call(bf16[4,256,2048]{2,1,0:T(8,128)(2,1)} %get-tuple-element.74.ready_hbm, bf16[256,2048]{1,0:T(8,128)(2,1)} %get-tuple-element.75.up_first, ...), custom_call_target="tpu_custom_call" | custom-call | flops 25769803776 | bytes 33554432 | tf_op jit(solution)/shard_map/line_beside_hidden_grad/pallas_call | solution.py:855
  328.3 56.0 %line_beside_norm_grad.1 = (f32[1024,512]{1,0:T(8,128)}, f32[8,1024]{1,0:T(8,128)}, bf16[256,2048]{1,0:T(8,128)(2,1)}, bf16[256,2048]{1,0:T(8,128)(2,1)}, bf16[256,2048]{1,0:T(8,128)(2,1)}, /*index=5*/f32[8,2048]{1,0:T(8,128)}) custom-call(bf16[4,256,2048]{2,1,0:T(8,128)(2,1)} %get-tuple-element.83.ready_hbm, bf16[1024,2048]{1,0:T(8,128)(2,1)} %get-tuple-element.84.gh_hbm, ...), custom_call_target="tpu_custom_call" | custom-call | flops 17179869184 | bytes 33554432 | tf_op jit(solution)/shard_map/line_beside_norm_grad/pallas_call | solution.py:855
  384.3 1.3 collective-permute-start.1
  385.6 4.6 %collective-permute-start = (bf16[256,2048]{1,0:T(8,128)(2,1)}, bf16[256,2048]{1,0:T(8,128)(2,1)S(1)}, u32[]{:S(2)}, u32[]{:S(2)}) collective-permute-start(bf16[256,2048]{1,0:T(8,128)(2,1)} %get-tuple-element.99.earlier), channel_id=1, source_target_pairs={{0,2},{1,3},{2,4},{3,5},{4,6},{5,7},{8,10},{9,11},{10,12},{11,13},... | collective-permute-start | bytes 3145736 | tf_op jit(solution)/shard_map/ppermute | solution.py:2240
  390.2 15.9 %down_weight.1 = (f32[1,1,2048,2048]{3,2,1,0:T(8,128)}, f32[1,1,256,256]{3,2,1,0:T(8,128)}, f32[2048,256]{1,0:T(8,128)}) custom-call(bf16[256,2048]{1,0:T(8,128)(2,1)} %get-tuple-element.103.grad, bf16[2,1,1,2048,2048]{4,3,2,1,0:T(8,128)(2,1)} %get-tuple-element.104.stats, f32[2,1,1,256,256]{4,3,2,1,0:T(8,128)} %small.2, f32[2048,256]{1,0:T(8,128)} %master.2, ...), custom_call_target="tpu_custom_call" | custom-call | flops 8589934592 | bytes 67108864 | tf_op jit(solution)/shard_map/down_weight/pallas_call | solution.py:1901
  406.1 19.1 %attention_weights.1 = (bf16[1024,512]{1,0:T(8,128)(2,1)}, f32[1,1,256,256]{3,2,1,0:T(8,128)}, f32[1,1,1536,1536]{3,2,1,0:T(8,128)}, f32[3,256,512]{2,1,0:T(8,12...) custom-call(bf16[256,2048]{1,0:T(8,128)(2,1)} %get-tuple-element.81., ...), custom_call_target="tpu_custom_call" | custom-call | flops 8589934592 | bytes 67108864 | tf_op jit(solution)/shard_map/attention_weights/pallas_call | solution.py:1901
  425.2 0.0 collective-permute-done.1.falling_ref
  425.2 0.0 copy-start
  425.2 0.0 collective-permute-done.rising_ref
  425.2 0.0 copy-start.1
  425.2 1.0 copy-done
  426.2 0.3 copy-done.1
  426.5 16.8 %up_weight.1 = (f32[1,1,256,256]{3,2,1,0:T(8,128)}, f32[1,1,2048,2048]{3,2,1,0:T(8,128)}, f32[256,2048]{1,0:T(8,128)}) custom-call(bf16[256,2048]{1,0:T(8,128)(2,1)} %get-tuple-element.98.own_ref, bf16[256,2048]{1,0:T(8,128)(2,1)} %copy-done.1, bf16[256,2048]{1,0:T(8,128)(2,1)} %copy-done, f32[2,1,1,256,256]{4,3,2,1,0:T(8,128)} %small.3, ...), custom_call_target="tpu_custom_call" | custom-call | flops 8589934592 | bytes 67108864 | tf_op jit(solution)/shard_map/up_weight/pallas_call | solution.py:1901
Async XLA Ops:
  384.3 40.9 %collective-permute-start.1 = (bf16[256,2048]{1,0:T(8,128)(2,1)}, bf16[256,2048]{1,0:T(8,128)(2,1)S(1)}, u32[]{:S(2)}, u32[]{:S(2)}) collective-permute-start(bf16[256,2048]{1,0:T(8,128)(2,1)} %get-tuple-element.100), channel_id=1, source_target_pairs={{2,0},{3,1},{4,2},{5,3},{6,4},{7,5},{10,8},{11,9},{12,10},{13,11},... | collective-permute-start | bytes 3145736 | tf_op jit(solution)/shard_map/ppermute | solution.py:2241
  385.6 39.6 %collective-permute-start = (bf16[256,2048]{1,0:T(8,128)(2,1)}, bf16[256,2048]{1,0:T(8,128)(2,1)S(1)}, u32[]{:S(2)}, u32[]{:S(2)}) collective-permute-start(bf16[256,2048]{1,0:T(8,128)(2,1)} %get-tuple-element.99.earlier), channel_id=1, source_target_pairs={{0,2},{1,3},{2,4},{3,5},{4,6},{5,7},{8,10},{9,11},{10,12},{11,13},... | collective-permute-start | bytes 3145736 | tf_op jit(solution)/shard_map/ppermute | solution.py:2240
  425.2 1.0 copy-start
  425.2 1.3 copy-start.1
